TPU v7x, 32 devices: a whole 2x2x4 slice. The times are simulated.
32 devices in a mesh: row: 8 (over y, x, core), col: 4 (over z).
Axes of the slice: x: 2, y: 2, z: 4, core: 2. Of those that a mesh axis runs over, the one named last changes fastest.
Arguments:
- top_inverse: bfloat16 [8, 4, 8, 4, 128, 128], P('row', None, None, 'col'), as said below
- upper_panel: bfloat16 [3, 8, 4, 128, 128], P(None, 'row', 'col'), may hold values from -0.25 to 0.25
- upper_pattern: int32 [3, 8, 4], P(None, 'row', 'col'), may hold values from 0 to 1
- upper_diagonal: float32 [3, 128, 128], replicated, may hold values from -6 to 6
- lower_panel: bfloat16 [8, 8, 4, 128, 128], P(None, 'row', 'col'), may hold values from -0.25 to 0.25
- lower_pattern: int32 [8, 8, 4], P(None, 'row', 'col'), may hold values from 0 to 1, as said below
- parents: int32 [8], replicated, may hold values from 0 to 2, as said below
- parent_panel: bfloat16 [8, 128, 128], replicated, may hold values from -0.5 to 0.5
- lower_diagonal: float32 [8, 128, 128], replicated, may hold values from -6 to 6
Outputs:
- upper_columns: bfloat16 [3, 8, 4, 128, 128], P(None, 'row', 'col')
- upper_blocks: float32 [3, 128, 128], replicated
- lower_columns: bfloat16 [8, 8, 4, 128, 128], P(None, 'row', 'col')
- lower_cross: float32 [8, 128, 128], replicated
- lower_blocks: float32 [8, 128, 128], replicated
Inputs may be any that keep to these rules, and one draw needn't show every extreme that they name: top_inverse is symmetric: block (I, J) is the transpose of block (J, I). `lower_pattern`: A second-level pattern is zero wherever the pattern of its parent is zero. `parents`: every first-level supernode is the parent of some second-level supernode.
All inputs are finite; a program needn't handle non-finite values.
Results may differ from a plain program's by a relative error of at most 0.0041.
Values may be sent and summed in bfloat16 or wider, within the bound.
No kernel may reach another device: no remote copies, remote signals or barrier semaphores. Data moves between devices by JAX's collectives and lax.ppermute only.
A program may use at most 128 MiB of HBM per device.

v0:
```python
import functools

import jax
import jax.numpy as jnp
import numpy as np
from jax import lax
from jax.experimental import pallas as pl
from jax.experimental.pallas import tpu as pltpu
from jax.sharding import PartitionSpec as P

F32 = jnp.float32
WIRE = jnp.bfloat16
VMEM = pl.BlockSpec(memory_space=pltpu.VMEM)
SMEM = pl.BlockSpec(memory_space=pltpu.SMEM)


def shape_of(dims, kind):
    return jax.ShapeDtypeStruct(dims, kind)


def flip(value, axis, mask):
    size = lax.axis_size(axis)
    return lax.ppermute(value, axis, [(i, i ^ mask) for i in range(size)])


def shift(value, axis, step):
    size = lax.axis_size(axis)
    return lax.ppermute(value, axis, [(i, (i + step) % size) for i in range(size)])


def ceil_to(value, step):
    return -(-value // step) * step


def params(refs, limit):
    size = sum(int(np.prod(r.shape)) * np.dtype(r.dtype).itemsize for r in refs)
    return pltpu.CompilerParams(vmem_limit_bytes=limit or ceil_to(size * 5 // 4, 1 << 20) + (4 << 20))


def call(kernel, name, scalars, arrays, outs, scratch=(), limit=0, cost=0):
    return pl.pallas_call(
        kernel,
        out_shape=outs,
        in_specs=[SMEM] * len(scalars) + [VMEM] * len(arrays),
        out_specs=[VMEM] * len(outs),
        scratch_shapes=[pltpu.VMEM(r.shape, r.dtype) for r in scratch],
        compiler_params=params([*arrays, *outs, *scratch], limit),
        cost_estimate=pl.CostEstimate(flops=cost, bytes_accessed=cost, transcendentals=0) if cost else None,
        name=name,
    )(*scalars, *arrays)


def stack_kernel(*refs):
    for i, piece in enumerate(refs[:-2]):
        refs[-1][i] = piece[...]


def mask_kernel(upper_pattern, lower_pattern, upper_panel, lower_panel, masked):
    uppers, lowers = upper_panel.shape[0], lower_panel.shape[0]
    for k in range(uppers):
        masked[k] = upper_panel[k] * upper_pattern[k].astype(F32).astype(jnp.bfloat16)
    for m in range(lowers):
        masked[uppers + m] = lower_panel[m] * lower_pattern[m].astype(F32).astype(jnp.bfloat16)


def turn_kernel(*refs):
    pieces, turned = refs[:-1], refs[-1]
    total, block = pieces[0].shape[0], pieces[0].shape[-1]
    for k in range(total):
        for o, piece in enumerate(pieces):
            turned[k, :, o * block : (o + 1) * block] = piece[k].T


def top_kernel(top, panel, out, out_turned, panel_turned):
    depth, width, block, _ = top.shape
    row, col = lax.axis_index("row"), lax.axis_index("col")
    half = width // 2

    def tile(o, i):
        return top[lax.rem(col + o, depth), row ^ (2 * (i % half) + i // half)]

    for o in range(out.shape[1] // block):
        rows = slice(o * block, (o + 1) * block)
        for i in range(width):
            out[i // half, rows, (i % half) * block : (i % half + 1) * block] = tile(o, i)

    for o in range(1, out.shape[1] // block):
        lanes = slice((o - 1) * block, o * block)
        for i in range(width):
            out_turned[i * block : (i + 1) * block, lanes] = tile(o, i).T
    for m in range(panel.shape[0]):
        panel_turned[m] = panel[m].T


def partial_kernel(top, *refs):
    pieces, (keep, away) = refs[:-2], refs[-2:]
    half, total, block, _ = keep.shape
    for first in range(0, total, 2):
        second = min(first + 1, total - 1)
        right = [jnp.concatenate([p[first], p[second]], axis=1) for p in pieces]
        value = jnp.dot(top[...], jnp.concatenate(right), preferred_element_type=F32)
        for lane, k in enumerate(range(first, second + 1)):
            for i in range(half):
                lanes = slice(lane * block, (lane + 1) * block)
                keep[i, k] = value[i * block : (i + 1) * block, lanes]
                far = value[(half + i) * block : (half + i + 1) * block, lanes]
                away[i, k] = far.astype(away.dtype)


def dot_pair(left, pieces, first, second):
    right = [
        jnp.concatenate([pieces[i, first], pieces[i, second]], axis=1)
        for i in range(pieces.shape[0])
    ]
    return jnp.dot(left, jnp.concatenate(right), preferred_element_type=F32)


def first_kernel(top, near, out):
    total = near.shape[1]
    for first in range(0, total, 2):
        out[first // 2] = dot_pair(top[0], near, first, min(first + 1, total - 1))


def second_kernel(uppers, parents, top, far, start, turned, *refs):
    own, returns, (sums_keep, sums_away, both, forms) = refs[0], refs[1:-4], refs[-4:]
    total, block, reach = turned.shape
    lowers = total - uppers
    half, _, chunk, _ = sums_keep.shape
    row = lax.axis_index("row")

    for first in range(0, total, 2):
        second = min(first + 1, total - 1)
        value = start[first // 2] + dot_pair(top[1], far, first, second)
        for lane, k in enumerate(range(first, second + 1)):
            part = value[:, lane * block : (lane + 1) * block]
            own[k] = part[:block]
            for o, out in enumerate(returns):
                out[k] = part[(o + 1) * block : (o + 2) * block].astype(WIRE)
            part = jnp.concatenate([0.5 * part[:block], part[block:reach]])
            high = part.astype(jnp.bfloat16)
            both[k, :, :block] = high
            both[k, :, block:] = (part - high.astype(F32)).astype(jnp.bfloat16)

    def fold(rows, k):
        value = jnp.dot(rows, both[k], preferred_element_type=F32)
        return value[:, :block] + value[:, block:]

    def spread(slot, index):
        for m in range(2 * half):
            place = pl.multiple_of((row ^ m) * chunk, chunk)
            (sums_away if m & 1 else sums_keep)[m // 2, index] = forms[slot, pl.ds(place, chunk)]

    for k in range(uppers):
        forms[k] = fold(turned[k], k)
        spread(k, k)
    for m in range(lowers):
        own_row, parent = turned[uppers + m], parents[m]
        value = fold(jnp.concatenate([own_row, turned[parent]], axis=0), uppers + m)
        slot = uppers + 2 * m
        forms[slot] = value[:block]
        forms[slot + 1] = value[block:] + fold(own_row, parent).T
        spread(slot, total + m)
        spread(slot + 1, uppers + m)


def line_kernel(*refs):
    parts, (total_out, order) = refs[:-2], refs[-2:]
    depth, col = len(parts), lax.axis_index("col")
    for o in range(depth):
        order[lax.rem(col + o, depth)] = parts[o][...].astype(F32)
    total = order[0]
    for c in range(1, depth):
        total = total + order[c]
    total_out[...] = total.astype(total_out.dtype)


def columns_kernel(parents, upper_pattern, lower_pattern, panel, own, front, back, *refs):
    got, (upper_out, lower_out) = refs[:-2], refs[-2:]
    uppers, lowers, middle = upper_out.shape[0], lower_out.shape[0], front.shape[0]

    def product(k):
        value = own[k] + (front[k] if k < middle else back[k - middle])
        for piece in got:
            value = value + piece[k].astype(F32)
        return value

    for k in range(uppers):
        upper_out[k] = (-product(k) * upper_pattern[k].astype(F32)).astype(jnp.bfloat16)
    extensions = [
        jnp.dot(upper_out[parents[m]], panel[m], preferred_element_type=F32) for m in range(lowers)
    ]
    for m in range(lowers):
        value = -(product(uppers + m) + extensions[m]) * lower_pattern[m].astype(F32)
        lower_out[m] = value.astype(jnp.bfloat16)


def split(wide):
    high = wide.astype(jnp.bfloat16)
    return high, (wide - high.astype(F32)).astype(jnp.bfloat16)


def blocks_kernel(
    width,
    parents,
    near,
    far,
    upper_diagonal,
    lower_diagonal,
    panel,
    panel_turned,
    upper_out,
    cross_out,
    lower_out,
    sums,
    halves,
):
    uppers, lowers = upper_out.shape[0], lower_out.shape[0]
    block = panel.shape[-1]
    chunk = block // width
    row = lax.axis_index("row")
    for m in range(width):
        start = pl.multiple_of((row ^ m) * chunk, chunk)
        sums[:, pl.ds(start, chunk)] = (far if m & 1 else near)[m // 2].astype(F32)
    for k in range(uppers):
        value = upper_diagonal[k] + (sums[k] + sums[k].T)
        upper_out[k] = value
        halves[k, :block], halves[k, block:] = split(value)
    products = [
        jnp.dot(halves[parents[m]], panel[m], preferred_element_type=F32) for m in range(lowers)
    ]
    rights = []
    for m in range(lowers):
        forms = sums[uppers + m]
        cross = forms - (products[m][:block] + products[m][block:])
        cross_out[m] = cross
        rights.append(jnp.concatenate([forms.astype(jnp.bfloat16), *split(cross)], axis=1))
    backs = [
        jnp.dot(panel_turned[m], rights[m], preferred_element_type=F32) for m in range(lowers)
    ]
    for m in range(lowers):
        value = backs[m]
        square = sums[uppers + lowers + m]
        turned = (square - value[:, :block]).T
        rest = value[:, block : 2 * block] + value[:, 2 * block :]
        lower_out[m] = lower_diagonal[m] + (square - rest) + turned


def gather_shifts(value, axis):
    size = lax.axis_size(axis)
    return [value] + [shift(value, axis, -o) for o in range(1, size)]


def pairs(size, offset):
    takers = range(size)
    if 2 * offset == size:
        takers = [c if c % 2 == 0 else c + offset for c in range(offset)]
    return [(c, (c + offset) % size) for c in takers]


def gather_pair(value, axis, offset):
    return lax.ppermute(value, axis, [(b, c) for c, b in pairs(lax.axis_size(axis), offset)])


def return_pair(value, axis, offset):
    return lax.ppermute(value, axis, pairs(lax.axis_size(axis), offset))


def halve(value, axis, bit, left):
    place = sorted(left, reverse=True).index(bit)
    value = value.reshape((2,) * len(left) + value.shape[-3:])
    away = lax.index_in_dim(value, 1, place, keepdims=False).astype(WIRE)
    keep = lax.index_in_dim(value, 0, place, keepdims=False)
    return keep, flip(away, axis, 1 << bit)


def gather_doubles(value, axis):
    value = value[None]
    for bit in range(1, lax.axis_size(axis).bit_length() - 1):
        value = jnp.concatenate([value, flip(value, axis, 1 << bit)])
    return value


def gather_near(value, axis):
    masks = range(2, lax.axis_size(axis), 2)
    return [value] + [flip(value, axis, m) for m in masks]


def scatter_flips(value, axis):
    masks = range(2, lax.axis_size(axis), 2)
    return [flip(value[m // 2].astype(WIRE), axis, m) for m in masks]


def tie(*values):
    return lax.optimization_barrier(values)


def per_device(
    top_inverse,
    upper_panel,
    upper_pattern,
    upper_diagonal,
    lower_panel,
    lower_pattern,
    parents,
    parent_panel,
    lower_diagonal,
):
    uppers, block = upper_panel.shape[0], upper_panel.shape[-1]
    lowers = lower_panel.shape[0]
    total = uppers + lowers
    sums_n = total + lowers
    width, depth = lax.axis_size("row"), lax.axis_size("col")
    half, chunk = width // 2, block // width
    bf16 = jnp.bfloat16
    upper_pattern, lower_pattern = upper_pattern.reshape(-1), lower_pattern.reshape(-1)

    (masked,) = call(
        mask_kernel,
        "mask",
        (upper_pattern, lower_pattern),
        (upper_panel.reshape(-1, block, block), lower_panel.reshape(-1, block, block)),
        [shape_of((total, block, block), bf16)],
        limit=60 << 20,
    )
    reach = depth // 2
    pieces = [gather_pair(masked, "col", o) for o in range(1, reach + 1)]
    (turned,) = call(
        turn_kernel,
        "turn",
        (),
        (masked, *pieces),
        [shape_of((total, block, (reach + 1) * block), bf16)],
    )
    (near,) = call(
        stack_kernel,
        "stack",
        (),
        (*gather_near(masked, "row"), turned),
        [shape_of((half, total, block, block), bf16)],
    )
    far = flip(near, "row", 1)
    top, top_turned, panel_turned = call(
        top_kernel,
        "top",
        (),
        (top_inverse[0, :, :, 0], parent_panel),
        [
            shape_of((2, (reach + 1) * block, half * block), bf16),
            shape_of((width * block, reach * block), bf16),
            shape_of(parent_panel.shape, bf16),
        ],
    )
    keep, away = call(
        partial_kernel,
        "partial",
        (),
        (top_turned, *pieces),
        [
            shape_of((half, total, block, block), F32),
            shape_of((half, total, block, block), WIRE),
        ],
    )
    columns_n = ceil_to(total, 2) // 2
    (start,) = call(
        first_kernel,
        "first",
        (),
        (top, near),
        [shape_of((columns_n, (reach + 1) * block, 2 * block), F32)],
    )
    own, *rest = call(
        functools.partial(second_kernel, uppers),
        "second",
        (parents,),
        (top, far, start, turned),
        [shape_of((total, block, block), F32)]
        + [shape_of((total, block, block), WIRE)] * reach
        + [shape_of((half, sums_n, chunk, block), F32)] * 2,
        [
            shape_of((total, (reach + 1) * block, 2 * block), bf16),
            shape_of((sums_n, block, block), F32),
        ],
    )
    returns, (sums_keep, sums_away) = rest[:-2], rest[-2:]

    other, across = tie(flip(sums_away, "row", 1), flip(away, "row", 1))
    sums = sums_keep + other
    pieces = scatter_flips(sums, "row")
    pieces[0], value = tie(pieces[0], keep + across.astype(F32))
    middle = total // 2
    bits = list(range(1, width.bit_length() - 1))
    sides = [value[:, :middle], value[:, middle:]]
    halves = [halve(side, "row", bit, bits) for side, bit in zip(sides, (bits[0], bits[-1]))]
    part = sums[0]
    for piece in pieces:
        part = part + piece.astype(F32)
    part = part.astype(WIRE)
    early = [return_pair(returns[o - 1], "col", o) for o in range(1, reach)]
    parts = gather_shifts(part, "col")
    tied = tie(*parts, *[got for _, got in halves], *early)
    early = tied[depth + 2 :]
    (part,) = call(
        line_kernel,
        "line",
        (),
        tied[:depth],
        [shape_of((sums_n, chunk, block), WIRE)],
        [shape_of((depth, sums_n, chunk, block), F32)],
    )
    sides = [keep + got.astype(F32) for (keep, _), got in zip(halves, tied[depth : depth + 2])]
    part, last, *sides = tie(part, returns[-1], *sides)
    near = gather_doubles(part, "row")
    far = flip(near, "row", 1)
    got = [*early, return_pair(last, "col", reach)]
    front, back = sides
    for i in range(1, len(bits)):
        keep, across = halve(front, "row", bits[i], bits[i:])
        front = keep + across.astype(F32)
        keep, across = halve(back, "row", bits[-1 - i], bits[: len(bits) - i])
        back = keep + across.astype(F32)
    front, back = [side.reshape(-1, block, block) for side in (front, back)]

    upper_blocks, lower_cross, lower_blocks = call(
        functools.partial(blocks_kernel, width),
        "blocks",
        (parents,),
        (near, far, upper_diagonal, lower_diagonal, parent_panel, panel_turned),
        [
            shape_of((uppers, block, block), F32),
            shape_of((lowers, block, block), F32),
            shape_of((lowers, block, block), F32),
        ],
        [shape_of((sums_n, block, block), F32), shape_of((uppers, 2 * block, block), bf16)],
    )
    upper_blocks, *got = tie(upper_blocks, *got)
    upper_columns, lower_columns = call(
        columns_kernel,
        "columns",
        (parents, upper_pattern, lower_pattern),
        (parent_panel, own, front, back, *got),
        [
            shape_of((uppers, block, block), bf16),
            shape_of((lowers, block, block), bf16),
        ],
    )
    return (
        upper_columns[:, None, None],
        upper_blocks,
        lower_columns[:, None, None],
        lower_cross,
        lower_blocks,
    )


def solution(mesh):
    return jax.shard_map(
        per_device,
        mesh=mesh,
        in_specs=(
            P("row", None, None, "col", None, None),
            P(None, "row", "col", None, None),
            P(None, "row", "col"),
            P(),
            P(None, "row", "col", None, None),
            P(None, "row", "col"),
            P(),
            P(),
            P(),
        ),
        out_specs=(
            P(None, "row", "col", None, None),
            P(),
            P(None, "row", "col", None, None),
            P(),
            P(),
        ),
        check_vma=False,
    )
```

profile of v0, /device:TPU:8, one launch (start us, length us, event | category | flops | bytes accessed | tf_op | source)
XLA Modules:
  0.0 71.8 jit_solution(3009387503304654717)
XLA Ops:
  0.6 1.8 %mask.1.refs_0_ = bf16[11,128,128]{2,1,0:T(8,128)(2,1)} custom-call(s32[3]{0:T(128)} %bitcast.47, s32[8]{0:T(128)} %bitcast.49, bf16[3,128,128]{2,1,0:T(8,128)(2,1)} %bitcast.54, bf16[8,128,128]{2,1,0:T(8,128)(2,1)} %bitcast.53), custom_call_target="tpu_custom_call" | custom-call | tf_op jit(solution)/shard_map/mask/pallas_call | solution.py:41
  2.4 4.5 %collective-permute-start.4 = (bf16[11,128,128]{2,1,0:T(8,128)(2,1)}, bf16[11,128,128]{2,1,0:T(8,128)(2,1)S(1)}, u32[]{:S(2)}, u32[]{:S(2)}) collective-permute-start(bf16[11,128,128]{2,1,0:T(8,128)(2,1)} %mask.1.refs_0_), channel_id=1, source_target_pairs={{2,0},{1,3},{6,4},{5,7},{10,8},{9,11},{14,12},{13,15},{18,16},{17,... | collective-permute-start | bytes 1081352 | tf_op jit(solution)/shard_map/ppermute | solution.py:261
  6.9 0.1 collective-permute-start.3
  7.0 2.5 %collective-permute-start.2 = (bf16[11,128,128]{2,1,0:T(8,128)(2,1)}, bf16[11,128,128]{2,1,0:T(8,128)(2,1)S(1)}, u32[]{:S(2)}, u32[]{:S(2)}) collective-permute-start(bf16[11,128,128]{2,1,0:T(8,128)(2,1)} %mask.1.refs_0_), channel_id=1, source_target_pairs={{0,24},{4,28},{8,16},{12,20},{16,8},{20,12},{24,0},{28,4},{1,25},{... | collective-permute-start | bytes 1081352 | tf_op jit(solution)/shard_map/ppermute | solution.py:23
  9.5 0.5 collective-permute-start.1
  10.0 0.5 collective-permute-start
  10.6 12.1 %collective-permute-done.4.refs_2_.refs_1_ = bf16[11,128,128]{2,1,0:T(8,128)(2,1)S(1)} collective-permute-done((bf16[11,128,128]{2,1,0:T(8,128)(2,1)}, bf16[11,128,128]{2,1,0:T(8,128)(2,1)S(1)}, u32[]{:S(2)}, u32[]{:S(2)}) %collective-permute-start.4) | collective-permute-done | bytes 360480 | tf_op jit(solution)/shard_map/ppermute | solution.py:261
  22.6 0.0 collective-permute-done.3.refs_1_.refs_0_
  22.6 1.0 %copy-done = bf16[11,128,128]{2,1,0:T(8,128)(2,1)S(1)} copy-done((bf16[11,128,128]{2,1,0:T(8,128)(2,1)S(1)}, bf16[11,128,128]{2,1,0:T(8,128)(2,1)}, u32[]{:S(2)}) %copy-start) | copy-done | bytes 360472
  23.6 0.3 turn.1.refs_4_.turned
  24.0 0.0 copy-start.2
  24.0 0.0 copy-start.3
  24.0 1.8 %collective-permute-done.1.refs_2_ = bf16[11,128,128]{2,1,0:T(8,128)(2,1)S(1)} collective-permute-done((bf16[11,128,128]{2,1,0:T(8,128)(2,1)}, bf16[11,128,128]{2,1,0:T(8,128)(2,1)S(1)}, u32[]{:S(2)}, u32[]{:S(2)}) %collective-permute-start.1) | collective-permute-done | bytes 360480 | tf_op jit(solution)/shard_map/ppermute | solution.py:23
  25.8 0.1 collective-permute-done.refs_1_
  25.9 0.1 stack.1.near
  26.0 0.1 collective-permute-start.5
  26.1 0.4 top.1
  26.4 1.0 %partial.1 = (f32[4,11,128,128]{3,2,1,0:T(8,128)S(1)}, bf16[4,11,128,128]{3,2,1,0:T(8,128)(2,1)S(1)}) custom-call(bf16[1024,256]{1,0:T(8,128)(2,1)S(1)} %get-tuple-element.42.top, bf16[11,128,128]{2,1,0:T(8,128)(2,1)S(1)} %collective-permute-done.3.refs_1_.refs_0_, bf16[11,128,128]{2,1,0:T(8,128)(2,1)S(1)} %collective-permute-done.4.refs_2_.refs_1_), custom_call_target="tpu_custom_call" | custom-call | tf_op jit(solution)/shard_map/partial/pallas_call | solution.py:41
  27.4 0.5 collective-permute-start.7
  28.0 0.8 %first.1.start = f32[6,384,256]{2,1,0:T(8,128)S(1)} custom-call(bf16[2,384,512]{2,1,0:T(8,128)(2,1)S(1)} %get-tuple-element.38.top, bf16[4,11,128,128]{3,2,1,0:T(8,128)(2,1)S(1)} %stack.1.near), custom_call_target="tpu_custom_call" | custom-call | tf_op jit(solution)/shard_map/first/pallas_call | solution.py:41
  28.8 0.5 collective-permute-done.5.far
  29.3 2.4 %second.1 = (f32[11,128,128]{2,1,0:T(8,128)S(1)}, bf16[11,128,128]{2,1,0:T(8,128)(2,1)S(1)}, bf16[11,128,128]{2,1,0:T(8,128)(2,1)S(1)}, f32[4,19,16,128]{3,2,1,0:T(8,128)S(1)}, f32[4,19,16,128]{3,2,1,0:T(8,128)S(1)}) custom-call(s32[8]{0:T(128)S(1)} %copy-done.6, bf16[2,384,512]{2,1,0:T(8,128)(2,1)S(1)} %get-tuple-element.38.top, ...), custom_call_target="tpu_custom_call" | custom-call | tf_op jit(solution)/shard_map/second/pallas_call | solution.py:41
  31.7 0.2 collective-permute-start.6
  31.9 1.7 %collective-permute-start.16 = (bf16[11,128,128]{2,1,0:T(8,128)(2,1)S(1)}, bf16[11,128,128]{2,1,0:T(8,128)(2,1)S(1)}, u32[]{:S(2)}, u32[]{:S(2)}) collective-permute-start(bf16[11,128,128]{2,1,0:T(8,128)(2,1)S(1)} %get-tuple-element.49), channel_id=1, source_target_pairs={{0,1},{1,2},{2,3},{3,0},{4,5},{5,6},{6,7},{7,4},{8,9},{9,10},{10,1... | collective-permute-start | bytes 1081352 | tf_op jit(solution)/shard_map/ppermute | solution.py:265
  33.6 0.0 collective-permute-done.7
  33.6 0.2 collective-permute-done.6
  33.8 0.1 fusion.8
  33.9 1.6 %collective-permute-start.8 = (bf16[19,16,128]{2,1,0:T(8,128)(2,1)S(1)}, bf16[19,16,128]{2,1,0:T(8,128)(2,1)S(1)}, u32[]{:S(2)}, u32[]{:S(2)}) collective-permute-start(bf16[19,16,128]{2,1,0:T(8,128)(2,1)S(1)} %get-tuple-element.78), channel_id=1, source_target_pairs={{0,8},{4,12},{8,0},{12,4},{16,24},{20,28},{24,16},{28,20},{1,9},{5... | collective-permute-start | bytes 233480 | tf_op jit(solution)/shard_map/ppermute | solution.py:23
  35.5 1.4 %collective-permute-start.10 = (bf16[19,16,128]{2,1,0:T(8,128)(2,1)S(1)}, bf16[19,16,128]{2,1,0:T(8,128)(2,1)S(1)}, u32[]{:S(2)}, u32[]{:S(2)}) collective-permute-start(bf16[19,16,128]{2,1,0:T(8,128)(2,1)S(1)} %get-tuple-element.79), channel_id=1, source_target_pairs={{0,24},{4,28},{8,16},{12,20},{16,8},{20,12},{24,0},{28,4},{1,25},{... | collective-permute-start | bytes 233480 | tf_op jit(solution)/shard_map/ppermute | solution.py:23
  36.9 0.6 collective-permute-start.9
  37.5 0.5 convert_add_fusion
  38.0 0.7 %collective-permute-done.8 = bf16[19,16,128]{2,1,0:T(8,128)(2,1)S(1)} collective-permute-done((bf16[19,16,128]{2,1,0:T(8,128)(2,1)S(1)}, bf16[19,16,128]{2,1,0:T(8,128)(2,1)S(1)}, u32[]{:S(2)}, u32[]{:S(2)}) %collective-permute-start.8) | collective-permute-done | bytes 77856 | tf_op jit(solution)/shard_map/ppermute | solution.py:23
  38.8 0.1 slice.95
  38.8 0.1 slice.55
  38.9 1.6 %collective-permute-start.15 = (bf16[2,6,128,128]{3,2,1,0:T(8,128)(2,1)S(1)}, bf16[2,6,128,128]{3,2,1,0:T(8,128)(2,1)S(1)}, u32[]{:S(2)}, u32[]{:S(2)}) collective-permute-start(bf16[2,6,128,128]{3,2,1,0:T(8,128)(2,1)S(1)} %slice.95), channel_id=1, source_target_pairs={{0,16},{4,20},{8,24},{12,28},{16,0},{20,4},{24,8},{28,12},{1,17},{... | collective-permute-start | bytes 1179656 | tf_op jit(solution)/shard_map/ppermute | solution.py:23
  40.6 0.1 fusion.1
  40.6 1.1 %collective-permute-start.14 = (bf16[2,5,128,128]{3,2,1,0:T(8,128)(2,1)S(1)}, bf16[2,5,128,128]{3,2,1,0:T(8,128)(2,1)S(1)}, u32[]{:S(2)}, u32[]{:S(2)}) collective-permute-start(bf16[2,5,128,128]{3,2,1,0:T(8,128)(2,1)S(1)} %fusion.1), channel_id=1, source_target_pairs={{0,8},{4,12},{8,0},{12,4},{16,24},{20,28},{24,16},{28,20},{1,9},{5... | collective-permute-start | bytes 983048 | tf_op jit(solution)/shard_map/ppermute | solution.py:23
  41.7 1.1 %collective-permute-done.9 = bf16[19,16,128]{2,1,0:T(8,128)(2,1)S(1)} collective-permute-done((bf16[19,16,128]{2,1,0:T(8,128)(2,1)S(1)}, bf16[19,16,128]{2,1,0:T(8,128)(2,1)S(1)}, u32[]{:S(2)}, u32[]{:S(2)}) %collective-permute-start.9) | collective-permute-done | bytes 77856 | tf_op jit(solution)/shard_map/ppermute | solution.py:23
  42.8 1.7 %collective-permute-start.13 = (bf16[19,16,128]{2,1,0:T(8,128)(2,1)S(1)}, bf16[19,16,128]{2,1,0:T(8,128)(2,1)S(1)}, u32[]{:S(2)}, u32[]{:S(2)}) collective-permute-start(bf16[19,16,128]{2,1,0:T(8,128)(2,1)S(1)} %fusion.7.refs_0_), channel_id=1, source_target_pairs={{0,1},{1,2},{2,3},{3,0},{4,5},{5,6},{6,7},{7,4},{8,9},{9,10},{10,1... | collective-permute-start | bytes 233480 | tf_op jit(solution)/shard_map/ppermute | solution.py:28
  44.5 1.4 %collective-permute-start.12 = (bf16[19,16,128]{2,1,0:T(8,128)(2,1)S(1)}, bf16[19,16,128]{2,1,0:T(8,128)(2,1)S(1)}, u32[]{:S(2)}, u32[]{:S(2)}) collective-permute-start(bf16[19,16,128]{2,1,0:T(8,128)(2,1)S(1)} %fusion.7.refs_0_), channel_id=1, source_target_pairs={{0,2},{1,3},{2,0},{3,1},{4,6},{5,7},{6,4},{7,5},{8,10},{9,11},{10,... | collective-permute-start | bytes 233480 | tf_op jit(solution)/shard_map/ppermute | solution.py:28
  46.0 1.0 %collective-permute-start.11 = (bf16[19,16,128]{2,1,0:T(8,128)(2,1)S(1)}, bf16[19,16,128]{2,1,0:T(8,128)(2,1)S(1)}, u32[]{:S(2)}, u32[]{:S(2)}) collective-permute-start(bf16[19,16,128]{2,1,0:T(8,128)(2,1)S(1)} %fusion.7.refs_0_), channel_id=1, source_target_pairs={{0,3},{1,0},{2,1},{3,2},{4,7},{5,4},{6,5},{7,6},{8,11},{9,8},{10,9... | collective-permute-start | bytes 233480 | tf_op jit(solution)/shard_map/ppermute | solution.py:28
  47.0 2.1 %collective-permute-done.13.refs_3_ = bf16[19,16,128]{2,1,0:T(8,128)(2,1)S(1)} collective-permute-done((bf16[19,16,128]{2,1,0:T(8,128)(2,1)S(1)}, bf16[19,16,128]{2,1,0:T(8,128)(2,1)S(1)}, u32[]{:S(2)}, u32[]{:S(2)}) %collective-permute-start.13) | collective-permute-done | bytes 77856 | tf_op jit(solution)/shard_map/ppermute | solution.py:28
  49.1 1.7 %collective-permute-done.12.refs_2_ = bf16[19,16,128]{2,1,0:T(8,128)(2,1)S(1)} collective-permute-done((bf16[19,16,128]{2,1,0:T(8,128)(2,1)S(1)}, bf16[19,16,128]{2,1,0:T(8,128)(2,1)S(1)}, u32[]{:S(2)}, u32[]{:S(2)}) %collective-permute-start.12) | collective-permute-done | bytes 77856 | tf_op jit(solution)/shard_map/ppermute | solution.py:28
  50.8 1.5 %collective-permute-done.11.refs_1_ = bf16[19,16,128]{2,1,0:T(8,128)(2,1)S(1)} collective-permute-done((bf16[19,16,128]{2,1,0:T(8,128)(2,1)S(1)}, bf16[19,16,128]{2,1,0:T(8,128)(2,1)S(1)}, u32[]{:S(2)}, u32[]{:S(2)}) %collective-permute-start.11) | collective-permute-done | bytes 77856 | tf_op jit(solution)/shard_map/ppermute | solution.py:28
  52.3 0.1 convert_add_fusion.1
  52.4 0.1 fusion
  52.5 0.1 line.1
  52.6 0.7 %collective-permute-start.19 = (bf16[1,19,16,128]{3,2,1,0:T(8,128)(2,1)S(1)}, bf16[1,19,16,128]{3,2,1,0:T(8,128)(2,1)S(1)}, u32[]{:S(2)}, u32[]{:S(2)}) collective-permute-start(bf16[1,19,16,128]{3,2,1,0:T(8,128)(2,1)S(1)} %bitcast.44), channel_id=1, source_target_pairs={{0,8},{4,12},{8,0},{12,4},{16,24},{20,28},{24,16},{28,20},{1,9},{5... | collective-permute-start | bytes 233480 | tf_op jit(solution)/shard_map/ppermute | solution.py:23
  53.3 1.4 %collective-permute-start.17 = (bf16[5,128,128]{2,1,0:T(8,128)(2,1)S(1)}, bf16[5,128,128]{2,1,0:T(8,128)(2,1)S(1)}, u32[]{:S(2)}, u32[]{:S(2)}) collective-permute-start(bf16[5,128,128]{2,1,0:T(8,128)(2,1)S(1)} %fusion.3), channel_id=1, source_target_pairs={{0,16},{4,20},{8,24},{12,28},{16,0},{20,4},{24,8},{28,12},{1,17},{... | collective-permute-start | bytes 491528 | tf_op jit(solution)/shard_map/ppermute | solution.py:23
  54.8 2.3 %collective-permute-done.19 = bf16[1,19,16,128]{3,2,1,0:T(8,128)(2,1)S(1)} collective-permute-done((bf16[1,19,16,128]{3,2,1,0:T(8,128)(2,1)S(1)}, bf16[1,19,16,128]{3,2,1,0:T(8,128)(2,1)S(1)}, u32[]{:S(2)}, u32[]{:S(2)}) %collective-permute-start.19) | collective-permute-done | bytes 77856 | tf_op jit(solution)/shard_map/ppermute | solution.py:23
  57.1 0.0 copy-start.4
  57.1 0.0 copy-start.5
  57.1 0.8 %collective-permute-start.20 = (bf16[2,19,16,128]{3,2,1,0:T(8,128)(2,1)S(1)}, bf16[2,19,16,128]{3,2,1,0:T(8,128)(2,1)S(1)}, u32[]{:S(2)}, u32[]{:S(2)}) collective-permute-start(bf16[2,19,16,128]{3,2,1,0:T(8,128)(2,1)S(1)} %pad_maximum_fusion.1), channel_id=1, source_target_pairs={{0,16},{4,20},{8,24},{12,28},{16,0},{20,4},{24,8},{28,12},{1,17},{... | collective-permute-start | bytes 466952 | tf_op jit(solution)/shard_map/ppermute | solution.py:23
  57.9 1.4 %collective-permute-start.18 = (bf16[6,128,128]{2,1,0:T(8,128)(2,1)S(1)}, bf16[6,128,128]{2,1,0:T(8,128)(2,1)S(1)}, u32[]{:S(2)}, u32[]{:S(2)}) collective-permute-start(bf16[6,128,128]{2,1,0:T(8,128)(2,1)S(1)} %fusion.2), channel_id=1, source_target_pairs={{0,8},{4,12},{8,0},{12,4},{16,24},{20,28},{24,16},{28,20},{1,9},{5... | collective-permute-start | bytes 589832 | tf_op jit(solution)/shard_map/ppermute | solution.py:23
  59.3 1.3 %collective-permute-start.22 = (bf16[11,128,128]{2,1,0:T(8,128)(2,1)S(1)}, bf16[11,128,128]{2,1,0:T(8,128)(2,1)S(1)}, u32[]{:S(2)}, u32[]{:S(2)}) collective-permute-start(bf16[11,128,128]{2,1,0:T(8,128)(2,1)S(1)} %get-tuple-element.63), channel_id=1, source_target_pairs={{0,2},{3,1},{4,6},{7,5},{8,10},{11,9},{12,14},{15,13},{16,18},{19,... | collective-permute-start | bytes 1081352 | tf_op jit(solution)/shard_map/ppermute | solution.py:265
  60.6 1.8 %collective-permute-done.20 = bf16[2,19,16,128]{3,2,1,0:T(8,128)(2,1)S(1)} collective-permute-done((bf16[2,19,16,128]{3,2,1,0:T(8,128)(2,1)S(1)}, bf16[2,19,16,128]{3,2,1,0:T(8,128)(2,1)S(1)}, u32[]{:S(2)}, u32[]{:S(2)}) %collective-permute-start.20) | collective-permute-done | bytes 155680 | tf_op jit(solution)/shard_map/ppermute | solution.py:23
  62.4 0.1 collective-permute-start.21
  62.5 0.0 copy-start.7
  62.5 0.0 copy-start.8
  62.6 1.1 %collective-permute-done.18 = bf16[6,128,128]{2,1,0:T(8,128)(2,1)S(1)} collective-permute-done((bf16[6,128,128]{2,1,0:T(8,128)(2,1)S(1)}, bf16[6,128,128]{2,1,0:T(8,128)(2,1)S(1)}, u32[]{:S(2)}, u32[]{:S(2)}) %collective-permute-start.18) | collective-permute-done | bytes 196640 | tf_op jit(solution)/shard_map/ppermute | solution.py:23
  63.7 0.4 collective-permute-done.21.far
  64.1 2.2 %blocks.1 = (f32[3,128,128]{2,1,0:T(8,128)}, f32[8,128,128]{2,1,0:T(8,128)}, f32[8,128,128]{2,1,0:T(8,128)}) custom-call(s32[8]{0:T(128)S(1)} %copy-done.6, bf16[4,19,16,128]{3,2,1,0:T(8,128)(2,1)S(1)} %pad_maximum_fusion.near, bf16[4,19,16,128]{3,2,1,0:T(8,128)(2,1)S(1)} %collective-permute-done.21.far, f32[3,128,128]{2,1,0:T(8,128)S(1)} %copy-done.5, ...), custom_call_target="tpu_custom_call" | custom-call | tf_op jit(solution)/shard_map/blocks/pallas_call | solution.py:41
  66.2 4.1 %collective-permute-done.22.refs_1_ = bf16[11,128,128]{2,1,0:T(8,128)(2,1)S(1)} collective-permute-done((bf16[11,128,128]{2,1,0:T(8,128)(2,1)S(1)}, bf16[11,128,128]{2,1,0:T(8,128)(2,1)S(1)}, u32[]{:S(2)}, u32[]{:S(2)}) %collective-permute-start.22) | collective-permute-done | bytes 360480 | tf_op jit(solution)/shard_map/ppermute | solution.py:265
  70.3 1.5 %columns.1 = (bf16[3,128,128]{2,1,0:T(8,128)(2,1)}, bf16[8,128,128]{2,1,0:T(8,128)(2,1)}) custom-call(s32[8]{0:T(128)S(1)} %copy-done.6, s32[3]{0:T(128)S(1)} %bitcast.48, s32[8]{0:T(128)S(1)} %bitcast.50, bf16[8,128,128]{2,1,0:T(8,128)(2,1)S(1)} %copy-done.2, f32[11,128,128]{2,1,0:T(8,128)S(1)} %get-tuple-element.39.own, ...), custom_call_target="tpu_custom_call" | custom-call | tf_op jit(solution)/shard_map/columns/pallas_call | solution.py:41
  (25 shorter events, 0.3 us)
Async XLA Ops:
  2.4 20.2 %collective-permute-start.4 = (bf16[11,128,128]{2,1,0:T(8,128)(2,1)}, bf16[11,128,128]{2,1,0:T(8,128)(2,1)S(1)}, u32[]{:S(2)}, u32[]{:S(2)}) collective-permute-start(bf16[11,128,128]{2,1,0:T(8,128)(2,1)} %mask.1.refs_0_), channel_id=1, source_target_pairs={{2,0},{1,3},{6,4},{5,7},{10,8},{9,11},{14,12},{13,15},{18,16},{17,... | collective-permute-start | bytes 1081352 | tf_op jit(solution)/shard_map/ppermute | solution.py:261
  6.9 15.7 %collective-permute-start.3 = (bf16[11,128,128]{2,1,0:T(8,128)(2,1)}, bf16[11,128,128]{2,1,0:T(8,128)(2,1)S(1)}, u32[]{:S(2)}, u32[]{:S(2)}) collective-permute-start(bf16[11,128,128]{2,1,0:T(8,128)(2,1)} %mask.1.refs_0_), channel_id=1, source_target_pairs={{1,0},{2,1},{3,2},{0,3},{5,4},{6,5},{7,6},{4,7},{9,8},{10,9},{11,1... | collective-permute-start | bytes 1081352 | tf_op jit(solution)/shard_map/ppermute | solution.py:261
  7.0 17.0 %collective-permute-start.2 = (bf16[11,128,128]{2,1,0:T(8,128)(2,1)}, bf16[11,128,128]{2,1,0:T(8,128)(2,1)S(1)}, u32[]{:S(2)}, u32[]{:S(2)}) collective-permute-start(bf16[11,128,128]{2,1,0:T(8,128)(2,1)} %mask.1.refs_0_), channel_id=1, source_target_pairs={{0,24},{4,28},{8,16},{12,20},{16,8},{20,12},{24,0},{28,4},{1,25},{... | collective-permute-start | bytes 1081352 | tf_op jit(solution)/shard_map/ppermute | solution.py:23
  9.5 16.3 %collective-permute-start.1 = (bf16[11,128,128]{2,1,0:T(8,128)(2,1)}, bf16[11,128,128]{2,1,0:T(8,128)(2,1)S(1)}, u32[]{:S(2)}, u32[]{:S(2)}) collective-permute-start(bf16[11,128,128]{2,1,0:T(8,128)(2,1)} %mask.1.refs_0_), channel_id=1, source_target_pairs={{0,16},{4,20},{8,24},{12,28},{16,0},{20,4},{24,8},{28,12},{1,17},{... | collective-permute-start | bytes 1081352 | tf_op jit(solution)/shard_map/ppermute | solution.py:23
  10.0 15.9 %collective-permute-start = (bf16[11,128,128]{2,1,0:T(8,128)(2,1)}, bf16[11,128,128]{2,1,0:T(8,128)(2,1)S(1)}, u32[]{:S(2)}, u32[]{:S(2)}) collective-permute-start(bf16[11,128,128]{2,1,0:T(8,128)(2,1)} %mask.1.refs_0_), channel_id=1, source_target_pairs={{0,8},{4,12},{8,0},{12,4},{16,24},{20,28},{24,16},{28,20},{1,9},{5... | collective-permute-start | bytes 1081352 | tf_op jit(solution)/shard_map/ppermute | solution.py:23
  22.6 1.0 %copy-start = (bf16[11,128,128]{2,1,0:T(8,128)(2,1)S(1)}, bf16[11,128,128]{2,1,0:T(8,128)(2,1)}, u32[]{:S(2)}) copy-start(bf16[11,128,128]{2,1,0:T(8,128)(2,1)} %mask.1.refs_0_) | copy-start | bytes 1081348
  23.6 2.3 %copy-start.1 = (bf16[11,128,128]{2,1,0:T(8,128)(2,1)S(1)}, bf16[11,128,128]{2,1,0:T(8,128)(2,1)}, u32[]{:S(2)}) copy-start(bf16[11,128,128]{2,1,0:T(8,128)(2,1)} %mask.1.refs_0_) | copy-start | bytes 1081348
  24.0 2.1 %copy-start.2 = (bf16[8,128,128]{2,1,0:T(8,128)(2,1)S(1)}, bf16[8,128,128]{2,1,0:T(8,128)(2,1)}, u32[]{:S(2)}) copy-start(bf16[8,128,128]{2,1,0:T(8,128)(2,1)} %panel.5) | copy-start | bytes 786436
  24.0 2.1 %copy-start.3 = (bf16[1,4,8,1,128,128]{5,4,3,2,1,0:T(8,128)(2,1)S(1)}, bf16[1,4,8,1,128,128]{5,4,3,2,1,0:T(8,128)(2,1)}, u32[]{:S(2)}) copy-start(bf16[1,4,8,1,128,128]{5,4,3,2,1,0:T(8,128)(2,1)} %param.9) | copy-start | bytes 3145732
  26.0 3.3 %collective-permute-start.5 = (bf16[4,11,128,128]{3,2,1,0:T(8,128)(2,1)S(1)}, bf16[4,11,128,128]{3,2,1,0:T(8,128)(2,1)S(1)}, u32[]{:S(2)}, u32[]{:S(2)}) collective-permute-start(bf16[4,11,128,128]{3,2,1,0:T(8,128)(2,1)S(1)} %stack.1.near), channel_id=1, source_target_pairs={{0,4},{4,0},{8,12},{12,8},{16,20},{20,16},{24,28},{28,24},{1,5},{5... | collective-permute-start | bytes 4325384 | tf_op jit(solution)/shard_map/ppermute | solution.py:23
  27.4 6.2 %collective-permute-start.7 = (bf16[4,11,128,128]{3,2,1,0:T(8,128)(2,1)S(1)}, bf16[4,11,128,128]{3,2,1,0:T(8,128)(2,1)S(1)}, u32[]{:S(2)}, u32[]{:S(2)}) collective-permute-start(bf16[4,11,128,128]{3,2,1,0:T(8,128)(2,1)S(1)} %get-tuple-element.43), channel_id=1, source_target_pairs={{0,4},{4,0},{8,12},{12,8},{16,20},{20,16},{24,28},{28,24},{1,5},{5... | collective-permute-start | bytes 4325384 | tf_op jit(solution)/shard_map/ppermute | solution.py:23
  28.0 1.3 %copy-start.6 = (s32[8]{0:T(128)S(1)}, s32[8]{0:T(128)}, u32[]{:S(2)}) copy-start(s32[8]{0:T(128)} %parents.5) | copy-start | bytes 100
  31.7 2.1 %collective-permute-start.6 = (f32[4,19,16,128]{3,2,1,0:T(8,128)S(1)}, f32[4,19,16,128]{3,2,1,0:T(8,128)S(1)}, u32[]{:S(2)}, u32[]{:S(2)}) collective-permute-start(f32[4,19,16,128]{3,2,1,0:T(8,128)S(1)} %get-tuple-element.41), channel_id=1, source_target_pairs={{0,4},{4,0},{8,12},{12,8},{16,20},{20,16},{24,28},{28,24},{1,5},{5... | collective-permute-start | bytes 1867784 | tf_op jit(solution)/shard_map/ppermute | solution.py:23
  31.9 14.1 %collective-permute-start.16 = (bf16[11,128,128]{2,1,0:T(8,128)(2,1)S(1)}, bf16[11,128,128]{2,1,0:T(8,128)(2,1)S(1)}, u32[]{:S(2)}, u32[]{:S(2)}) collective-permute-start(bf16[11,128,128]{2,1,0:T(8,128)(2,1)S(1)} %get-tuple-element.49), channel_id=1, source_target_pairs={{0,1},{1,2},{2,3},{3,0},{4,5},{5,6},{6,7},{7,4},{8,9},{9,10},{10,1... | collective-permute-start | bytes 1081352 | tf_op jit(solution)/shard_map/ppermute | solution.py:265
  33.9 4.8 %collective-permute-start.8 = (bf16[19,16,128]{2,1,0:T(8,128)(2,1)S(1)}, bf16[19,16,128]{2,1,0:T(8,128)(2,1)S(1)}, u32[]{:S(2)}, u32[]{:S(2)}) collective-permute-start(bf16[19,16,128]{2,1,0:T(8,128)(2,1)S(1)} %get-tuple-element.78), channel_id=1, source_target_pairs={{0,8},{4,12},{8,0},{12,4},{16,24},{20,28},{24,16},{28,20},{1,9},{5... | collective-permute-start | bytes 233480 | tf_op jit(solution)/shard_map/ppermute | solution.py:23
  35.5 6.2 %collective-permute-start.10 = (bf16[19,16,128]{2,1,0:T(8,128)(2,1)S(1)}, bf16[19,16,128]{2,1,0:T(8,128)(2,1)S(1)}, u32[]{:S(2)}, u32[]{:S(2)}) collective-permute-start(bf16[19,16,128]{2,1,0:T(8,128)(2,1)S(1)} %get-tuple-element.79), channel_id=1, source_target_pairs={{0,24},{4,28},{8,16},{12,20},{16,8},{20,12},{24,0},{28,4},{1,25},{... | collective-permute-start | bytes 233480 | tf_op jit(solution)/shard_map/ppermute | solution.py:23
  36.9 5.9 %collective-permute-start.9 = (bf16[19,16,128]{2,1,0:T(8,128)(2,1)S(1)}, bf16[19,16,128]{2,1,0:T(8,128)(2,1)S(1)}, u32[]{:S(2)}, u32[]{:S(2)}) collective-permute-start(bf16[19,16,128]{2,1,0:T(8,128)(2,1)S(1)} %get-tuple-element.80), channel_id=1, source_target_pairs={{0,16},{4,20},{8,24},{12,28},{16,0},{20,4},{24,8},{28,12},{1,17},{... | collective-permute-start | bytes 233480 | tf_op jit(solution)/shard_map/ppermute | solution.py:23
  38.9 13.4 %collective-permute-start.15 = (bf16[2,6,128,128]{3,2,1,0:T(8,128)(2,1)S(1)}, bf16[2,6,128,128]{3,2,1,0:T(8,128)(2,1)S(1)}, u32[]{:S(2)}, u32[]{:S(2)}) collective-permute-start(bf16[2,6,128,128]{3,2,1,0:T(8,128)(2,1)S(1)} %slice.95), channel_id=1, source_target_pairs={{0,16},{4,20},{8,24},{12,28},{16,0},{20,4},{24,8},{28,12},{1,17},{... | collective-permute-start | bytes 1179656 | tf_op jit(solution)/shard_map/ppermute | solution.py:23
  40.6 11.7 %collective-permute-start.14 = (bf16[2,5,128,128]{3,2,1,0:T(8,128)(2,1)S(1)}, bf16[2,5,128,128]{3,2,1,0:T(8,128)(2,1)S(1)}, u32[]{:S(2)}, u32[]{:S(2)}) collective-permute-start(bf16[2,5,128,128]{3,2,1,0:T(8,128)(2,1)S(1)} %fusion.1), channel_id=1, source_target_pairs={{0,8},{4,12},{8,0},{12,4},{16,24},{20,28},{24,16},{28,20},{1,9},{5... | collective-permute-start | bytes 983048 | tf_op jit(solution)/shard_map/ppermute | solution.py:23
  42.8 6.3 %collective-permute-start.13 = (bf16[19,16,128]{2,1,0:T(8,128)(2,1)S(1)}, bf16[19,16,128]{2,1,0:T(8,128)(2,1)S(1)}, u32[]{:S(2)}, u32[]{:S(2)}) collective-permute-start(bf16[19,16,128]{2,1,0:T(8,128)(2,1)S(1)} %fusion.7.refs_0_), channel_id=1, source_target_pairs={{0,1},{1,2},{2,3},{3,0},{4,5},{5,6},{6,7},{7,4},{8,9},{9,10},{10,1... | collective-permute-start | bytes 233480 | tf_op jit(solution)/shard_map/ppermute | solution.py:28
  44.5 6.3 %collective-permute-start.12 = (bf16[19,16,128]{2,1,0:T(8,128)(2,1)S(1)}, bf16[19,16,128]{2,1,0:T(8,128)(2,1)S(1)}, u32[]{:S(2)}, u32[]{:S(2)}) collective-permute-start(bf16[19,16,128]{2,1,0:T(8,128)(2,1)S(1)} %fusion.7.refs_0_), channel_id=1, source_target_pairs={{0,2},{1,3},{2,0},{3,1},{4,6},{5,7},{6,4},{7,5},{8,10},{9,11},{10,... | collective-permute-start | bytes 233480 | tf_op jit(solution)/shard_map/ppermute | solution.py:28
  46.0 6.3 %collective-permute-start.11 = (bf16[19,16,128]{2,1,0:T(8,128)(2,1)S(1)}, bf16[19,16,128]{2,1,0:T(8,128)(2,1)S(1)}, u32[]{:S(2)}, u32[]{:S(2)}) collective-permute-start(bf16[19,16,128]{2,1,0:T(8,128)(2,1)S(1)} %fusion.7.refs_0_), channel_id=1, source_target_pairs={{0,3},{1,0},{2,1},{3,2},{4,7},{5,4},{6,5},{7,6},{8,11},{9,8},{10,9... | collective-permute-start | bytes 233480 | tf_op jit(solution)/shard_map/ppermute | solution.py:28
  52.6 4.5 %collective-permute-start.19 = (bf16[1,19,16,128]{3,2,1,0:T(8,128)(2,1)S(1)}, bf16[1,19,16,128]{3,2,1,0:T(8,128)(2,1)S(1)}, u32[]{:S(2)}, u32[]{:S(2)}) collective-permute-start(bf16[1,19,16,128]{3,2,1,0:T(8,128)(2,1)S(1)} %bitcast.44), channel_id=1, source_target_pairs={{0,8},{4,12},{8,0},{12,4},{16,24},{20,28},{24,16},{28,20},{1,9},{5... | collective-permute-start | bytes 233480 | tf_op jit(solution)/shard_map/ppermute | solution.py:23
  53.3 9.2 %collective-permute-start.17 = (bf16[5,128,128]{2,1,0:T(8,128)(2,1)S(1)}, bf16[5,128,128]{2,1,0:T(8,128)(2,1)S(1)}, u32[]{:S(2)}, u32[]{:S(2)}) collective-permute-start(bf16[5,128,128]{2,1,0:T(8,128)(2,1)S(1)} %fusion.3), channel_id=1, source_target_pairs={{0,16},{4,20},{8,24},{12,28},{16,0},{20,4},{24,8},{28,12},{1,17},{... | collective-permute-start | bytes 491528 | tf_op jit(solution)/shard_map/ppermute | solution.py:23
  57.1 7.0 %copy-start.4 = (f32[8,128,128]{2,1,0:T(8,128)S(1)}, f32[8,128,128]{2,1,0:T(8,128)}, u32[]{:S(2)}) copy-start(f32[8,128,128]{2,1,0:T(8,128)} %lower_diagonal.1) | copy-start | bytes 1572868
  57.1 7.0 %copy-start.5 = (f32[3,128,128]{2,1,0:T(8,128)S(1)}, f32[3,128,128]{2,1,0:T(8,128)}, u32[]{:S(2)}) copy-start(f32[3,128,128]{2,1,0:T(8,128)} %upper_diagonal.1) | copy-start | bytes 589828
  57.1 5.3 %collective-permute-start.20 = (bf16[2,19,16,128]{3,2,1,0:T(8,128)(2,1)S(1)}, bf16[2,19,16,128]{3,2,1,0:T(8,128)(2,1)S(1)}, u32[]{:S(2)}, u32[]{:S(2)}) collective-permute-start(bf16[2,19,16,128]{3,2,1,0:T(8,128)(2,1)S(1)} %pad_maximum_fusion.1), channel_id=1, source_target_pairs={{0,16},{4,20},{8,24},{12,28},{16,0},{20,4},{24,8},{28,12},{1,17},{... | collective-permute-start | bytes 466952 | tf_op jit(solution)/shard_map/ppermute | solution.py:23
  57.9 5.7 %collective-permute-start.18 = (bf16[6,128,128]{2,1,0:T(8,128)(2,1)S(1)}, bf16[6,128,128]{2,1,0:T(8,128)(2,1)S(1)}, u32[]{:S(2)}, u32[]{:S(2)}) collective-permute-start(bf16[6,128,128]{2,1,0:T(8,128)(2,1)S(1)} %fusion.2), channel_id=1, source_target_pairs={{0,8},{4,12},{8,0},{12,4},{16,24},{20,28},{24,16},{28,20},{1,9},{5... | collective-permute-start | bytes 589832 | tf_op jit(solution)/shard_map/ppermute | solution.py:23
  59.3 11.0 %collective-permute-start.22 = (bf16[11,128,128]{2,1,0:T(8,128)(2,1)S(1)}, bf16[11,128,128]{2,1,0:T(8,128)(2,1)S(1)}, u32[]{:S(2)}, u32[]{:S(2)}) collective-permute-start(bf16[11,128,128]{2,1,0:T(8,128)(2,1)S(1)} %get-tuple-element.63), channel_id=1, source_target_pairs={{0,2},{3,1},{4,6},{7,5},{8,10},{11,9},{12,14},{15,13},{16,18},{19,... | collective-permute-start | bytes 1081352 | tf_op jit(solution)/shard_map/ppermute | solution.py:265
  62.4 1.7 %collective-permute-start.21 = (bf16[4,19,16,128]{3,2,1,0:T(8,128)(2,1)S(1)}, bf16[4,19,16,128]{3,2,1,0:T(8,128)(2,1)S(1)}, u32[]{:S(2)}, u32[]{:S(2)}) collective-permute-start(bf16[4,19,16,128]{3,2,1,0:T(8,128)(2,1)S(1)} %pad_maximum_fusion.near), channel_id=1, source_target_pairs={{0,4},{4,0},{8,12},{12,8},{16,20},{20,16},{24,28},{28,24},{1,5},{5... | collective-permute-start | bytes 933896 | tf_op jit(solution)/shard_map/ppermute | solution.py:23
  62.5 7.8 %copy-start.7 = (s32[3,1,1]{0,2,1:T(1,128)S(1)}, s32[3,1,1]{0,2,1:T(1,128)}, u32[]{:S(2)}) copy-start(s32[3,1,1]{0,2,1:T(1,128)} %param.11) | copy-start | bytes 40
  62.5 7.8 %copy-start.8 = (s32[8,1,1]{0,2,1:T(1,128)S(1)}, s32[8,1,1]{0,2,1:T(1,128)}, u32[]{:S(2)}) copy-start(s32[8,1,1]{0,2,1:T(1,128)} %param.14) | copy-start | bytes 100
where the time goes:
time: 72 us; the launch traced here: 71.8 us
  waiting for transfers between devices  31.5 us (44%)
  starting transfers between devices  26.7 us (37%)
  Pallas kernels  10.5 us (15%)
  local copies, waits for them, and re-layouts  1.32 us (2%)
  between operations  0.91 us (1%)
  other arithmetic  0.9 us (1%)
    ppermute x16, starting transfers between devices, flip(): return lax.ppermute(value, axis, [(i, i ^ mask) for i in range(size)])  15 us
    ppermute x2, waiting for transfers between devices, gather_pair(): lax.ppermute(value, axis, [(b, c) for c, b in pairs(lax.axis_size(axis),...  12.1 us
    pallas_call x10, Pallas kernels, call(): pl.pallas_call(kernel, out_shape=outs, in_specs=[SMEM] * len(scalars) + [...  10.5 us
    ppermute x16, waiting for transfers between devices, flip(): return lax.ppermute(value, axis, [(i, i ^ mask) for i in range(size)])  10 us
    ppermute x3, waiting for transfers between devices, shift(): lax.ppermute(value, axis, [(i, (i + step) % size) for i in range(size)])  5.35 us
    ppermute x2, starting transfers between devices, gather_pair(): lax.ppermute(value, axis, [(b, c) for c, b in pairs(lax.axis_size(axis),...  4.56 us
    ppermute x3, starting transfers between devices, shift(): lax.ppermute(value, axis, [(i, (i + step) % size) for i in range(size)])  4.16 us
    ppermute x2, waiting for transfers between devices, return_pair(): return lax.ppermute(value, axis, pairs(lax.axis_size(axis), offset))  4.05 us
  transfers between devices with their start and end apart: 23, of which 15 were waited for; matrix products, arithmetic and copies ran while one was open for 1% of the time, Pallas kernels for 10%

commit v1 on v0

--- a/solution.py
+++ b/solution.py
@@ -121,11 +121,43 @@
         out[first // 2] = dot_pair(top[0], near, first, min(first + 1, total - 1))
 
 
+def triangle(block):
+    rows = lax.broadcasted_iota(jnp.int32, (block, block), 0)
+    lanes = lax.broadcasted_iota(jnp.int32, (block, block), 1)
+    return rows < lanes, rows == lanes
+
+
+def pack(squares, packed, start):
+    total, block = squares.shape[:2]
+    above, diagonal = triangle(block)
+    for p in range(total // 2):
+        first, second = [squares[k] + squares[k].T for k in (2 * p, 2 * p + 1)]
+        packed[p * block : (p + 1) * block] = jnp.where(above, first, second)
+        row = jnp.sum(jnp.where(diagonal, first, 0.0), axis=0, keepdims=True)
+        packed[start + p : start + p + 1] = row
+    if total % 2:
+        packed[(total // 2) * block : (total // 2 + 1) * block] = squares[total - 1] + squares[total - 1].T
+
+
+def unpack(packed, total, block, start):
+    above, diagonal = triangle(block)
+    squares = []
+    for p in range(total // 2):
+        value = packed[p * block : (p + 1) * block]
+        turned = value.T
+        row = packed[start + p : start + p + 1]
+        squares.append(jnp.where(above, value, jnp.where(diagonal, row, turned)))
+        squares.append(jnp.where(above, turned, value))
+    if total % 2:
+        squares.append(packed[(total // 2) * block : (total // 2 + 1) * block])
+    return squares
+
+
 def second_kernel(uppers, parents, top, far, start, turned, *refs):
-    own, returns, (sums_keep, sums_away, both, forms) = refs[0], refs[1:-4], refs[-4:]
+    own, returns, (sums_keep, sums_away, both, squares, packed) = refs[0], refs[1:-5], refs[-5:]
     total, block, reach = turned.shape
     lowers = total - uppers
-    half, _, chunk, _ = sums_keep.shape
+    half, chunk, _ = sums_keep.shape
     row = lax.axis_index("row")
 
     for first in range(0, total, 2):
@@ -145,22 +177,21 @@
         value = jnp.dot(rows, both[k], preferred_element_type=F32)
         return value[:, :block] + value[:, block:]
 
-    def spread(slot, index):
-        for m in range(2 * half):
-            place = pl.multiple_of((row ^ m) * chunk, chunk)
-            (sums_away if m & 1 else sums_keep)[m // 2, index] = forms[slot, pl.ds(place, chunk)]
-
+    base = (total + 1) // 2 * block
     for k in range(uppers):
-        forms[k] = fold(turned[k], k)
-        spread(k, k)
+        squares[k] = fold(turned[k], k)
     for m in range(lowers):
         own_row, parent = turned[uppers + m], parents[m]
         value = fold(jnp.concatenate([own_row, turned[parent]], axis=0), uppers + m)
-        slot = uppers + 2 * m
-        forms[slot] = value[:block]
-        forms[slot + 1] = value[block:] + fold(own_row, parent).T
-        spread(slot, total + m)
-        spread(slot + 1, uppers + m)
+        squares[uppers + m] = value[:block]
+        place = base + m * block
+        packed[place : place + block] = value[block:] + fold(own_row, parent).T
+    end = base + lowers * block
+    packed[end:] = jnp.zeros((packed.shape[0] - end, block), F32)
+    pack(squares, packed, end)
+    for m in range(2 * half):
+        place = pl.multiple_of((row ^ m) * chunk, chunk)
+        (sums_away if m & 1 else sums_keep)[m // 2] = packed[pl.ds(place, chunk)]
 
 
 def line_kernel(*refs):
@@ -211,18 +242,20 @@
     upper_out,
     cross_out,
     lower_out,
-    sums,
+    packed,
     halves,
 ):
     uppers, lowers = upper_out.shape[0], lower_out.shape[0]
     block = panel.shape[-1]
-    chunk = block // width
+    chunk = near.shape[1]
     row = lax.axis_index("row")
     for m in range(width):
-        start = pl.multiple_of((row ^ m) * chunk, chunk)
-        sums[:, pl.ds(start, chunk)] = (far if m & 1 else near)[m // 2].astype(F32)
+        place = pl.multiple_of((row ^ m) * chunk, chunk)
+        packed[pl.ds(place, chunk)] = (far if m & 1 else near)[m // 2].astype(F32)
+    base = (uppers + lowers + 1) // 2 * block
+    squares = unpack(packed, uppers + lowers, block, base + lowers * block)
     for k in range(uppers):
-        value = upper_diagonal[k] + (sums[k] + sums[k].T)
+        value = upper_diagonal[k] + squares[k]
         upper_out[k] = value
         halves[k, :block], halves[k, block:] = split(value)
     products = [
@@ -230,7 +263,7 @@
     ]
     rights = []
     for m in range(lowers):
-        forms = sums[uppers + m]
+        forms = packed[base + m * block : base + (m + 1) * block]
         cross = forms - (products[m][:block] + products[m][block:])
         cross_out[m] = cross
         rights.append(jnp.concatenate([forms.astype(jnp.bfloat16), *split(cross)], axis=1))
@@ -239,10 +272,8 @@
     ]
     for m in range(lowers):
         value = backs[m]
-        square = sums[uppers + lowers + m]
-        turned = (square - value[:, :block]).T
         rest = value[:, block : 2 * block] + value[:, 2 * block :]
-        lower_out[m] = lower_diagonal[m] + (square - rest) + turned
+        lower_out[m] = lower_diagonal[m] + squares[uppers + m] - rest - value[:, :block].T
 
 
 def gather_shifts(value, axis):
@@ -308,9 +339,10 @@
     uppers, block = upper_panel.shape[0], upper_panel.shape[-1]
     lowers = lower_panel.shape[0]
     total = uppers + lowers
-    sums_n = total + lowers
     width, depth = lax.axis_size("row"), lax.axis_size("col")
-    half, chunk = width // 2, block // width
+    half = width // 2
+    packed_n = (total + 1) // 2 * block + lowers * block + total // 2
+    chunk = ceil_to(packed_n, 16 * width) // width
     bf16 = jnp.bfloat16
     upper_pattern, lower_pattern = upper_pattern.reshape(-1), lower_pattern.reshape(-1)
 
@@ -375,10 +407,11 @@
         (top, far, start, turned),
         [shape_of((total, block, block), F32)]
         + [shape_of((total, block, block), WIRE)] * reach
-        + [shape_of((half, sums_n, chunk, block), F32)] * 2,
+        + [shape_of((half, chunk, block), F32)] * 2,
         [
             shape_of((total, (reach + 1) * block, 2 * block), bf16),
-            shape_of((sums_n, block, block), F32),
+            shape_of((total, block, block), F32),
+            shape_of((width * chunk, block), F32),
         ],
     )
     returns, (sums_keep, sums_away) = rest[:-2], rest[-2:]
@@ -404,14 +437,14 @@
         "line",
         (),
         tied[:depth],
-        [shape_of((sums_n, chunk, block), WIRE)],
-        [shape_of((depth, sums_n, chunk, block), F32)],
+        [shape_of((chunk, block), WIRE)],
+        [shape_of((depth, chunk, block), F32)],
     )
     sides = [keep + got.astype(F32) for (keep, _), got in zip(halves, tied[depth : depth + 2])]
     part, last, *sides = tie(part, returns[-1], *sides)
     near = gather_doubles(part, "row")
-    far = flip(near, "row", 1)
-    got = [*early, return_pair(last, "col", reach)]
+    far, last = tie(flip(near, "row", 1), return_pair(last, "col", reach))
+    got = [*early, last]
     front, back = sides
     for i in range(1, len(bits)):
         keep, across = halve(front, "row", bits[i], bits[i:])
@@ -430,9 +463,8 @@
             shape_of((lowers, block, block), F32),
             shape_of((lowers, block, block), F32),
         ],
-        [shape_of((sums_n, block, block), F32), shape_of((uppers, 2 * block, block), bf16)],
-    )
-    upper_blocks, *got = tie(upper_blocks, *got)
+        [shape_of((width * chunk, block), F32), shape_of((uppers, 2 * block, block), bf16)],
+    )
     upper_columns, lower_columns = call(
         columns_kernel,
         "columns",

time: 72 us -> 69.6 us (0.967)
  the two profiles are of different devices: /device:TPU:8 before, /device:TPU:0 now
where the time goes in v1:
time: 69.6 us; the launch traced here: 69.4 us
  starting transfers between devices  31.9 us (46%)
  waiting for transfers between devices  23.8 us (34%)
  Pallas kernels  10.6 us (15%)
  local copies, waits for them, and re-layouts  1.32 us (2%)
  between operations  0.92 us (1%)
  other arithmetic  0.86 us (1%)
    ppermute x16, starting transfers between devices, flip(): return lax.ppermute(value, axis, [(i, i ^ mask) for i in range(size)])  14.8 us
    ppermute x2, waiting for transfers between devices, gather_pair(): lax.ppermute(value, axis, [(b, c) for c, b in pairs(lax.axis_size(axis),...  11.8 us
    pallas_call x10, Pallas kernels, call(): pl.pallas_call(kernel, out_shape=outs, in_specs=[SMEM] * len(scalars) + [...  10.6 us
    ppermute x16, waiting for transfers between devices, flip(): return lax.ppermute(value, axis, [(i, i ^ mask) for i in range(size)])  8.42 us
    ppermute x2, starting transfers between devices, gather_pair(): lax.ppermute(value, axis, [(b, c) for c, b in pairs(lax.axis_size(axis),...  6.38 us
    ppermute x3, starting transfers between devices, shift(): lax.ppermute(value, axis, [(i, (i + step) % size) for i in range(size)])  5.36 us
    ppermute x2, starting transfers between devices, return_pair(): return lax.ppermute(value, axis, pairs(lax.axis_size(axis), offset))  5.32 us
    ppermute x3, waiting for transfers between devices, shift(): lax.ppermute(value, axis, [(i, (i + step) % size) for i in range(size)])  2.83 us
  transfers between devices with their start and end apart: 23, of which 13 were waited for; matrix products, arithmetic and copies ran while one was open for 1% of the time, Pallas kernels for 7%

profile of v1, /device:TPU:0, one launch (start us, length us, event | category | flops | bytes accessed | tf_op | source)
XLA Modules:
  0.0 69.4 jit_solution(6549252045510512467)
XLA Ops:
  0.6 1.8 %mask.1.refs_0_ = bf16[11,128,128]{2,1,0:T(8,128)(2,1)} custom-call(s32[3]{0:T(128)} %bitcast.47, s32[8]{0:T(128)} %bitcast.49, bf16[3,128,128]{2,1,0:T(8,128)(2,1)} %bitcast.54, bf16[8,128,128]{2,1,0:T(8,128)(2,1)} %bitcast.53), custom_call_target="tpu_custom_call" | custom-call | tf_op jit(solution)/shard_map/mask/pallas_call | solution.py:41
  2.4 1.3 %collective-permute-start.4 = (bf16[11,128,128]{2,1,0:T(8,128)(2,1)}, bf16[11,128,128]{2,1,0:T(8,128)(2,1)S(1)}, u32[]{:S(2)}, u32[]{:S(2)}) collective-permute-start(bf16[11,128,128]{2,1,0:T(8,128)(2,1)} %mask.1.refs_0_), channel_id=1, source_target_pairs={{2,0},{1,3},{6,4},{5,7},{10,8},{9,11},{14,12},{13,15},{18,16},{17,... | collective-permute-start | bytes 1081352 | tf_op jit(solution)/shard_map/ppermute | solution.py:292
  3.7 5.1 %collective-permute-start.3 = (bf16[11,128,128]{2,1,0:T(8,128)(2,1)}, bf16[11,128,128]{2,1,0:T(8,128)(2,1)S(1)}, u32[]{:S(2)}, u32[]{:S(2)}) collective-permute-start(bf16[11,128,128]{2,1,0:T(8,128)(2,1)} %mask.1.refs_0_), channel_id=1, source_target_pairs={{1,0},{2,1},{3,2},{0,3},{5,4},{6,5},{7,6},{4,7},{9,8},{10,9},{11,1... | collective-permute-start | bytes 1081352 | tf_op jit(solution)/shard_map/ppermute | solution.py:292
  8.8 2.4 %collective-permute-start.2 = (bf16[11,128,128]{2,1,0:T(8,128)(2,1)}, bf16[11,128,128]{2,1,0:T(8,128)(2,1)S(1)}, u32[]{:S(2)}, u32[]{:S(2)}) collective-permute-start(bf16[11,128,128]{2,1,0:T(8,128)(2,1)} %mask.1.refs_0_), channel_id=1, source_target_pairs={{0,24},{4,28},{8,16},{12,20},{16,8},{20,12},{24,0},{28,4},{1,25},{... | collective-permute-start | bytes 1081352 | tf_op jit(solution)/shard_map/ppermute | solution.py:23
  11.3 0.5 collective-permute-start.1
  11.8 0.5 collective-permute-start
  12.3 4.9 %collective-permute-done.4.refs_2_.refs_1_ = bf16[11,128,128]{2,1,0:T(8,128)(2,1)S(1)} collective-permute-done((bf16[11,128,128]{2,1,0:T(8,128)(2,1)}, bf16[11,128,128]{2,1,0:T(8,128)(2,1)S(1)}, u32[]{:S(2)}, u32[]{:S(2)}) %collective-permute-start.4) | collective-permute-done | bytes 360480 | tf_op jit(solution)/shard_map/ppermute | solution.py:292
  17.2 6.9 %collective-permute-done.3.refs_1_.refs_0_ = bf16[11,128,128]{2,1,0:T(8,128)(2,1)S(1)} collective-permute-done((bf16[11,128,128]{2,1,0:T(8,128)(2,1)}, bf16[11,128,128]{2,1,0:T(8,128)(2,1)S(1)}, u32[]{:S(2)}, u32[]{:S(2)}) %collective-permute-start.3) | collective-permute-done | bytes 360480 | tf_op jit(solution)/shard_map/ppermute | solution.py:292
  24.1 1.0 %copy-done = bf16[11,128,128]{2,1,0:T(8,128)(2,1)S(1)} copy-done((bf16[11,128,128]{2,1,0:T(8,128)(2,1)S(1)}, bf16[11,128,128]{2,1,0:T(8,128)(2,1)}, u32[]{:S(2)}) %copy-start) | copy-done | bytes 360472
  25.1 0.3 turn.1.refs_4_.turned
  25.4 0.0 copy-start.2
  25.4 0.0 copy-start.3
  25.4 0.0 collective-permute-done.2.refs_3_
  25.4 2.1 %collective-permute-done.1.refs_2_ = bf16[11,128,128]{2,1,0:T(8,128)(2,1)S(1)} collective-permute-done((bf16[11,128,128]{2,1,0:T(8,128)(2,1)}, bf16[11,128,128]{2,1,0:T(8,128)(2,1)S(1)}, u32[]{:S(2)}, u32[]{:S(2)}) %collective-permute-start.1) | collective-permute-done | bytes 360480 | tf_op jit(solution)/shard_map/ppermute | solution.py:23
  27.5 0.1 collective-permute-done.refs_1_
  27.6 0.1 stack.1.near
  27.7 0.1 collective-permute-start.5
  27.8 0.4 top.1
  28.2 1.0 %partial.1 = (f32[4,11,128,128]{3,2,1,0:T(8,128)S(1)}, bf16[4,11,128,128]{3,2,1,0:T(8,128)(2,1)S(1)}) custom-call(bf16[1024,256]{1,0:T(8,128)(2,1)S(1)} %get-tuple-element.41.top, bf16[11,128,128]{2,1,0:T(8,128)(2,1)S(1)} %collective-permute-done.3.refs_1_.refs_0_, bf16[11,128,128]{2,1,0:T(8,128)(2,1)S(1)} %collective-permute-done.4.refs_2_.refs_1_), custom_call_target="tpu_custom_call" | custom-call | tf_op jit(solution)/shard_map/partial/pallas_call | solution.py:41
  29.2 0.5 collective-permute-start.7
  29.7 0.8 %first.1.start = f32[6,384,256]{2,1,0:T(8,128)S(1)} custom-call(bf16[2,384,512]{2,1,0:T(8,128)(2,1)S(1)} %get-tuple-element.37.top, bf16[4,11,128,128]{3,2,1,0:T(8,128)(2,1)S(1)} %stack.1.near), custom_call_target="tpu_custom_call" | custom-call | tf_op jit(solution)/shard_map/first/pallas_call | solution.py:41
  30.5 0.5 collective-permute-done.5.far
  31.0 2.5 %second.1 = (f32[11,128,128]{2,1,0:T(8,128)S(1)}, bf16[11,128,128]{2,1,0:T(8,128)(2,1)S(1)}, bf16[11,128,128]{2,1,0:T(8,128)(2,1)S(1)}, f32[4,240,128]{2,1,0:T(8,128)S(1)}, f32[4,240,128]{2,1,0:T(8,128)S(1)}) custom-call(s32[8]{0:T(128)S(1)} %copy-done.6, bf16[2,384,512]{2,1,0:T(8,128)(2,1)S(1)} %get-tuple-element.37.top, ...), custom_call_target="tpu_custom_call" | custom-call | tf_op jit(solution)/shard_map/second/pallas_call | solution.py:41
  33.5 0.2 collective-permute-start.6
  33.7 1.3 %collective-permute-start.16 = (bf16[11,128,128]{2,1,0:T(8,128)(2,1)S(1)}, bf16[11,128,128]{2,1,0:T(8,128)(2,1)S(1)}, u32[]{:S(2)}, u32[]{:S(2)}) collective-permute-start(bf16[11,128,128]{2,1,0:T(8,128)(2,1)S(1)} %get-tuple-element.48), channel_id=1, source_target_pairs={{0,1},{1,2},{2,3},{3,0},{4,5},{5,6},{6,7},{7,4},{8,9},{9,10},{10,1... | collective-permute-start | bytes 1081352 | tf_op jit(solution)/shard_map/ppermute | solution.py:296
  35.0 0.0 collective-permute-done.7
  35.0 0.4 collective-permute-done.6
  35.5 0.1 fusion.8
  35.6 1.6 %collective-permute-start.8 = (bf16[240,128]{1,0:T(8,128)(2,1)S(1)}, bf16[240,128]{1,0:T(8,128)(2,1)S(1)}, u32[]{:S(2)}, u32[]{:S(2)}) collective-permute-start(bf16[240,128]{1,0:T(8,128)(2,1)S(1)} %get-tuple-element.76), channel_id=1, source_target_pairs={{0,8},{4,12},{8,0},{12,4},{16,24},{20,28},{24,16},{28,20},{1,9},{5... | collective-permute-start | bytes 184328 | tf_op jit(solution)/shard_map/ppermute | solution.py:23
  37.1 1.4 %collective-permute-start.10 = (bf16[240,128]{1,0:T(8,128)(2,1)S(1)}, bf16[240,128]{1,0:T(8,128)(2,1)S(1)}, u32[]{:S(2)}, u32[]{:S(2)}) collective-permute-start(bf16[240,128]{1,0:T(8,128)(2,1)S(1)} %get-tuple-element.77), channel_id=1, source_target_pairs={{0,24},{4,28},{8,16},{12,20},{16,8},{20,12},{24,0},{28,4},{1,25},{... | collective-permute-start | bytes 184328 | tf_op jit(solution)/shard_map/ppermute | solution.py:23
  38.5 0.6 collective-permute-start.9
  39.1 0.5 convert_add_fusion
  39.6 0.4 collective-permute-done.8
  40.0 0.1 slice.95
  40.1 0.1 slice.55
  40.2 1.6 %collective-permute-start.15 = (bf16[2,6,128,128]{3,2,1,0:T(8,128)(2,1)S(1)}, bf16[2,6,128,128]{3,2,1,0:T(8,128)(2,1)S(1)}, u32[]{:S(2)}, u32[]{:S(2)}) collective-permute-start(bf16[2,6,128,128]{3,2,1,0:T(8,128)(2,1)S(1)} %slice.95), channel_id=1, source_target_pairs={{0,16},{4,20},{8,24},{12,28},{16,0},{20,4},{24,8},{28,12},{1,17},{... | collective-permute-start | bytes 1179656 | tf_op jit(solution)/shard_map/ppermute | solution.py:23
  41.8 0.1 fusion.1
  41.9 1.0 %collective-permute-start.14 = (bf16[2,5,128,128]{3,2,1,0:T(8,128)(2,1)S(1)}, bf16[2,5,128,128]{3,2,1,0:T(8,128)(2,1)S(1)}, u32[]{:S(2)}, u32[]{:S(2)}) collective-permute-start(bf16[2,5,128,128]{3,2,1,0:T(8,128)(2,1)S(1)} %fusion.1), channel_id=1, source_target_pairs={{0,8},{4,12},{8,0},{12,4},{16,24},{20,28},{24,16},{28,20},{1,9},{5... | collective-permute-start | bytes 983048 | tf_op jit(solution)/shard_map/ppermute | solution.py:23
  42.9 0.0 collective-permute-done.10
  42.9 0.7 %collective-permute-done.9 = bf16[240,128]{1,0:T(8,128)(2,1)S(1)} collective-permute-done((bf16[240,128]{1,0:T(8,128)(2,1)S(1)}, bf16[240,128]{1,0:T(8,128)(2,1)S(1)}, u32[]{:S(2)}, u32[]{:S(2)}) %collective-permute-start.9) | collective-permute-done | bytes 61472 | tf_op jit(solution)/shard_map/ppermute | solution.py:23
  43.7 1.3 %collective-permute-start.13 = (bf16[240,128]{1,0:T(8,128)(2,1)S(1)}, bf16[240,128]{1,0:T(8,128)(2,1)S(1)}, u32[]{:S(2)}, u32[]{:S(2)}) collective-permute-start(bf16[240,128]{1,0:T(8,128)(2,1)S(1)} %fusion.7.refs_0_), channel_id=1, source_target_pairs={{0,1},{1,2},{2,3},{3,0},{4,5},{5,6},{6,7},{7,4},{8,9},{9,10},{10,1... | collective-permute-start | bytes 184328 | tf_op jit(solution)/shard_map/ppermute | solution.py:28
  45.0 2.0 %collective-permute-start.12 = (bf16[240,128]{1,0:T(8,128)(2,1)S(1)}, bf16[240,128]{1,0:T(8,128)(2,1)S(1)}, u32[]{:S(2)}, u32[]{:S(2)}) collective-permute-start(bf16[240,128]{1,0:T(8,128)(2,1)S(1)} %fusion.7.refs_0_), channel_id=1, source_target_pairs={{0,2},{1,3},{2,0},{3,1},{4,6},{5,7},{6,4},{7,5},{8,10},{9,11},{10,... | collective-permute-start | bytes 184328 | tf_op jit(solution)/shard_map/ppermute | solution.py:28
  47.1 2.0 %collective-permute-start.11 = (bf16[240,128]{1,0:T(8,128)(2,1)S(1)}, bf16[240,128]{1,0:T(8,128)(2,1)S(1)}, u32[]{:S(2)}, u32[]{:S(2)}) collective-permute-start(bf16[240,128]{1,0:T(8,128)(2,1)S(1)} %fusion.7.refs_0_), channel_id=1, source_target_pairs={{0,3},{1,0},{2,1},{3,2},{4,7},{5,4},{6,5},{7,6},{8,11},{9,8},{10,9... | collective-permute-start | bytes 184328 | tf_op jit(solution)/shard_map/ppermute | solution.py:28
  49.0 1.3 %collective-permute-done.13.refs_3_ = bf16[240,128]{1,0:T(8,128)(2,1)S(1)} collective-permute-done((bf16[240,128]{1,0:T(8,128)(2,1)S(1)}, bf16[240,128]{1,0:T(8,128)(2,1)S(1)}, u32[]{:S(2)}, u32[]{:S(2)}) %collective-permute-start.13) | collective-permute-done | bytes 61472 | tf_op jit(solution)/shard_map/ppermute | solution.py:28
  50.4 1.5 %collective-permute-done.12.refs_2_ = bf16[240,128]{1,0:T(8,128)(2,1)S(1)} collective-permute-done((bf16[240,128]{1,0:T(8,128)(2,1)S(1)}, bf16[240,128]{1,0:T(8,128)(2,1)S(1)}, u32[]{:S(2)}, u32[]{:S(2)}) %collective-permute-start.12) | collective-permute-done | bytes 61472 | tf_op jit(solution)/shard_map/ppermute | solution.py:28
  51.9 0.1 convert_add_fusion.1
  52.0 0.1 fusion
  52.0 0.1 line.1
  52.1 1.2 %collective-permute-start.19 = (bf16[1,240,128]{2,1,0:T(8,128)(2,1)S(1)}, bf16[1,240,128]{2,1,0:T(8,128)(2,1)S(1)}, u32[]{:S(2)}, u32[]{:S(2)}) collective-permute-start(bf16[1,240,128]{2,1,0:T(8,128)(2,1)S(1)} %bitcast.44), channel_id=1, source_target_pairs={{0,8},{4,12},{8,0},{12,4},{16,24},{20,28},{24,16},{28,20},{1,9},{5... | collective-permute-start | bytes 184328 | tf_op jit(solution)/shard_map/ppermute | solution.py:23
  53.3 0.0 copy-start.4
  53.3 0.0 copy-start.5
  53.3 1.2 %collective-permute-start.17 = (bf16[5,128,128]{2,1,0:T(8,128)(2,1)S(1)}, bf16[5,128,128]{2,1,0:T(8,128)(2,1)S(1)}, u32[]{:S(2)}, u32[]{:S(2)}) collective-permute-start(bf16[5,128,128]{2,1,0:T(8,128)(2,1)S(1)} %fusion.3), channel_id=1, source_target_pairs={{0,16},{4,20},{8,24},{12,28},{16,0},{20,4},{24,8},{28,12},{1,17},{... | collective-permute-start | bytes 491528 | tf_op jit(solution)/shard_map/ppermute | solution.py:23
  54.6 0.5 collective-permute-start.18
  55.1 4.0 %collective-permute-start.22 = (bf16[11,128,128]{2,1,0:T(8,128)(2,1)S(1)}, bf16[11,128,128]{2,1,0:T(8,128)(2,1)S(1)}, u32[]{:S(2)}, u32[]{:S(2)}) collective-permute-start(bf16[11,128,128]{2,1,0:T(8,128)(2,1)S(1)} %get-tuple-element.60), channel_id=1, source_target_pairs={{0,2},{3,1},{4,6},{7,5},{8,10},{11,9},{12,14},{15,13},{16,18},{19,... | collective-permute-start | bytes 1081352 | tf_op jit(solution)/shard_map/ppermute | solution.py:296
  59.1 0.0 collective-permute-done.19
  59.1 1.4 %collective-permute-start.20 = (bf16[2,240,128]{2,1,0:T(8,128)(2,1)S(1)}, bf16[2,240,128]{2,1,0:T(8,128)(2,1)S(1)}, u32[]{:S(2)}, u32[]{:S(2)}) collective-permute-start(bf16[2,240,128]{2,1,0:T(8,128)(2,1)S(1)} %pad_maximum_fusion.1), channel_id=1, source_target_pairs={{0,16},{4,20},{8,24},{12,28},{16,0},{20,4},{24,8},{28,12},{1,17},{... | collective-permute-start | bytes 368648 | tf_op jit(solution)/shard_map/ppermute | solution.py:23
  60.6 3.5 %collective-permute-done.20 = bf16[2,240,128]{2,1,0:T(8,128)(2,1)S(1)} collective-permute-done((bf16[2,240,128]{2,1,0:T(8,128)(2,1)S(1)}, bf16[2,240,128]{2,1,0:T(8,128)(2,1)S(1)}, u32[]{:S(2)}, u32[]{:S(2)}) %collective-permute-start.20) | collective-permute-done | bytes 122912 | tf_op jit(solution)/shard_map/ppermute | solution.py:23
  64.1 0.0 copy-start.7
  64.1 0.0 copy-start.8
  64.1 0.1 collective-permute-start.21
  64.3 0.8 %collective-permute-done.22.refs_1_ = bf16[11,128,128]{2,1,0:T(8,128)(2,1)S(1)} collective-permute-done((bf16[11,128,128]{2,1,0:T(8,128)(2,1)S(1)}, bf16[11,128,128]{2,1,0:T(8,128)(2,1)S(1)}, u32[]{:S(2)}, u32[]{:S(2)}) %collective-permute-start.22) | collective-permute-done | bytes 360480 | tf_op jit(solution)/shard_map/ppermute | solution.py:296
  65.0 0.7 collective-permute-done.21.far
  65.7 2.1 %blocks.1 = (f32[3,128,128]{2,1,0:T(8,128)}, f32[8,128,128]{2,1,0:T(8,128)}, f32[8,128,128]{2,1,0:T(8,128)}) custom-call(s32[8]{0:T(128)S(1)} %copy-done.6, bf16[4,240,128]{2,1,0:T(8,128)(2,1)S(1)} %pad_maximum_fusion.near, bf16[4,240,128]{2,1,0:T(8,128)(2,1)S(1)} %collective-permute-done.21.far, f32[3,128,128]{2,1,0:T(8,128)S(1)} %copy-done.5, ...), custom_call_target="tpu_custom_call" | custom-call | tf_op jit(solution)/shard_map/blocks/pallas_call | solution.py:41
  67.9 1.5 %columns.1 = (bf16[3,128,128]{2,1,0:T(8,128)(2,1)}, bf16[8,128,128]{2,1,0:T(8,128)(2,1)}) custom-call(s32[8]{0:T(128)S(1)} %copy-done.6, s32[3]{0:T(128)S(1)} %bitcast.48, s32[8]{0:T(128)S(1)} %bitcast.50, bf16[8,128,128]{2,1,0:T(8,128)(2,1)S(1)} %copy-done.2, f32[11,128,128]{2,1,0:T(8,128)S(1)} %get-tuple-element.38.own, ...), custom_call_target="tpu_custom_call" | custom-call | tf_op jit(solution)/shard_map/columns/pallas_call | solution.py:41
  (25 shorter events, 0.3 us)
Async XLA Ops:
  2.4 14.8 %collective-permute-start.4 = (bf16[11,128,128]{2,1,0:T(8,128)(2,1)}, bf16[11,128,128]{2,1,0:T(8,128)(2,1)S(1)}, u32[]{:S(2)}, u32[]{:S(2)}) collective-permute-start(bf16[11,128,128]{2,1,0:T(8,128)(2,1)} %mask.1.refs_0_), channel_id=1, source_target_pairs={{2,0},{1,3},{6,4},{5,7},{10,8},{9,11},{14,12},{13,15},{18,16},{17,... | collective-permute-start | bytes 1081352 | tf_op jit(solution)/shard_map/ppermute | solution.py:292
  3.7 20.4 %collective-permute-start.3 = (bf16[11,128,128]{2,1,0:T(8,128)(2,1)}, bf16[11,128,128]{2,1,0:T(8,128)(2,1)S(1)}, u32[]{:S(2)}, u32[]{:S(2)}) collective-permute-start(bf16[11,128,128]{2,1,0:T(8,128)(2,1)} %mask.1.refs_0_), channel_id=1, source_target_pairs={{1,0},{2,1},{3,2},{0,3},{5,4},{6,5},{7,6},{4,7},{9,8},{10,9},{11,1... | collective-permute-start | bytes 1081352 | tf_op jit(solution)/shard_map/ppermute | solution.py:292
  8.8 16.6 %collective-permute-start.2 = (bf16[11,128,128]{2,1,0:T(8,128)(2,1)}, bf16[11,128,128]{2,1,0:T(8,128)(2,1)S(1)}, u32[]{:S(2)}, u32[]{:S(2)}) collective-permute-start(bf16[11,128,128]{2,1,0:T(8,128)(2,1)} %mask.1.refs_0_), channel_id=1, source_target_pairs={{0,24},{4,28},{8,16},{12,20},{16,8},{20,12},{24,0},{28,4},{1,25},{... | collective-permute-start | bytes 1081352 | tf_op jit(solution)/shard_map/ppermute | solution.py:23
  11.3 16.3 %collective-permute-start.1 = (bf16[11,128,128]{2,1,0:T(8,128)(2,1)}, bf16[11,128,128]{2,1,0:T(8,128)(2,1)S(1)}, u32[]{:S(2)}, u32[]{:S(2)}) collective-permute-start(bf16[11,128,128]{2,1,0:T(8,128)(2,1)} %mask.1.refs_0_), channel_id=1, source_target_pairs={{0,16},{4,20},{8,24},{12,28},{16,0},{20,4},{24,8},{28,12},{1,17},{... | collective-permute-start | bytes 1081352 | tf_op jit(solution)/shard_map/ppermute | solution.py:23
  11.8 15.9 %collective-permute-start = (bf16[11,128,128]{2,1,0:T(8,128)(2,1)}, bf16[11,128,128]{2,1,0:T(8,128)(2,1)S(1)}, u32[]{:S(2)}, u32[]{:S(2)}) collective-permute-start(bf16[11,128,128]{2,1,0:T(8,128)(2,1)} %mask.1.refs_0_), channel_id=1, source_target_pairs={{0,8},{4,12},{8,0},{12,4},{16,24},{20,28},{24,16},{28,20},{1,9},{5... | collective-permute-start | bytes 1081352 | tf_op jit(solution)/shard_map/ppermute | solution.py:23
  24.1 1.0 %copy-start = (bf16[11,128,128]{2,1,0:T(8,128)(2,1)S(1)}, bf16[11,128,128]{2,1,0:T(8,128)(2,1)}, u32[]{:S(2)}) copy-start(bf16[11,128,128]{2,1,0:T(8,128)(2,1)} %mask.1.refs_0_) | copy-start | bytes 1081348
  25.1 2.6 %copy-start.1 = (bf16[11,128,128]{2,1,0:T(8,128)(2,1)S(1)}, bf16[11,128,128]{2,1,0:T(8,128)(2,1)}, u32[]{:S(2)}) copy-start(bf16[11,128,128]{2,1,0:T(8,128)(2,1)} %mask.1.refs_0_) | copy-start | bytes 1081348
  25.4 2.4 %copy-start.2 = (bf16[8,128,128]{2,1,0:T(8,128)(2,1)S(1)}, bf16[8,128,128]{2,1,0:T(8,128)(2,1)}, u32[]{:S(2)}) copy-start(bf16[8,128,128]{2,1,0:T(8,128)(2,1)} %panel.5) | copy-start | bytes 786436
  25.4 2.4 %copy-start.3 = (bf16[1,4,8,1,128,128]{5,4,3,2,1,0:T(8,128)(2,1)S(1)}, bf16[1,4,8,1,128,128]{5,4,3,2,1,0:T(8,128)(2,1)}, u32[]{:S(2)}) copy-start(bf16[1,4,8,1,128,128]{5,4,3,2,1,0:T(8,128)(2,1)} %param.9) | copy-start | bytes 3145732
  27.7 3.3 %collective-permute-start.5 = (bf16[4,11,128,128]{3,2,1,0:T(8,128)(2,1)S(1)}, bf16[4,11,128,128]{3,2,1,0:T(8,128)(2,1)S(1)}, u32[]{:S(2)}, u32[]{:S(2)}) collective-permute-start(bf16[4,11,128,128]{3,2,1,0:T(8,128)(2,1)S(1)} %stack.1.near), channel_id=1, source_target_pairs={{0,4},{4,0},{8,12},{12,8},{16,20},{20,16},{24,28},{28,24},{1,5},{5... | collective-permute-start | bytes 4325384 | tf_op jit(solution)/shard_map/ppermute | solution.py:23
  29.2 5.8 %collective-permute-start.7 = (bf16[4,11,128,128]{3,2,1,0:T(8,128)(2,1)S(1)}, bf16[4,11,128,128]{3,2,1,0:T(8,128)(2,1)S(1)}, u32[]{:S(2)}, u32[]{:S(2)}) collective-permute-start(bf16[4,11,128,128]{3,2,1,0:T(8,128)(2,1)S(1)} %get-tuple-element.42), channel_id=1, source_target_pairs={{0,4},{4,0},{8,12},{12,8},{16,20},{20,16},{24,28},{28,24},{1,5},{5... | collective-permute-start | bytes 4325384 | tf_op jit(solution)/shard_map/ppermute | solution.py:23
  29.7 1.3 %copy-start.6 = (s32[8]{0:T(128)S(1)}, s32[8]{0:T(128)}, u32[]{:S(2)}) copy-start(s32[8]{0:T(128)} %parents.5) | copy-start | bytes 100
  33.5 1.9 %collective-permute-start.6 = (f32[4,240,128]{2,1,0:T(8,128)S(1)}, f32[4,240,128]{2,1,0:T(8,128)S(1)}, u32[]{:S(2)}, u32[]{:S(2)}) collective-permute-start(f32[4,240,128]{2,1,0:T(8,128)S(1)} %get-tuple-element.40), channel_id=1, source_target_pairs={{0,4},{4,0},{8,12},{12,8},{16,20},{20,16},{24,28},{28,24},{1,5},{5... | collective-permute-start | bytes 1474568 | tf_op jit(solution)/shard_map/ppermute | solution.py:23
  33.7 13.3 %collective-permute-start.16 = (bf16[11,128,128]{2,1,0:T(8,128)(2,1)S(1)}, bf16[11,128,128]{2,1,0:T(8,128)(2,1)S(1)}, u32[]{:S(2)}, u32[]{:S(2)}) collective-permute-start(bf16[11,128,128]{2,1,0:T(8,128)(2,1)S(1)} %get-tuple-element.48), channel_id=1, source_target_pairs={{0,1},{1,2},{2,3},{3,0},{4,5},{5,6},{6,7},{7,4},{8,9},{9,10},{10,1... | collective-permute-start | bytes 1081352 | tf_op jit(solution)/shard_map/ppermute | solution.py:296
  35.6 4.5 %collective-permute-start.8 = (bf16[240,128]{1,0:T(8,128)(2,1)S(1)}, bf16[240,128]{1,0:T(8,128)(2,1)S(1)}, u32[]{:S(2)}, u32[]{:S(2)}) collective-permute-start(bf16[240,128]{1,0:T(8,128)(2,1)S(1)} %get-tuple-element.76), channel_id=1, source_target_pairs={{0,8},{4,12},{8,0},{12,4},{16,24},{20,28},{24,16},{28,20},{1,9},{5... | collective-permute-start | bytes 184328 | tf_op jit(solution)/shard_map/ppermute | solution.py:23
  37.1 5.8 %collective-permute-start.10 = (bf16[240,128]{1,0:T(8,128)(2,1)S(1)}, bf16[240,128]{1,0:T(8,128)(2,1)S(1)}, u32[]{:S(2)}, u32[]{:S(2)}) collective-permute-start(bf16[240,128]{1,0:T(8,128)(2,1)S(1)} %get-tuple-element.77), channel_id=1, source_target_pairs={{0,24},{4,28},{8,16},{12,20},{16,8},{20,12},{24,0},{28,4},{1,25},{... | collective-permute-start | bytes 184328 | tf_op jit(solution)/shard_map/ppermute | solution.py:23
  38.5 5.1 %collective-permute-start.9 = (bf16[240,128]{1,0:T(8,128)(2,1)S(1)}, bf16[240,128]{1,0:T(8,128)(2,1)S(1)}, u32[]{:S(2)}, u32[]{:S(2)}) collective-permute-start(bf16[240,128]{1,0:T(8,128)(2,1)S(1)} %get-tuple-element.78), channel_id=1, source_target_pairs={{0,16},{4,20},{8,24},{12,28},{16,0},{20,4},{24,8},{28,12},{1,17},{... | collective-permute-start | bytes 184328 | tf_op jit(solution)/shard_map/ppermute | solution.py:23
  40.2 11.7 %collective-permute-start.15 = (bf16[2,6,128,128]{3,2,1,0:T(8,128)(2,1)S(1)}, bf16[2,6,128,128]{3,2,1,0:T(8,128)(2,1)S(1)}, u32[]{:S(2)}, u32[]{:S(2)}) collective-permute-start(bf16[2,6,128,128]{3,2,1,0:T(8,128)(2,1)S(1)} %slice.95), channel_id=1, source_target_pairs={{0,16},{4,20},{8,24},{12,28},{16,0},{20,4},{24,8},{28,12},{1,17},{... | collective-permute-start | bytes 1179656 | tf_op jit(solution)/shard_map/ppermute | solution.py:23
  41.9 10.0 %collective-permute-start.14 = (bf16[2,5,128,128]{3,2,1,0:T(8,128)(2,1)S(1)}, bf16[2,5,128,128]{3,2,1,0:T(8,128)(2,1)S(1)}, u32[]{:S(2)}, u32[]{:S(2)}) collective-permute-start(bf16[2,5,128,128]{3,2,1,0:T(8,128)(2,1)S(1)} %fusion.1), channel_id=1, source_target_pairs={{0,8},{4,12},{8,0},{12,4},{16,24},{20,28},{24,16},{28,20},{1,9},{5... | collective-permute-start | bytes 983048 | tf_op jit(solution)/shard_map/ppermute | solution.py:23
  43.7 6.7 %collective-permute-start.13 = (bf16[240,128]{1,0:T(8,128)(2,1)S(1)}, bf16[240,128]{1,0:T(8,128)(2,1)S(1)}, u32[]{:S(2)}, u32[]{:S(2)}) collective-permute-start(bf16[240,128]{1,0:T(8,128)(2,1)S(1)} %fusion.7.refs_0_), channel_id=1, source_target_pairs={{0,1},{1,2},{2,3},{3,0},{4,5},{5,6},{6,7},{7,4},{8,9},{9,10},{10,1... | collective-permute-start | bytes 184328 | tf_op jit(solution)/shard_map/ppermute | solution.py:28
  45.0 6.9 %collective-permute-start.12 = (bf16[240,128]{1,0:T(8,128)(2,1)S(1)}, bf16[240,128]{1,0:T(8,128)(2,1)S(1)}, u32[]{:S(2)}, u32[]{:S(2)}) collective-permute-start(bf16[240,128]{1,0:T(8,128)(2,1)S(1)} %fusion.7.refs_0_), channel_id=1, source_target_pairs={{0,2},{1,3},{2,0},{3,1},{4,6},{5,7},{6,4},{7,5},{8,10},{9,11},{10,... | collective-permute-start | bytes 184328 | tf_op jit(solution)/shard_map/ppermute | solution.py:28
  47.1 4.8 %collective-permute-start.11 = (bf16[240,128]{1,0:T(8,128)(2,1)S(1)}, bf16[240,128]{1,0:T(8,128)(2,1)S(1)}, u32[]{:S(2)}, u32[]{:S(2)}) collective-permute-start(bf16[240,128]{1,0:T(8,128)(2,1)S(1)} %fusion.7.refs_0_), channel_id=1, source_target_pairs={{0,3},{1,0},{2,1},{3,2},{4,7},{5,4},{6,5},{7,6},{8,11},{9,8},{10,9... | collective-permute-start | bytes 184328 | tf_op jit(solution)/shard_map/ppermute | solution.py:28
  52.1 7.0 %collective-permute-start.19 = (bf16[1,240,128]{2,1,0:T(8,128)(2,1)S(1)}, bf16[1,240,128]{2,1,0:T(8,128)(2,1)S(1)}, u32[]{:S(2)}, u32[]{:S(2)}) collective-permute-start(bf16[1,240,128]{2,1,0:T(8,128)(2,1)S(1)} %bitcast.44), channel_id=1, source_target_pairs={{0,8},{4,12},{8,0},{12,4},{16,24},{20,28},{24,16},{28,20},{1,9},{5... | collective-permute-start | bytes 184328 | tf_op jit(solution)/shard_map/ppermute | solution.py:23
  53.3 12.4 %copy-start.4 = (f32[8,128,128]{2,1,0:T(8,128)S(1)}, f32[8,128,128]{2,1,0:T(8,128)}, u32[]{:S(2)}) copy-start(f32[8,128,128]{2,1,0:T(8,128)} %lower_diagonal.1) | copy-start | bytes 1572868
  53.3 12.4 %copy-start.5 = (f32[3,128,128]{2,1,0:T(8,128)S(1)}, f32[3,128,128]{2,1,0:T(8,128)}, u32[]{:S(2)}) copy-start(f32[3,128,128]{2,1,0:T(8,128)} %upper_diagonal.1) | copy-start | bytes 589828
  53.3 7.2 %collective-permute-start.17 = (bf16[5,128,128]{2,1,0:T(8,128)(2,1)S(1)}, bf16[5,128,128]{2,1,0:T(8,128)(2,1)S(1)}, u32[]{:S(2)}, u32[]{:S(2)}) collective-permute-start(bf16[5,128,128]{2,1,0:T(8,128)(2,1)S(1)} %fusion.3), channel_id=1, source_target_pairs={{0,16},{4,20},{8,24},{12,28},{16,0},{20,4},{24,8},{28,12},{1,17},{... | collective-permute-start | bytes 491528 | tf_op jit(solution)/shard_map/ppermute | solution.py:23
  54.6 9.6 %collective-permute-start.18 = (bf16[6,128,128]{2,1,0:T(8,128)(2,1)S(1)}, bf16[6,128,128]{2,1,0:T(8,128)(2,1)S(1)}, u32[]{:S(2)}, u32[]{:S(2)}) collective-permute-start(bf16[6,128,128]{2,1,0:T(8,128)(2,1)S(1)} %fusion.2), channel_id=1, source_target_pairs={{0,8},{4,12},{8,0},{12,4},{16,24},{20,28},{24,16},{28,20},{1,9},{5... | collective-permute-start | bytes 589832 | tf_op jit(solution)/shard_map/ppermute | solution.py:23
  55.1 10.0 %collective-permute-start.22 = (bf16[11,128,128]{2,1,0:T(8,128)(2,1)S(1)}, bf16[11,128,128]{2,1,0:T(8,128)(2,1)S(1)}, u32[]{:S(2)}, u32[]{:S(2)}) collective-permute-start(bf16[11,128,128]{2,1,0:T(8,128)(2,1)S(1)} %get-tuple-element.60), channel_id=1, source_target_pairs={{0,2},{3,1},{4,6},{7,5},{8,10},{11,9},{12,14},{15,13},{16,18},{19,... | collective-permute-start | bytes 1081352 | tf_op jit(solution)/shard_map/ppermute | solution.py:296
  59.1 4.9 %collective-permute-start.20 = (bf16[2,240,128]{2,1,0:T(8,128)(2,1)S(1)}, bf16[2,240,128]{2,1,0:T(8,128)(2,1)S(1)}, u32[]{:S(2)}, u32[]{:S(2)}) collective-permute-start(bf16[2,240,128]{2,1,0:T(8,128)(2,1)S(1)} %pad_maximum_fusion.1), channel_id=1, source_target_pairs={{0,16},{4,20},{8,24},{12,28},{16,0},{20,4},{24,8},{28,12},{1,17},{... | collective-permute-start | bytes 368648 | tf_op jit(solution)/shard_map/ppermute | solution.py:23
  64.1 3.7 %copy-start.7 = (s32[3,1,1]{0,2,1:T(1,128)S(1)}, s32[3,1,1]{0,2,1:T(1,128)}, u32[]{:S(2)}) copy-start(s32[3,1,1]{0,2,1:T(1,128)} %param.11) | copy-start | bytes 40
  64.1 3.7 %copy-start.8 = (s32[8,1,1]{0,2,1:T(1,128)S(1)}, s32[8,1,1]{0,2,1:T(1,128)}, u32[]{:S(2)}) copy-start(s32[8,1,1]{0,2,1:T(1,128)} %param.14) | copy-start | bytes 100
  64.1 1.6 %collective-permute-start.21 = (bf16[4,240,128]{2,1,0:T(8,128)(2,1)S(1)}, bf16[4,240,128]{2,1,0:T(8,128)(2,1)S(1)}, u32[]{:S(2)}, u32[]{:S(2)}) collective-permute-start(bf16[4,240,128]{2,1,0:T(8,128)(2,1)S(1)} %pad_maximum_fusion.near), channel_id=1, source_target_pairs={{0,4},{4,0},{8,12},{12,8},{16,20},{20,16},{24,28},{28,24},{1,5},{5... | collective-permute-start | bytes 737288 | tf_op jit(solution)/shard_map/ppermute | solution.py:23

commit v2 on v1

--- a/solution.py
+++ b/solution.py
@@ -205,12 +205,14 @@
     total_out[...] = total.astype(total_out.dtype)
 
 
-def columns_kernel(parents, upper_pattern, lower_pattern, panel, own, front, back, *refs):
-    got, (upper_out, lower_out) = refs[:-2], refs[-2:]
-    uppers, lowers, middle = upper_out.shape[0], lower_out.shape[0], front.shape[0]
+def columns_kernel(parents, upper_pattern, lower_pattern, panel, own, *refs):
+    front, back, got, (upper_out, lower_out) = refs[0:4:2], refs[1:4:2], refs[4:-2], refs[-2:]
+    uppers, lowers, middle = upper_out.shape[0], lower_out.shape[0], front[0].shape[0]
 
     def product(k):
-        value = own[k] + (front[k] if k < middle else back[k - middle])
+        value = own[k]
+        for piece in front if k < middle else back:
+            value = value + piece[k - (0 if k < middle else middle)].astype(F32)
         for piece in got:
             value = value + piece[k].astype(F32)
         return value
@@ -304,13 +306,6 @@
     return keep, flip(away, axis, 1 << bit)
 
 
-def gather_doubles(value, axis):
-    value = value[None]
-    for bit in range(1, lax.axis_size(axis).bit_length() - 1):
-        value = jnp.concatenate([value, flip(value, axis, 1 << bit)])
-    return value
-
-
 def gather_near(value, axis):
     masks = range(2, lax.axis_size(axis), 2)
     return [value] + [flip(value, axis, m) for m in masks]
@@ -442,16 +437,22 @@
     )
     sides = [keep + got.astype(F32) for (keep, _), got in zip(halves, tied[depth : depth + 2])]
     part, last, *sides = tie(part, returns[-1], *sides)
-    near = gather_doubles(part, "row")
-    far, last = tie(flip(near, "row", 1), return_pair(last, "col", reach))
-    got = [*early, last]
-    front, back = sides
+    nears = gather_near(part, "row")
+    nears[-1], *sides = tie(nears[-1], *sides)
+    near = jnp.stack(nears)
+    far = flip(near, "row", 1)
+    got = [*early, return_pair(last, "col", reach)]
     for i in range(1, len(bits)):
-        keep, across = halve(front, "row", bits[i], bits[i:])
-        front = keep + across.astype(F32)
-        keep, across = halve(back, "row", bits[-1 - i], bits[: len(bits) - i])
-        back = keep + across.astype(F32)
-    front, back = [side.reshape(-1, block, block) for side in (front, back)]
+        keeps, across = zip(
+            halve(sides[0], "row", bits[i], bits[i:]),
+            halve(sides[1], "row", bits[-1 - i], bits[: len(bits) - i]),
+        )
+        if i == len(bits) - 1:
+            got += across
+            sides = keeps
+        else:
+            sides = [keep + piece.astype(F32) for keep, piece in zip(keeps, across)]
+    front, back = [side.reshape(-1, block, block) for side in sides]
 
     upper_blocks, lower_cross, lower_blocks = call(
         functools.partial(blocks_kernel, width),
@@ -465,11 +466,13 @@
         ],
         [shape_of((width * chunk, block), F32), shape_of((uppers, 2 * block, block), bf16)],
     )
+    upper_blocks, *got = tie(upper_blocks, *got)
+    across = [piece.reshape(-1, block, block) for piece in got[reach:]]
     upper_columns, lower_columns = call(
         columns_kernel,
         "columns",
         (parents, upper_pattern, lower_pattern),
-        (parent_panel, own, front, back, *got),
+        (parent_panel, own, front, back, *across, *got[:reach]),
         [
             shape_of((uppers, block, block), bf16),
             shape_of((lowers, block, block), bf16),

time: 69.6 us -> 69.6 us (level)
  waiting for transfers between devices: 23.8 us -> 22.3 us
  starting transfers between devices: 31.9 us -> 33.3 us
    ppermute x16 -> x17, starting transfers between devices: 14.8 us -> 16.2 us  [flip(): return lax.ppermute(value, axis, [(i, i ^ mask) for i in range(size)])]
    ppermute x2, waiting for transfers between devices: 0.78 us -> 0.01 us  [return_pair(): return lax.ppermute(value, axis, pairs(lax.axis_size(axis), offset))]
    ppermute x16 -> x17, waiting for transfers between devices: 8.42 us -> 7.71 us  [flip(): return lax.ppermute(value, axis, [(i, i ^ mask) for i in range(size)])]
  transfers between devices with their start and end apart: 23 -> 24, of which waited for: 13 -> 12; matrix products, arithmetic and copies ran while one was open for 1% -> 1% of each run, Pallas kernels for 7% -> 10%
where the time goes in v2:
time: 69.6 us; the launch traced here: 69.3 us
  starting transfers between devices  33.3 us (48%)
  waiting for transfers between devices  22.3 us (32%)
  Pallas kernels  10.7 us (15%)
  local copies, waits for them, and re-layouts  1.37 us (2%)
  between operations  0.96 us (1%)
  other arithmetic  0.78 us (1%)
    ppermute x17, starting transfers between devices, flip(): return lax.ppermute(value, axis, [(i, i ^ mask) for i in range(size)])  16.2 us
    ppermute x2, waiting for transfers between devices, gather_pair(): lax.ppermute(value, axis, [(b, c) for c, b in pairs(lax.axis_size(axis),...  11.8 us
    pallas_call x10, Pallas kernels, call(): pl.pallas_call(kernel, out_shape=outs, in_specs=[SMEM] * len(scalars) + [...  10.7 us
    ppermute x17, waiting for transfers between devices, flip(): return lax.ppermute(value, axis, [(i, i ^ mask) for i in range(size)])  7.71 us
    ppermute x2, starting transfers between devices, gather_pair(): lax.ppermute(value, axis, [(b, c) for c, b in pairs(lax.axis_size(axis),...  6.38 us
    ppermute x3, starting transfers between devices, shift(): lax.ppermute(value, axis, [(i, (i + step) % size) for i in range(size)])  5.36 us
    ppermute x2, starting transfers between devices, return_pair(): return lax.ppermute(value, axis, pairs(lax.axis_size(axis), offset))  5.28 us
    ppermute x3, waiting for transfers between devices, shift(): lax.ppermute(value, axis, [(i, (i + step) % size) for i in range(size)])  2.83 us
  transfers between devices with their start and end apart: 24, of which 12 were waited for; matrix products, arithmetic and copies ran while one was open for 1% of the time, Pallas kernels for 10%

profile of v2, /device:TPU:0, one launch (start us, length us, event | category | flops | bytes accessed | tf_op | source)
XLA Modules:
  0.0 69.3 jit_solution(4511871180150324674)
XLA Ops:
  0.6 1.8 %mask.1.refs_0_ = bf16[11,128,128]{2,1,0:T(8,128)(2,1)} custom-call(s32[3]{0:T(128)} %bitcast.48, s32[8]{0:T(128)} %bitcast.50, bf16[3,128,128]{2,1,0:T(8,128)(2,1)} %bitcast.55, bf16[8,128,128]{2,1,0:T(8,128)(2,1)} %bitcast.54), custom_call_target="tpu_custom_call" | custom-call | tf_op jit(solution)/shard_map/mask/pallas_call | solution.py:41
  2.4 1.3 %collective-permute-start.4 = (bf16[11,128,128]{2,1,0:T(8,128)(2,1)}, bf16[11,128,128]{2,1,0:T(8,128)(2,1)S(1)}, u32[]{:S(2)}, u32[]{:S(2)}) collective-permute-start(bf16[11,128,128]{2,1,0:T(8,128)(2,1)} %mask.1.refs_0_), channel_id=1, source_target_pairs={{2,0},{1,3},{6,4},{5,7},{10,8},{9,11},{14,12},{13,15},{18,16},{17,... | collective-permute-start | bytes 1081352 | tf_op jit(solution)/shard_map/ppermute | solution.py:294
  3.7 5.1 %collective-permute-start.3 = (bf16[11,128,128]{2,1,0:T(8,128)(2,1)}, bf16[11,128,128]{2,1,0:T(8,128)(2,1)S(1)}, u32[]{:S(2)}, u32[]{:S(2)}) collective-permute-start(bf16[11,128,128]{2,1,0:T(8,128)(2,1)} %mask.1.refs_0_), channel_id=1, source_target_pairs={{1,0},{2,1},{3,2},{0,3},{5,4},{6,5},{7,6},{4,7},{9,8},{10,9},{11,1... | collective-permute-start | bytes 1081352 | tf_op jit(solution)/shard_map/ppermute | solution.py:294
  8.8 2.4 %collective-permute-start.2 = (bf16[11,128,128]{2,1,0:T(8,128)(2,1)}, bf16[11,128,128]{2,1,0:T(8,128)(2,1)S(1)}, u32[]{:S(2)}, u32[]{:S(2)}) collective-permute-start(bf16[11,128,128]{2,1,0:T(8,128)(2,1)} %mask.1.refs_0_), channel_id=1, source_target_pairs={{0,24},{4,28},{8,16},{12,20},{16,8},{20,12},{24,0},{28,4},{1,25},{... | collective-permute-start | bytes 1081352 | tf_op jit(solution)/shard_map/ppermute | solution.py:23
  11.3 0.5 collective-permute-start.1
  11.8 0.5 collective-permute-start
  12.3 4.9 %collective-permute-done.4.refs_2_.refs_1_ = bf16[11,128,128]{2,1,0:T(8,128)(2,1)S(1)} collective-permute-done((bf16[11,128,128]{2,1,0:T(8,128)(2,1)}, bf16[11,128,128]{2,1,0:T(8,128)(2,1)S(1)}, u32[]{:S(2)}, u32[]{:S(2)}) %collective-permute-start.4) | collective-permute-done | bytes 360480 | tf_op jit(solution)/shard_map/ppermute | solution.py:294
  17.2 6.9 %collective-permute-done.3.refs_1_.refs_0_ = bf16[11,128,128]{2,1,0:T(8,128)(2,1)S(1)} collective-permute-done((bf16[11,128,128]{2,1,0:T(8,128)(2,1)}, bf16[11,128,128]{2,1,0:T(8,128)(2,1)S(1)}, u32[]{:S(2)}, u32[]{:S(2)}) %collective-permute-start.3) | collective-permute-done | bytes 360480 | tf_op jit(solution)/shard_map/ppermute | solution.py:294
  24.1 1.0 %copy-done = bf16[11,128,128]{2,1,0:T(8,128)(2,1)S(1)} copy-done((bf16[11,128,128]{2,1,0:T(8,128)(2,1)S(1)}, bf16[11,128,128]{2,1,0:T(8,128)(2,1)}, u32[]{:S(2)}) %copy-start) | copy-done | bytes 360472
  25.1 0.3 turn.1.refs_4_.turned
  25.4 0.0 copy-start.2
  25.4 0.0 copy-start.3
  25.4 2.1 %collective-permute-done.1.refs_2_ = bf16[11,128,128]{2,1,0:T(8,128)(2,1)S(1)} collective-permute-done((bf16[11,128,128]{2,1,0:T(8,128)(2,1)}, bf16[11,128,128]{2,1,0:T(8,128)(2,1)S(1)}, u32[]{:S(2)}, u32[]{:S(2)}) %collective-permute-start.1) | collective-permute-done | bytes 360480 | tf_op jit(solution)/shard_map/ppermute | solution.py:23
  27.5 0.1 collective-permute-done.refs_1_
  27.6 0.1 stack.21.near
  27.7 0.1 collective-permute-start.5
  27.8 0.4 top.1
  28.2 1.0 %partial.1 = (f32[4,11,128,128]{3,2,1,0:T(8,128)S(1)}, bf16[4,11,128,128]{3,2,1,0:T(8,128)(2,1)S(1)}) custom-call(bf16[1024,256]{1,0:T(8,128)(2,1)S(1)} %get-tuple-element.47.top, bf16[11,128,128]{2,1,0:T(8,128)(2,1)S(1)} %collective-permute-done.3.refs_1_.refs_0_, bf16[11,128,128]{2,1,0:T(8,128)(2,1)S(1)} %collective-permute-done.4.refs_2_.refs_1_), custom_call_target="tpu_custom_call" | custom-call | tf_op jit(solution)/shard_map/partial/pallas_call | solution.py:41
  29.2 0.5 collective-permute-start.7
  29.7 0.8 %first.1.start = f32[6,384,256]{2,1,0:T(8,128)S(1)} custom-call(bf16[2,384,512]{2,1,0:T(8,128)(2,1)S(1)} %get-tuple-element.43.top, bf16[4,11,128,128]{3,2,1,0:T(8,128)(2,1)S(1)} %stack.21.near), custom_call_target="tpu_custom_call" | custom-call | tf_op jit(solution)/shard_map/first/pallas_call | solution.py:41
  30.5 0.5 collective-permute-done.5.far
  31.0 2.5 %second.1 = (f32[11,128,128]{2,1,0:T(8,128)S(1)}, bf16[11,128,128]{2,1,0:T(8,128)(2,1)S(1)}, bf16[11,128,128]{2,1,0:T(8,128)(2,1)S(1)}, f32[4,240,128]{2,1,0:T(8,128)S(1)}, f32[4,240,128]{2,1,0:T(8,128)S(1)}) custom-call(s32[8]{0:T(128)S(1)} %copy-done.6, bf16[2,384,512]{2,1,0:T(8,128)(2,1)S(1)} %get-tuple-element.43.top, ...), custom_call_target="tpu_custom_call" | custom-call | tf_op jit(solution)/shard_map/second/pallas_call | solution.py:41
  33.5 0.2 collective-permute-start.6
  33.7 1.3 %collective-permute-start.16 = (bf16[11,128,128]{2,1,0:T(8,128)(2,1)S(1)}, bf16[11,128,128]{2,1,0:T(8,128)(2,1)S(1)}, u32[]{:S(2)}, u32[]{:S(2)}) collective-permute-start(bf16[11,128,128]{2,1,0:T(8,128)(2,1)S(1)} %get-tuple-element.54), channel_id=1, source_target_pairs={{0,1},{1,2},{2,3},{3,0},{4,5},{5,6},{6,7},{7,4},{8,9},{9,10},{10,1... | collective-permute-start | bytes 1081352 | tf_op jit(solution)/shard_map/ppermute | solution.py:298
  35.0 0.0 collective-permute-done.7
  35.0 0.4 collective-permute-done.6
  35.5 0.1 fusion.8
  35.6 1.6 %collective-permute-start.8 = (bf16[240,128]{1,0:T(8,128)(2,1)S(1)}, bf16[240,128]{1,0:T(8,128)(2,1)S(1)}, u32[]{:S(2)}, u32[]{:S(2)}) collective-permute-start(bf16[240,128]{1,0:T(8,128)(2,1)S(1)} %get-tuple-element.88), channel_id=1, source_target_pairs={{0,8},{4,12},{8,0},{12,4},{16,24},{20,28},{24,16},{28,20},{1,9},{5... | collective-permute-start | bytes 184328 | tf_op jit(solution)/shard_map/ppermute | solution.py:23
  37.1 1.4 %collective-permute-start.10 = (bf16[240,128]{1,0:T(8,128)(2,1)S(1)}, bf16[240,128]{1,0:T(8,128)(2,1)S(1)}, u32[]{:S(2)}, u32[]{:S(2)}) collective-permute-start(bf16[240,128]{1,0:T(8,128)(2,1)S(1)} %get-tuple-element.89), channel_id=1, source_target_pairs={{0,24},{4,28},{8,16},{12,20},{16,8},{20,12},{24,0},{28,4},{1,25},{... | collective-permute-start | bytes 184328 | tf_op jit(solution)/shard_map/ppermute | solution.py:23
  38.5 0.6 collective-permute-start.9
  39.1 0.5 convert_add_fusion
  39.6 0.4 collective-permute-done.8
  40.0 0.1 slice.95
  40.1 0.1 slice.55
  40.2 1.6 %collective-permute-start.15 = (bf16[2,6,128,128]{3,2,1,0:T(8,128)(2,1)S(1)}, bf16[2,6,128,128]{3,2,1,0:T(8,128)(2,1)S(1)}, u32[]{:S(2)}, u32[]{:S(2)}) collective-permute-start(bf16[2,6,128,128]{3,2,1,0:T(8,128)(2,1)S(1)} %slice.95), channel_id=1, source_target_pairs={{0,16},{4,20},{8,24},{12,28},{16,0},{20,4},{24,8},{28,12},{1,17},{... | collective-permute-start | bytes 1179656 | tf_op jit(solution)/shard_map/ppermute | solution.py:23
  41.8 0.1 fusion.1
  41.9 1.0 %collective-permute-start.14 = (bf16[2,5,128,128]{3,2,1,0:T(8,128)(2,1)S(1)}, bf16[2,5,128,128]{3,2,1,0:T(8,128)(2,1)S(1)}, u32[]{:S(2)}, u32[]{:S(2)}) collective-permute-start(bf16[2,5,128,128]{3,2,1,0:T(8,128)(2,1)S(1)} %fusion.1), channel_id=1, source_target_pairs={{0,8},{4,12},{8,0},{12,4},{16,24},{20,28},{24,16},{28,20},{1,9},{5... | collective-permute-start | bytes 983048 | tf_op jit(solution)/shard_map/ppermute | solution.py:23
  42.9 0.0 collective-permute-done.10
  42.9 0.7 %collective-permute-done.9 = bf16[240,128]{1,0:T(8,128)(2,1)S(1)} collective-permute-done((bf16[240,128]{1,0:T(8,128)(2,1)S(1)}, bf16[240,128]{1,0:T(8,128)(2,1)S(1)}, u32[]{:S(2)}, u32[]{:S(2)}) %collective-permute-start.9) | collective-permute-done | bytes 61472 | tf_op jit(solution)/shard_map/ppermute | solution.py:23
  43.7 1.3 %collective-permute-start.13 = (bf16[240,128]{1,0:T(8,128)(2,1)S(1)}, bf16[240,128]{1,0:T(8,128)(2,1)S(1)}, u32[]{:S(2)}, u32[]{:S(2)}) collective-permute-start(bf16[240,128]{1,0:T(8,128)(2,1)S(1)} %fusion.7.refs_0_), channel_id=1, source_target_pairs={{0,1},{1,2},{2,3},{3,0},{4,5},{5,6},{6,7},{7,4},{8,9},{9,10},{10,1... | collective-permute-start | bytes 184328 | tf_op jit(solution)/shard_map/ppermute | solution.py:28
  45.0 2.0 %collective-permute-start.12 = (bf16[240,128]{1,0:T(8,128)(2,1)S(1)}, bf16[240,128]{1,0:T(8,128)(2,1)S(1)}, u32[]{:S(2)}, u32[]{:S(2)}) collective-permute-start(bf16[240,128]{1,0:T(8,128)(2,1)S(1)} %fusion.7.refs_0_), channel_id=1, source_target_pairs={{0,2},{1,3},{2,0},{3,1},{4,6},{5,7},{6,4},{7,5},{8,10},{9,11},{10,... | collective-permute-start | bytes 184328 | tf_op jit(solution)/shard_map/ppermute | solution.py:28
  47.1 0.0 collective-permute-done.16.refs_4_
  47.1 2.0 %collective-permute-start.11 = (bf16[240,128]{1,0:T(8,128)(2,1)S(1)}, bf16[240,128]{1,0:T(8,128)(2,1)S(1)}, u32[]{:S(2)}, u32[]{:S(2)}) collective-permute-start(bf16[240,128]{1,0:T(8,128)(2,1)S(1)} %fusion.7.refs_0_), channel_id=1, source_target_pairs={{0,3},{1,0},{2,1},{3,2},{4,7},{5,4},{6,5},{7,6},{8,11},{9,8},{10,9... | collective-permute-start | bytes 184328 | tf_op jit(solution)/shard_map/ppermute | solution.py:28
  49.0 1.3 %collective-permute-done.13.refs_3_ = bf16[240,128]{1,0:T(8,128)(2,1)S(1)} collective-permute-done((bf16[240,128]{1,0:T(8,128)(2,1)S(1)}, bf16[240,128]{1,0:T(8,128)(2,1)S(1)}, u32[]{:S(2)}, u32[]{:S(2)}) %collective-permute-start.13) | collective-permute-done | bytes 61472 | tf_op jit(solution)/shard_map/ppermute | solution.py:28
  50.4 1.5 %collective-permute-done.12.refs_2_ = bf16[240,128]{1,0:T(8,128)(2,1)S(1)} collective-permute-done((bf16[240,128]{1,0:T(8,128)(2,1)S(1)}, bf16[240,128]{1,0:T(8,128)(2,1)S(1)}, u32[]{:S(2)}, u32[]{:S(2)}) %collective-permute-start.12) | collective-permute-done | bytes 61472 | tf_op jit(solution)/shard_map/ppermute | solution.py:28
  51.9 0.1 convert_add_fusion.1
  52.0 0.1 fusion
  52.0 0.0 copy-start.4
  52.1 0.0 copy-start.5
  52.1 0.1 line.1
  52.1 1.7 %collective-permute-start.17 = (bf16[240,128]{1,0:T(8,128)(2,1)S(1)}, bf16[240,128]{1,0:T(8,128)(2,1)S(1)}, u32[]{:S(2)}, u32[]{:S(2)}) collective-permute-start(bf16[240,128]{1,0:T(8,128)(2,1)S(1)} %line.1), channel_id=1, source_target_pairs={{0,24},{4,28},{8,16},{12,20},{16,8},{20,12},{24,0},{28,4},{1,25},{... | collective-permute-start | bytes 184328 | tf_op jit(solution)/shard_map/ppermute | solution.py:23
  53.9 0.9 %collective-permute-start.19 = (bf16[240,128]{1,0:T(8,128)(2,1)S(1)}, bf16[240,128]{1,0:T(8,128)(2,1)S(1)}, u32[]{:S(2)}, u32[]{:S(2)}) collective-permute-start(bf16[240,128]{1,0:T(8,128)(2,1)S(1)} %line.1), channel_id=1, source_target_pairs={{0,16},{4,20},{8,24},{12,28},{16,0},{20,4},{24,8},{28,12},{1,17},{... | collective-permute-start | bytes 184328 | tf_op jit(solution)/shard_map/ppermute | solution.py:23
  54.8 0.9 %collective-permute-start.18 = (bf16[240,128]{1,0:T(8,128)(2,1)S(1)}, bf16[240,128]{1,0:T(8,128)(2,1)S(1)}, u32[]{:S(2)}, u32[]{:S(2)}) collective-permute-start(bf16[240,128]{1,0:T(8,128)(2,1)S(1)} %line.1), channel_id=1, source_target_pairs={{0,8},{4,12},{8,0},{12,4},{16,24},{20,28},{24,16},{28,20},{1,9},{5... | collective-permute-start | bytes 184328 | tf_op jit(solution)/shard_map/ppermute | solution.py:23
  55.7 4.0 %collective-permute-start.21 = (bf16[11,128,128]{2,1,0:T(8,128)(2,1)S(1)}, bf16[11,128,128]{2,1,0:T(8,128)(2,1)S(1)}, u32[]{:S(2)}, u32[]{:S(2)}) collective-permute-start(bf16[11,128,128]{2,1,0:T(8,128)(2,1)S(1)} %get-tuple-element.71), channel_id=1, source_target_pairs={{0,2},{3,1},{4,6},{7,5},{8,10},{11,9},{12,14},{15,13},{16,18},{19,... | collective-permute-start | bytes 1081352 | tf_op jit(solution)/shard_map/ppermute | solution.py:298
  59.7 0.0 collective-permute-done.17
  59.8 0.0 copy-start.7
  59.9 0.0 copy-start.8
  59.9 0.1 collective-permute-start.20
  60.0 0.7 %collective-permute-start.22 = (bf16[5,128,128]{2,1,0:T(8,128)(2,1)S(1)}, bf16[5,128,128]{2,1,0:T(8,128)(2,1)S(1)}, u32[]{:S(2)}, u32[]{:S(2)}) collective-permute-start(bf16[5,128,128]{2,1,0:T(8,128)(2,1)S(1)} %fusion.3), channel_id=1, source_target_pairs={{0,16},{4,20},{8,24},{12,28},{16,0},{20,4},{24,8},{28,12},{1,17},{... | collective-permute-start | bytes 491528 | tf_op jit(solution)/shard_map/ppermute | solution.py:23
  60.7 1.4 %collective-permute-start.23 = (bf16[6,128,128]{2,1,0:T(8,128)(2,1)S(1)}, bf16[6,128,128]{2,1,0:T(8,128)(2,1)S(1)}, u32[]{:S(2)}, u32[]{:S(2)}) collective-permute-start(bf16[6,128,128]{2,1,0:T(8,128)(2,1)S(1)} %fusion.2), channel_id=1, source_target_pairs={{0,8},{4,12},{8,0},{12,4},{16,24},{20,28},{24,16},{28,20},{1,9},{5... | collective-permute-start | bytes 589832 | tf_op jit(solution)/shard_map/ppermute | solution.py:23
  62.2 2.1 %blocks.1 = (f32[3,128,128]{2,1,0:T(8,128)}, f32[8,128,128]{2,1,0:T(8,128)}, f32[8,128,128]{2,1,0:T(8,128)}) custom-call(s32[8]{0:T(128)S(1)} %copy-done.6, bf16[4,240,128]{2,1,0:T(8,128)(2,1)S(1)} %pad_maximum_fusion.near, bf16[4,240,128]{2,1,0:T(8,128)(2,1)S(1)} %collective-permute-done.20.far, f32[3,128,128]{2,1,0:T(8,128)S(1)} %copy-done.5, ...), custom_call_target="tpu_custom_call" | custom-call | tf_op jit(solution)/shard_map/blocks/pallas_call | solution.py:41
  64.3 2.3 %collective-permute-done.22.refs_2_ = bf16[5,128,128]{2,1,0:T(8,128)(2,1)S(1)} collective-permute-done((bf16[5,128,128]{2,1,0:T(8,128)(2,1)S(1)}, bf16[5,128,128]{2,1,0:T(8,128)(2,1)S(1)}, u32[]{:S(2)}, u32[]{:S(2)}) %collective-permute-start.22) | collective-permute-done | bytes 163872 | tf_op jit(solution)/shard_map/ppermute | solution.py:23
  66.6 1.1 %collective-permute-done.23.refs_3_ = bf16[6,128,128]{2,1,0:T(8,128)(2,1)S(1)} collective-permute-done((bf16[6,128,128]{2,1,0:T(8,128)(2,1)S(1)}, bf16[6,128,128]{2,1,0:T(8,128)(2,1)S(1)}, u32[]{:S(2)}, u32[]{:S(2)}) %collective-permute-start.23) | collective-permute-done | bytes 196640 | tf_op jit(solution)/shard_map/ppermute | solution.py:23
  67.7 1.6 %columns.1 = (bf16[3,128,128]{2,1,0:T(8,128)(2,1)}, bf16[8,128,128]{2,1,0:T(8,128)(2,1)}) custom-call(s32[8]{0:T(128)S(1)} %copy-done.6, s32[3]{0:T(128)S(1)} %bitcast.49, s32[8]{0:T(128)S(1)} %bitcast.51, bf16[8,128,128]{2,1,0:T(8,128)(2,1)S(1)} %copy-done.2, f32[11,128,128]{2,1,0:T(8,128)S(1)} %get-tuple-element.44.own, ...), custom_call_target="tpu_custom_call" | custom-call | tf_op jit(solution)/shard_map/columns/pallas_call | solution.py:41
  (26 shorter events, 0.2 us)
Async XLA Ops:
  2.4 14.8 %collective-permute-start.4 = (bf16[11,128,128]{2,1,0:T(8,128)(2,1)}, bf16[11,128,128]{2,1,0:T(8,128)(2,1)S(1)}, u32[]{:S(2)}, u32[]{:S(2)}) collective-permute-start(bf16[11,128,128]{2,1,0:T(8,128)(2,1)} %mask.1.refs_0_), channel_id=1, source_target_pairs={{2,0},{1,3},{6,4},{5,7},{10,8},{9,11},{14,12},{13,15},{18,16},{17,... | collective-permute-start | bytes 1081352 | tf_op jit(solution)/shard_map/ppermute | solution.py:294
  3.7 20.4 %collective-permute-start.3 = (bf16[11,128,128]{2,1,0:T(8,128)(2,1)}, bf16[11,128,128]{2,1,0:T(8,128)(2,1)S(1)}, u32[]{:S(2)}, u32[]{:S(2)}) collective-permute-start(bf16[11,128,128]{2,1,0:T(8,128)(2,1)} %mask.1.refs_0_), channel_id=1, source_target_pairs={{1,0},{2,1},{3,2},{0,3},{5,4},{6,5},{7,6},{4,7},{9,8},{10,9},{11,1... | collective-permute-start | bytes 1081352 | tf_op jit(solution)/shard_map/ppermute | solution.py:294
  8.8 16.6 %collective-permute-start.2 = (bf16[11,128,128]{2,1,0:T(8,128)(2,1)}, bf16[11,128,128]{2,1,0:T(8,128)(2,1)S(1)}, u32[]{:S(2)}, u32[]{:S(2)}) collective-permute-start(bf16[11,128,128]{2,1,0:T(8,128)(2,1)} %mask.1.refs_0_), channel_id=1, source_target_pairs={{0,24},{4,28},{8,16},{12,20},{16,8},{20,12},{24,0},{28,4},{1,25},{... | collective-permute-start | bytes 1081352 | tf_op jit(solution)/shard_map/ppermute | solution.py:23
  11.3 16.3 %collective-permute-start.1 = (bf16[11,128,128]{2,1,0:T(8,128)(2,1)}, bf16[11,128,128]{2,1,0:T(8,128)(2,1)S(1)}, u32[]{:S(2)}, u32[]{:S(2)}) collective-permute-start(bf16[11,128,128]{2,1,0:T(8,128)(2,1)} %mask.1.refs_0_), channel_id=1, source_target_pairs={{0,16},{4,20},{8,24},{12,28},{16,0},{20,4},{24,8},{28,12},{1,17},{... | collective-permute-start | bytes 1081352 | tf_op jit(solution)/shard_map/ppermute | solution.py:23
  11.8 15.9 %collective-permute-start = (bf16[11,128,128]{2,1,0:T(8,128)(2,1)}, bf16[11,128,128]{2,1,0:T(8,128)(2,1)S(1)}, u32[]{:S(2)}, u32[]{:S(2)}) collective-permute-start(bf16[11,128,128]{2,1,0:T(8,128)(2,1)} %mask.1.refs_0_), channel_id=1, source_target_pairs={{0,8},{4,12},{8,0},{12,4},{16,24},{20,28},{24,16},{28,20},{1,9},{5... | collective-permute-start | bytes 1081352 | tf_op jit(solution)/shard_map/ppermute | solution.py:23
  24.1 1.0 %copy-start = (bf16[11,128,128]{2,1,0:T(8,128)(2,1)S(1)}, bf16[11,128,128]{2,1,0:T(8,128)(2,1)}, u32[]{:S(2)}) copy-start(bf16[11,128,128]{2,1,0:T(8,128)(2,1)} %mask.1.refs_0_) | copy-start | bytes 1081348
  25.1 2.6 %copy-start.1 = (bf16[11,128,128]{2,1,0:T(8,128)(2,1)S(1)}, bf16[11,128,128]{2,1,0:T(8,128)(2,1)}, u32[]{:S(2)}) copy-start(bf16[11,128,128]{2,1,0:T(8,128)(2,1)} %mask.1.refs_0_) | copy-start | bytes 1081348
  25.4 2.4 %copy-start.2 = (bf16[8,128,128]{2,1,0:T(8,128)(2,1)S(1)}, bf16[8,128,128]{2,1,0:T(8,128)(2,1)}, u32[]{:S(2)}) copy-start(bf16[8,128,128]{2,1,0:T(8,128)(2,1)} %panel.5) | copy-start | bytes 786436
  25.4 2.4 %copy-start.3 = (bf16[1,4,8,1,128,128]{5,4,3,2,1,0:T(8,128)(2,1)S(1)}, bf16[1,4,8,1,128,128]{5,4,3,2,1,0:T(8,128)(2,1)}, u32[]{:S(2)}) copy-start(bf16[1,4,8,1,128,128]{5,4,3,2,1,0:T(8,128)(2,1)} %param.9) | copy-start | bytes 3145732
  27.7 3.3 %collective-permute-start.5 = (bf16[4,11,128,128]{3,2,1,0:T(8,128)(2,1)S(1)}, bf16[4,11,128,128]{3,2,1,0:T(8,128)(2,1)S(1)}, u32[]{:S(2)}, u32[]{:S(2)}) collective-permute-start(bf16[4,11,128,128]{3,2,1,0:T(8,128)(2,1)S(1)} %stack.21.near), channel_id=1, source_target_pairs={{0,4},{4,0},{8,12},{12,8},{16,20},{20,16},{24,28},{28,24},{1,5},{5... | collective-permute-start | bytes 4325384 | tf_op jit(solution)/shard_map/ppermute | solution.py:23
  29.2 5.8 %collective-permute-start.7 = (bf16[4,11,128,128]{3,2,1,0:T(8,128)(2,1)S(1)}, bf16[4,11,128,128]{3,2,1,0:T(8,128)(2,1)S(1)}, u32[]{:S(2)}, u32[]{:S(2)}) collective-permute-start(bf16[4,11,128,128]{3,2,1,0:T(8,128)(2,1)S(1)} %get-tuple-element.48), channel_id=1, source_target_pairs={{0,4},{4,0},{8,12},{12,8},{16,20},{20,16},{24,28},{28,24},{1,5},{5... | collective-permute-start | bytes 4325384 | tf_op jit(solution)/shard_map/ppermute | solution.py:23
  29.7 1.3 %copy-start.6 = (s32[8]{0:T(128)S(1)}, s32[8]{0:T(128)}, u32[]{:S(2)}) copy-start(s32[8]{0:T(128)} %parents.5) | copy-start | bytes 100
  33.5 1.9 %collective-permute-start.6 = (f32[4,240,128]{2,1,0:T(8,128)S(1)}, f32[4,240,128]{2,1,0:T(8,128)S(1)}, u32[]{:S(2)}, u32[]{:S(2)}) collective-permute-start(f32[4,240,128]{2,1,0:T(8,128)S(1)} %get-tuple-element.46), channel_id=1, source_target_pairs={{0,4},{4,0},{8,12},{12,8},{16,20},{20,16},{24,28},{28,24},{1,5},{5... | collective-permute-start | bytes 1474568 | tf_op jit(solution)/shard_map/ppermute | solution.py:23
  33.7 13.3 %collective-permute-start.16 = (bf16[11,128,128]{2,1,0:T(8,128)(2,1)S(1)}, bf16[11,128,128]{2,1,0:T(8,128)(2,1)S(1)}, u32[]{:S(2)}, u32[]{:S(2)}) collective-permute-start(bf16[11,128,128]{2,1,0:T(8,128)(2,1)S(1)} %get-tuple-element.54), channel_id=1, source_target_pairs={{0,1},{1,2},{2,3},{3,0},{4,5},{5,6},{6,7},{7,4},{8,9},{9,10},{10,1... | collective-permute-start | bytes 1081352 | tf_op jit(solution)/shard_map/ppermute | solution.py:298
  35.6 4.5 %collective-permute-start.8 = (bf16[240,128]{1,0:T(8,128)(2,1)S(1)}, bf16[240,128]{1,0:T(8,128)(2,1)S(1)}, u32[]{:S(2)}, u32[]{:S(2)}) collective-permute-start(bf16[240,128]{1,0:T(8,128)(2,1)S(1)} %get-tuple-element.88), channel_id=1, source_target_pairs={{0,8},{4,12},{8,0},{12,4},{16,24},{20,28},{24,16},{28,20},{1,9},{5... | collective-permute-start | bytes 184328 | tf_op jit(solution)/shard_map/ppermute | solution.py:23
  37.1 5.8 %collective-permute-start.10 = (bf16[240,128]{1,0:T(8,128)(2,1)S(1)}, bf16[240,128]{1,0:T(8,128)(2,1)S(1)}, u32[]{:S(2)}, u32[]{:S(2)}) collective-permute-start(bf16[240,128]{1,0:T(8,128)(2,1)S(1)} %get-tuple-element.89), channel_id=1, source_target_pairs={{0,24},{4,28},{8,16},{12,20},{16,8},{20,12},{24,0},{28,4},{1,25},{... | collective-permute-start | bytes 184328 | tf_op jit(solution)/shard_map/ppermute | solution.py:23
  38.5 5.1 %collective-permute-start.9 = (bf16[240,128]{1,0:T(8,128)(2,1)S(1)}, bf16[240,128]{1,0:T(8,128)(2,1)S(1)}, u32[]{:S(2)}, u32[]{:S(2)}) collective-permute-start(bf16[240,128]{1,0:T(8,128)(2,1)S(1)} %get-tuple-element.90), channel_id=1, source_target_pairs={{0,16},{4,20},{8,24},{12,28},{16,0},{20,4},{24,8},{28,12},{1,17},{... | collective-permute-start | bytes 184328 | tf_op jit(solution)/shard_map/ppermute | solution.py:23
  40.2 11.7 %collective-permute-start.15 = (bf16[2,6,128,128]{3,2,1,0:T(8,128)(2,1)S(1)}, bf16[2,6,128,128]{3,2,1,0:T(8,128)(2,1)S(1)}, u32[]{:S(2)}, u32[]{:S(2)}) collective-permute-start(bf16[2,6,128,128]{3,2,1,0:T(8,128)(2,1)S(1)} %slice.95), channel_id=1, source_target_pairs={{0,16},{4,20},{8,24},{12,28},{16,0},{20,4},{24,8},{28,12},{1,17},{... | collective-permute-start | bytes 1179656 | tf_op jit(solution)/shard_map/ppermute | solution.py:23
  41.9 10.0 %collective-permute-start.14 = (bf16[2,5,128,128]{3,2,1,0:T(8,128)(2,1)S(1)}, bf16[2,5,128,128]{3,2,1,0:T(8,128)(2,1)S(1)}, u32[]{:S(2)}, u32[]{:S(2)}) collective-permute-start(bf16[2,5,128,128]{3,2,1,0:T(8,128)(2,1)S(1)} %fusion.1), channel_id=1, source_target_pairs={{0,8},{4,12},{8,0},{12,4},{16,24},{20,28},{24,16},{28,20},{1,9},{5... | collective-permute-start | bytes 983048 | tf_op jit(solution)/shard_map/ppermute | solution.py:23
  43.7 6.7 %collective-permute-start.13 = (bf16[240,128]{1,0:T(8,128)(2,1)S(1)}, bf16[240,128]{1,0:T(8,128)(2,1)S(1)}, u32[]{:S(2)}, u32[]{:S(2)}) collective-permute-start(bf16[240,128]{1,0:T(8,128)(2,1)S(1)} %fusion.7.refs_0_), channel_id=1, source_target_pairs={{0,1},{1,2},{2,3},{3,0},{4,5},{5,6},{6,7},{7,4},{8,9},{9,10},{10,1... | collective-permute-start | bytes 184328 | tf_op jit(solution)/shard_map/ppermute | solution.py:28
  45.0 6.9 %collective-permute-start.12 = (bf16[240,128]{1,0:T(8,128)(2,1)S(1)}, bf16[240,128]{1,0:T(8,128)(2,1)S(1)}, u32[]{:S(2)}, u32[]{:S(2)}) collective-permute-start(bf16[240,128]{1,0:T(8,128)(2,1)S(1)} %fusion.7.refs_0_), channel_id=1, source_target_pairs={{0,2},{1,3},{2,0},{3,1},{4,6},{5,7},{6,4},{7,5},{8,10},{9,11},{10,... | collective-permute-start | bytes 184328 | tf_op jit(solution)/shard_map/ppermute | solution.py:28
  47.1 4.8 %collective-permute-start.11 = (bf16[240,128]{1,0:T(8,128)(2,1)S(1)}, bf16[240,128]{1,0:T(8,128)(2,1)S(1)}, u32[]{:S(2)}, u32[]{:S(2)}) collective-permute-start(bf16[240,128]{1,0:T(8,128)(2,1)S(1)} %fusion.7.refs_0_), channel_id=1, source_target_pairs={{0,3},{1,0},{2,1},{3,2},{4,7},{5,4},{6,5},{7,6},{8,11},{9,8},{10,9... | collective-permute-start | bytes 184328 | tf_op jit(solution)/shard_map/ppermute | solution.py:28
  52.0 10.1 %copy-start.4 = (f32[8,128,128]{2,1,0:T(8,128)S(1)}, f32[8,128,128]{2,1,0:T(8,128)}, u32[]{:S(2)}) copy-start(f32[8,128,128]{2,1,0:T(8,128)} %lower_diagonal.1) | copy-start | bytes 1572868
  52.1 10.1 %copy-start.5 = (f32[3,128,128]{2,1,0:T(8,128)S(1)}, f32[3,128,128]{2,1,0:T(8,128)}, u32[]{:S(2)}) copy-start(f32[3,128,128]{2,1,0:T(8,128)} %upper_diagonal.1) | copy-start | bytes 589828
  52.1 7.6 %collective-permute-start.17 = (bf16[240,128]{1,0:T(8,128)(2,1)S(1)}, bf16[240,128]{1,0:T(8,128)(2,1)S(1)}, u32[]{:S(2)}, u32[]{:S(2)}) collective-permute-start(bf16[240,128]{1,0:T(8,128)(2,1)S(1)} %line.1), channel_id=1, source_target_pairs={{0,24},{4,28},{8,16},{12,20},{16,8},{20,12},{24,0},{28,4},{1,25},{... | collective-permute-start | bytes 184328 | tf_op jit(solution)/shard_map/ppermute | solution.py:23
  53.9 5.9 %collective-permute-start.19 = (bf16[240,128]{1,0:T(8,128)(2,1)S(1)}, bf16[240,128]{1,0:T(8,128)(2,1)S(1)}, u32[]{:S(2)}, u32[]{:S(2)}) collective-permute-start(bf16[240,128]{1,0:T(8,128)(2,1)S(1)} %line.1), channel_id=1, source_target_pairs={{0,16},{4,20},{8,24},{12,28},{16,0},{20,4},{24,8},{28,12},{1,17},{... | collective-permute-start | bytes 184328 | tf_op jit(solution)/shard_map/ppermute | solution.py:23
  54.8 5.0 %collective-permute-start.18 = (bf16[240,128]{1,0:T(8,128)(2,1)S(1)}, bf16[240,128]{1,0:T(8,128)(2,1)S(1)}, u32[]{:S(2)}, u32[]{:S(2)}) collective-permute-start(bf16[240,128]{1,0:T(8,128)(2,1)S(1)} %line.1), channel_id=1, source_target_pairs={{0,8},{4,12},{8,0},{12,4},{16,24},{20,28},{24,16},{28,20},{1,9},{5... | collective-permute-start | bytes 184328 | tf_op jit(solution)/shard_map/ppermute | solution.py:23
  55.7 12.0 %collective-permute-start.21 = (bf16[11,128,128]{2,1,0:T(8,128)(2,1)S(1)}, bf16[11,128,128]{2,1,0:T(8,128)(2,1)S(1)}, u32[]{:S(2)}, u32[]{:S(2)}) collective-permute-start(bf16[11,128,128]{2,1,0:T(8,128)(2,1)S(1)} %get-tuple-element.71), channel_id=1, source_target_pairs={{0,2},{3,1},{4,6},{7,5},{8,10},{11,9},{12,14},{15,13},{16,18},{19,... | collective-permute-start | bytes 1081352 | tf_op jit(solution)/shard_map/ppermute | solution.py:298
  59.8 7.9 %copy-start.7 = (s32[3,1,1]{0,2,1:T(1,128)S(1)}, s32[3,1,1]{0,2,1:T(1,128)}, u32[]{:S(2)}) copy-start(s32[3,1,1]{0,2,1:T(1,128)} %param.11) | copy-start | bytes 40
  59.9 7.9 %copy-start.8 = (s32[8,1,1]{0,2,1:T(1,128)S(1)}, s32[8,1,1]{0,2,1:T(1,128)}, u32[]{:S(2)}) copy-start(s32[8,1,1]{0,2,1:T(1,128)} %param.14) | copy-start | bytes 100
  59.9 2.3 %collective-permute-start.20 = (bf16[4,240,128]{2,1,0:T(8,128)(2,1)S(1)}, bf16[4,240,128]{2,1,0:T(8,128)(2,1)S(1)}, u32[]{:S(2)}, u32[]{:S(2)}) collective-permute-start(bf16[4,240,128]{2,1,0:T(8,128)(2,1)S(1)} %pad_maximum_fusion.near), channel_id=1, source_target_pairs={{0,4},{4,0},{8,12},{12,8},{16,20},{20,16},{24,28},{28,24},{1,5},{5... | collective-permute-start | bytes 737288 | tf_op jit(solution)/shard_map/ppermute | solution.py:23
  60.0 6.7 %collective-permute-start.22 = (bf16[5,128,128]{2,1,0:T(8,128)(2,1)S(1)}, bf16[5,128,128]{2,1,0:T(8,128)(2,1)S(1)}, u32[]{:S(2)}, u32[]{:S(2)}) collective-permute-start(bf16[5,128,128]{2,1,0:T(8,128)(2,1)S(1)} %fusion.3), channel_id=1, source_target_pairs={{0,16},{4,20},{8,24},{12,28},{16,0},{20,4},{24,8},{28,12},{1,17},{... | collective-permute-start | bytes 491528 | tf_op jit(solution)/shard_map/ppermute | solution.py:23
  60.7 7.0 %collective-permute-start.23 = (bf16[6,128,128]{2,1,0:T(8,128)(2,1)S(1)}, bf16[6,128,128]{2,1,0:T(8,128)(2,1)S(1)}, u32[]{:S(2)}, u32[]{:S(2)}) collective-permute-start(bf16[6,128,128]{2,1,0:T(8,128)(2,1)S(1)} %fusion.2), channel_id=1, source_target_pairs={{0,8},{4,12},{8,0},{12,4},{16,24},{20,28},{24,16},{28,20},{1,9},{5... | collective-permute-start | bytes 589832 | tf_op jit(solution)/shard_map/ppermute | solution.py:23

commit v3 on v1

--- a/solution.py
+++ b/solution.py
@@ -304,13 +304,6 @@
     return keep, flip(away, axis, 1 << bit)
 
 
-def gather_doubles(value, axis):
-    value = value[None]
-    for bit in range(1, lax.axis_size(axis).bit_length() - 1):
-        value = jnp.concatenate([value, flip(value, axis, 1 << bit)])
-    return value
-
-
 def gather_near(value, axis):
     masks = range(2, lax.axis_size(axis), 2)
     return [value] + [flip(value, axis, m) for m in masks]
@@ -441,10 +434,12 @@
         [shape_of((depth, chunk, block), F32)],
     )
     sides = [keep + got.astype(F32) for (keep, _), got in zip(halves, tied[depth : depth + 2])]
-    part, last, *sides = tie(part, returns[-1], *sides)
-    near = gather_doubles(part, "row")
-    far, last = tie(flip(near, "row", 1), return_pair(last, "col", reach))
-    got = [*early, last]
+    part, *sides = tie(part, *sides)
+    last = returns[-1]
+    nears = gather_near(part, "row")
+    near = jnp.stack(nears)
+    far = flip(near, "row", 1)
+    got = [*early, return_pair(last, "col", reach)]
     front, back = sides
     for i in range(1, len(bits)):
         keep, across = halve(front, "row", bits[i], bits[i:])
@@ -465,6 +460,7 @@
         ],
         [shape_of((width * chunk, block), F32), shape_of((uppers, 2 * block, block), bf16)],
     )
+    upper_blocks, *got = tie(upper_blocks, *got)
     upper_columns, lower_columns = call(
         columns_kernel,
         "columns",

time: 69.6 us -> 72.9 us (1.047)
  the two profiles are of different devices: /device:TPU:0 before, /device:TPU:8 now
where the time goes in v3:
time: 72.9 us; the launch traced here: 72.7 us
  waiting for transfers between devices  32.1 us (44%)
  starting transfers between devices  26.9 us (37%)
  Pallas kernels  10.6 us (15%)
  local copies, waits for them, and re-layouts  1.32 us (2%)
  between operations  0.92 us (1%)
  other arithmetic  0.84 us (1%)
    ppermute x17, starting transfers between devices, flip(): return lax.ppermute(value, axis, [(i, i ^ mask) for i in range(size)])  15.3 us
    ppermute x2, waiting for transfers between devices, gather_pair(): lax.ppermute(value, axis, [(b, c) for c, b in pairs(lax.axis_size(axis),...  12.1 us
    pallas_call x10, Pallas kernels, call(): pl.pallas_call(kernel, out_shape=outs, in_specs=[SMEM] * len(scalars) + [...  10.6 us
    ppermute x3, waiting for transfers between devices, shift(): lax.ppermute(value, axis, [(i, (i + step) % size) for i in range(size)])  10.4 us
    ppermute x17, waiting for transfers between devices, flip(): return lax.ppermute(value, axis, [(i, i ^ mask) for i in range(size)])  9.59 us
    ppermute x2, starting transfers between devices, gather_pair(): lax.ppermute(value, axis, [(b, c) for c, b in pairs(lax.axis_size(axis),...  4.56 us
    ppermute x3, starting transfers between devices, shift(): lax.ppermute(value, axis, [(i, (i + step) % size) for i in range(size)])  4.12 us
    ppermute x2, starting transfers between devices, return_pair(): return lax.ppermute(value, axis, pairs(lax.axis_size(axis), offset))  2.97 us
  transfers between devices with their start and end apart: 24, of which 12 were waited for; matrix products, arithmetic and copies ran while one was open for 2% of the time, Pallas kernels for 10%

profile of v3, /device:TPU:8, one launch (start us, length us, event | category | flops | bytes accessed | tf_op | source)
XLA Modules:
  0.0 72.7 jit_solution(2072457424051661465)
XLA Ops:
  0.6 1.8 %mask.1.refs_0_ = bf16[11,128,128]{2,1,0:T(8,128)(2,1)} custom-call(s32[3]{0:T(128)} %bitcast.48, s32[8]{0:T(128)} %bitcast.50, bf16[3,128,128]{2,1,0:T(8,128)(2,1)} %bitcast.55, bf16[8,128,128]{2,1,0:T(8,128)(2,1)} %bitcast.54), custom_call_target="tpu_custom_call" | custom-call | tf_op jit(solution)/shard_map/mask/pallas_call | solution.py:41
  2.4 4.5 %collective-permute-start.4 = (bf16[11,128,128]{2,1,0:T(8,128)(2,1)}, bf16[11,128,128]{2,1,0:T(8,128)(2,1)S(1)}, u32[]{:S(2)}, u32[]{:S(2)}) collective-permute-start(bf16[11,128,128]{2,1,0:T(8,128)(2,1)} %mask.1.refs_0_), channel_id=1, source_target_pairs={{2,0},{1,3},{6,4},{5,7},{10,8},{9,11},{14,12},{13,15},{18,16},{17,... | collective-permute-start | bytes 1081352 | tf_op jit(solution)/shard_map/ppermute | solution.py:292
  6.9 0.1 collective-permute-start.3
  7.0 2.5 %collective-permute-start.2 = (bf16[11,128,128]{2,1,0:T(8,128)(2,1)}, bf16[11,128,128]{2,1,0:T(8,128)(2,1)S(1)}, u32[]{:S(2)}, u32[]{:S(2)}) collective-permute-start(bf16[11,128,128]{2,1,0:T(8,128)(2,1)} %mask.1.refs_0_), channel_id=1, source_target_pairs={{0,24},{4,28},{8,16},{12,20},{16,8},{20,12},{24,0},{28,4},{1,25},{... | collective-permute-start | bytes 1081352 | tf_op jit(solution)/shard_map/ppermute | solution.py:23
  9.5 0.5 collective-permute-start.1
  10.0 0.5 collective-permute-start
  10.6 12.1 %collective-permute-done.4.refs_2_.refs_1_ = bf16[11,128,128]{2,1,0:T(8,128)(2,1)S(1)} collective-permute-done((bf16[11,128,128]{2,1,0:T(8,128)(2,1)}, bf16[11,128,128]{2,1,0:T(8,128)(2,1)S(1)}, u32[]{:S(2)}, u32[]{:S(2)}) %collective-permute-start.4) | collective-permute-done | bytes 360480 | tf_op jit(solution)/shard_map/ppermute | solution.py:292
  22.6 0.0 collective-permute-done.3.refs_1_.refs_0_
  22.6 1.0 %copy-done = bf16[11,128,128]{2,1,0:T(8,128)(2,1)S(1)} copy-done((bf16[11,128,128]{2,1,0:T(8,128)(2,1)S(1)}, bf16[11,128,128]{2,1,0:T(8,128)(2,1)}, u32[]{:S(2)}) %copy-start) | copy-done | bytes 360472
  23.6 0.3 turn.1.refs_4_.turned
  24.0 0.0 copy-start.2
  24.0 0.0 copy-start.3
  24.0 1.8 %collective-permute-done.1.refs_2_ = bf16[11,128,128]{2,1,0:T(8,128)(2,1)S(1)} collective-permute-done((bf16[11,128,128]{2,1,0:T(8,128)(2,1)}, bf16[11,128,128]{2,1,0:T(8,128)(2,1)S(1)}, u32[]{:S(2)}, u32[]{:S(2)}) %collective-permute-start.1) | collective-permute-done | bytes 360480 | tf_op jit(solution)/shard_map/ppermute | solution.py:23
  25.8 0.1 collective-permute-done.refs_1_
  25.9 0.1 stack.21.near
  26.0 0.1 collective-permute-start.5
  26.1 0.4 top.1
  26.4 1.0 %partial.1 = (f32[4,11,128,128]{3,2,1,0:T(8,128)S(1)}, bf16[4,11,128,128]{3,2,1,0:T(8,128)(2,1)S(1)}) custom-call(bf16[1024,256]{1,0:T(8,128)(2,1)S(1)} %get-tuple-element.41.top, bf16[11,128,128]{2,1,0:T(8,128)(2,1)S(1)} %collective-permute-done.3.refs_1_.refs_0_, bf16[11,128,128]{2,1,0:T(8,128)(2,1)S(1)} %collective-permute-done.4.refs_2_.refs_1_), custom_call_target="tpu_custom_call" | custom-call | tf_op jit(solution)/shard_map/partial/pallas_call | solution.py:41
  27.4 0.5 collective-permute-start.7
  28.0 0.8 %first.1.start = f32[6,384,256]{2,1,0:T(8,128)S(1)} custom-call(bf16[2,384,512]{2,1,0:T(8,128)(2,1)S(1)} %get-tuple-element.37.top, bf16[4,11,128,128]{3,2,1,0:T(8,128)(2,1)S(1)} %stack.21.near), custom_call_target="tpu_custom_call" | custom-call | tf_op jit(solution)/shard_map/first/pallas_call | solution.py:41
  28.8 0.5 collective-permute-done.5.far
  29.3 2.5 %second.1 = (f32[11,128,128]{2,1,0:T(8,128)S(1)}, bf16[11,128,128]{2,1,0:T(8,128)(2,1)S(1)}, bf16[11,128,128]{2,1,0:T(8,128)(2,1)S(1)}, f32[4,240,128]{2,1,0:T(8,128)S(1)}, f32[4,240,128]{2,1,0:T(8,128)S(1)}) custom-call(s32[8]{0:T(128)S(1)} %copy-done.6, bf16[2,384,512]{2,1,0:T(8,128)(2,1)S(1)} %get-tuple-element.37.top, ...), custom_call_target="tpu_custom_call" | custom-call | tf_op jit(solution)/shard_map/second/pallas_call | solution.py:41
  31.8 0.2 collective-permute-start.6
  32.0 1.7 %collective-permute-start.16 = (bf16[11,128,128]{2,1,0:T(8,128)(2,1)S(1)}, bf16[11,128,128]{2,1,0:T(8,128)(2,1)S(1)}, u32[]{:S(2)}, u32[]{:S(2)}) collective-permute-start(bf16[11,128,128]{2,1,0:T(8,128)(2,1)S(1)} %get-tuple-element.48), channel_id=1, source_target_pairs={{0,1},{1,2},{2,3},{3,0},{4,5},{5,6},{6,7},{7,4},{8,9},{9,10},{10,1... | collective-permute-start | bytes 1081352 | tf_op jit(solution)/shard_map/ppermute | solution.py:296
  33.7 0.0 collective-permute-done.6
  33.7 0.1 fusion.8
  33.8 1.6 %collective-permute-start.8 = (bf16[240,128]{1,0:T(8,128)(2,1)S(1)}, bf16[240,128]{1,0:T(8,128)(2,1)S(1)}, u32[]{:S(2)}, u32[]{:S(2)}) collective-permute-start(bf16[240,128]{1,0:T(8,128)(2,1)S(1)} %get-tuple-element.76), channel_id=1, source_target_pairs={{0,8},{4,12},{8,0},{12,4},{16,24},{20,28},{24,16},{28,20},{1,9},{5... | collective-permute-start | bytes 184328 | tf_op jit(solution)/shard_map/ppermute | solution.py:23
  35.4 1.4 %collective-permute-start.10 = (bf16[240,128]{1,0:T(8,128)(2,1)S(1)}, bf16[240,128]{1,0:T(8,128)(2,1)S(1)}, u32[]{:S(2)}, u32[]{:S(2)}) collective-permute-start(bf16[240,128]{1,0:T(8,128)(2,1)S(1)} %get-tuple-element.77), channel_id=1, source_target_pairs={{0,24},{4,28},{8,16},{12,20},{16,8},{20,12},{24,0},{28,4},{1,25},{... | collective-permute-start | bytes 184328 | tf_op jit(solution)/shard_map/ppermute | solution.py:23
  36.8 0.6 collective-permute-start.9
  37.4 0.5 convert_add_fusion
  37.9 0.4 collective-permute-done.8
  38.3 0.1 slice.95
  38.3 0.1 slice.55
  38.5 1.6 %collective-permute-start.15 = (bf16[2,6,128,128]{3,2,1,0:T(8,128)(2,1)S(1)}, bf16[2,6,128,128]{3,2,1,0:T(8,128)(2,1)S(1)}, u32[]{:S(2)}, u32[]{:S(2)}) collective-permute-start(bf16[2,6,128,128]{3,2,1,0:T(8,128)(2,1)S(1)} %slice.95), channel_id=1, source_target_pairs={{0,16},{4,20},{8,24},{12,28},{16,0},{20,4},{24,8},{28,12},{1,17},{... | collective-permute-start | bytes 1179656 | tf_op jit(solution)/shard_map/ppermute | solution.py:23
  40.1 0.1 fusion.1
  40.1 1.0 %collective-permute-start.14 = (bf16[2,5,128,128]{3,2,1,0:T(8,128)(2,1)S(1)}, bf16[2,5,128,128]{3,2,1,0:T(8,128)(2,1)S(1)}, u32[]{:S(2)}, u32[]{:S(2)}) collective-permute-start(bf16[2,5,128,128]{3,2,1,0:T(8,128)(2,1)S(1)} %fusion.1), channel_id=1, source_target_pairs={{0,8},{4,12},{8,0},{12,4},{16,24},{20,28},{24,16},{28,20},{1,9},{5... | collective-permute-start | bytes 983048 | tf_op jit(solution)/shard_map/ppermute | solution.py:23
  41.2 0.0 collective-permute-done.10
  41.2 0.7 collective-permute-done.9
  41.9 1.7 %collective-permute-start.13 = (bf16[240,128]{1,0:T(8,128)(2,1)S(1)}, bf16[240,128]{1,0:T(8,128)(2,1)S(1)}, u32[]{:S(2)}, u32[]{:S(2)}) collective-permute-start(bf16[240,128]{1,0:T(8,128)(2,1)S(1)} %fusion.7.refs_0_), channel_id=1, source_target_pairs={{0,1},{1,2},{2,3},{3,0},{4,5},{5,6},{6,7},{7,4},{8,9},{9,10},{10,1... | collective-permute-start | bytes 184328 | tf_op jit(solution)/shard_map/ppermute | solution.py:28
  43.7 1.4 %collective-permute-start.12 = (bf16[240,128]{1,0:T(8,128)(2,1)S(1)}, bf16[240,128]{1,0:T(8,128)(2,1)S(1)}, u32[]{:S(2)}, u32[]{:S(2)}) collective-permute-start(bf16[240,128]{1,0:T(8,128)(2,1)S(1)} %fusion.7.refs_0_), channel_id=1, source_target_pairs={{0,2},{1,3},{2,0},{3,1},{4,6},{5,7},{6,4},{7,5},{8,10},{9,11},{10,... | collective-permute-start | bytes 184328 | tf_op jit(solution)/shard_map/ppermute | solution.py:28
  45.1 0.0 collective-permute-done.16.refs_0_
  45.1 1.0 %collective-permute-start.11 = (bf16[240,128]{1,0:T(8,128)(2,1)S(1)}, bf16[240,128]{1,0:T(8,128)(2,1)S(1)}, u32[]{:S(2)}, u32[]{:S(2)}) collective-permute-start(bf16[240,128]{1,0:T(8,128)(2,1)S(1)} %fusion.7.refs_0_), channel_id=1, source_target_pairs={{0,3},{1,0},{2,1},{3,2},{4,7},{5,4},{6,5},{7,6},{8,11},{9,8},{10,9... | collective-permute-start | bytes 184328 | tf_op jit(solution)/shard_map/ppermute | solution.py:28
  46.1 0.7 collective-permute-done.13.refs_3_
  46.8 1.3 %collective-permute-start.23 = (bf16[11,128,128]{2,1,0:T(8,128)(2,1)S(1)}, bf16[11,128,128]{2,1,0:T(8,128)(2,1)S(1)}, u32[]{:S(2)}, u32[]{:S(2)}) collective-permute-start(bf16[11,128,128]{2,1,0:T(8,128)(2,1)S(1)} %get-tuple-element.61), channel_id=1, source_target_pairs={{0,2},{3,1},{4,6},{7,5},{8,10},{11,9},{12,14},{15,13},{16,18},{19,... | collective-permute-start | bytes 1081352 | tf_op jit(solution)/shard_map/ppermute | solution.py:296
  48.1 0.7 collective-permute-done.12.refs_2_
  48.8 9.0 %collective-permute-done.11.refs_1_ = bf16[240,128]{1,0:T(8,128)(2,1)S(1)} collective-permute-done((bf16[240,128]{1,0:T(8,128)(2,1)S(1)}, bf16[240,128]{1,0:T(8,128)(2,1)S(1)}, u32[]{:S(2)}, u32[]{:S(2)}) %collective-permute-start.11) | collective-permute-done | bytes 61472 | tf_op jit(solution)/shard_map/ppermute | solution.py:28
  57.8 0.0 collective-permute-done.15
  57.8 0.1 convert_add_fusion.1
  57.9 0.1 fusion
  58.0 0.1 line.1
  58.0 0.0 copy-start.4
  58.0 0.0 copy-start.5
  58.1 1.7 %collective-permute-start.21 = (bf16[240,128]{1,0:T(8,128)(2,1)S(1)}, bf16[240,128]{1,0:T(8,128)(2,1)S(1)}, u32[]{:S(2)}, u32[]{:S(2)}) collective-permute-start(bf16[240,128]{1,0:T(8,128)(2,1)S(1)} %line.1), channel_id=1, source_target_pairs={{0,24},{4,28},{8,16},{12,20},{16,8},{20,12},{24,0},{28,4},{1,25},{... | collective-permute-start | bytes 184328 | tf_op jit(solution)/shard_map/ppermute | solution.py:23
  59.8 1.8 %collective-permute-start.19 = (bf16[240,128]{1,0:T(8,128)(2,1)S(1)}, bf16[240,128]{1,0:T(8,128)(2,1)S(1)}, u32[]{:S(2)}, u32[]{:S(2)}) collective-permute-start(bf16[240,128]{1,0:T(8,128)(2,1)S(1)} %line.1), channel_id=1, source_target_pairs={{0,8},{4,12},{8,0},{12,4},{16,24},{20,28},{24,16},{28,20},{1,9},{5... | collective-permute-start | bytes 184328 | tf_op jit(solution)/shard_map/ppermute | solution.py:23
  61.6 0.3 collective-permute-start.17
  61.9 1.3 %collective-permute-done.21 = bf16[240,128]{1,0:T(8,128)(2,1)S(1)} collective-permute-done((bf16[240,128]{1,0:T(8,128)(2,1)S(1)}, bf16[240,128]{1,0:T(8,128)(2,1)S(1)}, u32[]{:S(2)}, u32[]{:S(2)}) %collective-permute-start.21) | collective-permute-done | bytes 61472 | tf_op jit(solution)/shard_map/ppermute | solution.py:23
  63.2 0.8 %collective-permute-start.18 = (bf16[6,128,128]{2,1,0:T(8,128)(2,1)S(1)}, bf16[6,128,128]{2,1,0:T(8,128)(2,1)S(1)}, u32[]{:S(2)}, u32[]{:S(2)}) collective-permute-start(bf16[6,128,128]{2,1,0:T(8,128)(2,1)S(1)} %fusion.2), channel_id=1, source_target_pairs={{0,8},{4,12},{8,0},{12,4},{16,24},{20,28},{24,16},{28,20},{1,9},{5... | collective-permute-start | bytes 589832 | tf_op jit(solution)/shard_map/ppermute | solution.py:23
  64.1 0.1 collective-permute-start.22
  64.2 2.9 %collective-permute-done.17 = bf16[5,128,128]{2,1,0:T(8,128)(2,1)S(1)} collective-permute-done((bf16[5,128,128]{2,1,0:T(8,128)(2,1)S(1)}, bf16[5,128,128]{2,1,0:T(8,128)(2,1)S(1)}, u32[]{:S(2)}, u32[]{:S(2)}) %collective-permute-start.17) | collective-permute-done | bytes 163872 | tf_op jit(solution)/shard_map/ppermute | solution.py:23
  67.1 0.0 copy-start.7
  67.1 0.0 copy-start.8
  67.1 1.8 %collective-permute-done.18 = bf16[6,128,128]{2,1,0:T(8,128)(2,1)S(1)} collective-permute-done((bf16[6,128,128]{2,1,0:T(8,128)(2,1)S(1)}, bf16[6,128,128]{2,1,0:T(8,128)(2,1)S(1)}, u32[]{:S(2)}, u32[]{:S(2)}) %collective-permute-start.18) | collective-permute-done | bytes 196640 | tf_op jit(solution)/shard_map/ppermute | solution.py:23
  69.0 2.1 %blocks.1 = (f32[3,128,128]{2,1,0:T(8,128)}, f32[8,128,128]{2,1,0:T(8,128)}, f32[8,128,128]{2,1,0:T(8,128)}) custom-call(s32[8]{0:T(128)S(1)} %copy-done.6, bf16[4,240,128]{2,1,0:T(8,128)(2,1)S(1)} %pad_maximum_fusion.near, bf16[4,240,128]{2,1,0:T(8,128)(2,1)S(1)} %collective-permute-done.22.far, f32[3,128,128]{2,1,0:T(8,128)S(1)} %copy-done.5, ...), custom_call_target="tpu_custom_call" | custom-call | tf_op jit(solution)/shard_map/blocks/pallas_call | solution.py:41
  71.1 1.5 %columns.1 = (bf16[3,128,128]{2,1,0:T(8,128)(2,1)}, bf16[8,128,128]{2,1,0:T(8,128)(2,1)}) custom-call(s32[8]{0:T(128)S(1)} %copy-done.6, s32[3]{0:T(128)S(1)} %bitcast.49, s32[8]{0:T(128)S(1)} %bitcast.51, bf16[8,128,128]{2,1,0:T(8,128)(2,1)S(1)} %copy-done.2, f32[11,128,128]{2,1,0:T(8,128)S(1)} %get-tuple-element.38.own, ...), custom_call_target="tpu_custom_call" | custom-call | tf_op jit(solution)/shard_map/columns/pallas_call | solution.py:41
  (26 shorter events, 0.2 us)
Async XLA Ops:
  2.4 20.2 %collective-permute-start.4 = (bf16[11,128,128]{2,1,0:T(8,128)(2,1)}, bf16[11,128,128]{2,1,0:T(8,128)(2,1)S(1)}, u32[]{:S(2)}, u32[]{:S(2)}) collective-permute-start(bf16[11,128,128]{2,1,0:T(8,128)(2,1)} %mask.1.refs_0_), channel_id=1, source_target_pairs={{2,0},{1,3},{6,4},{5,7},{10,8},{9,11},{14,12},{13,15},{18,16},{17,... | collective-permute-start | bytes 1081352 | tf_op jit(solution)/shard_map/ppermute | solution.py:292
  6.9 15.7 %collective-permute-start.3 = (bf16[11,128,128]{2,1,0:T(8,128)(2,1)}, bf16[11,128,128]{2,1,0:T(8,128)(2,1)S(1)}, u32[]{:S(2)}, u32[]{:S(2)}) collective-permute-start(bf16[11,128,128]{2,1,0:T(8,128)(2,1)} %mask.1.refs_0_), channel_id=1, source_target_pairs={{1,0},{2,1},{3,2},{0,3},{5,4},{6,5},{7,6},{4,7},{9,8},{10,9},{11,1... | collective-permute-start | bytes 1081352 | tf_op jit(solution)/shard_map/ppermute | solution.py:292
  7.0 17.0 %collective-permute-start.2 = (bf16[11,128,128]{2,1,0:T(8,128)(2,1)}, bf16[11,128,128]{2,1,0:T(8,128)(2,1)S(1)}, u32[]{:S(2)}, u32[]{:S(2)}) collective-permute-start(bf16[11,128,128]{2,1,0:T(8,128)(2,1)} %mask.1.refs_0_), channel_id=1, source_target_pairs={{0,24},{4,28},{8,16},{12,20},{16,8},{20,12},{24,0},{28,4},{1,25},{... | collective-permute-start | bytes 1081352 | tf_op jit(solution)/shard_map/ppermute | solution.py:23
  9.5 16.3 %collective-permute-start.1 = (bf16[11,128,128]{2,1,0:T(8,128)(2,1)}, bf16[11,128,128]{2,1,0:T(8,128)(2,1)S(1)}, u32[]{:S(2)}, u32[]{:S(2)}) collective-permute-start(bf16[11,128,128]{2,1,0:T(8,128)(2,1)} %mask.1.refs_0_), channel_id=1, source_target_pairs={{0,16},{4,20},{8,24},{12,28},{16,0},{20,4},{24,8},{28,12},{1,17},{... | collective-permute-start | bytes 1081352 | tf_op jit(solution)/shard_map/ppermute | solution.py:23
  10.0 15.9 %collective-permute-start = (bf16[11,128,128]{2,1,0:T(8,128)(2,1)}, bf16[11,128,128]{2,1,0:T(8,128)(2,1)S(1)}, u32[]{:S(2)}, u32[]{:S(2)}) collective-permute-start(bf16[11,128,128]{2,1,0:T(8,128)(2,1)} %mask.1.refs_0_), channel_id=1, source_target_pairs={{0,8},{4,12},{8,0},{12,4},{16,24},{20,28},{24,16},{28,20},{1,9},{5... | collective-permute-start | bytes 1081352 | tf_op jit(solution)/shard_map/ppermute | solution.py:23
  22.6 1.0 %copy-start = (bf16[11,128,128]{2,1,0:T(8,128)(2,1)S(1)}, bf16[11,128,128]{2,1,0:T(8,128)(2,1)}, u32[]{:S(2)}) copy-start(bf16[11,128,128]{2,1,0:T(8,128)(2,1)} %mask.1.refs_0_) | copy-start | bytes 1081348
  23.6 2.3 %copy-start.1 = (bf16[11,128,128]{2,1,0:T(8,128)(2,1)S(1)}, bf16[11,128,128]{2,1,0:T(8,128)(2,1)}, u32[]{:S(2)}) copy-start(bf16[11,128,128]{2,1,0:T(8,128)(2,1)} %mask.1.refs_0_) | copy-start | bytes 1081348
  24.0 2.1 %copy-start.2 = (bf16[8,128,128]{2,1,0:T(8,128)(2,1)S(1)}, bf16[8,128,128]{2,1,0:T(8,128)(2,1)}, u32[]{:S(2)}) copy-start(bf16[8,128,128]{2,1,0:T(8,128)(2,1)} %panel.5) | copy-start | bytes 786436
  24.0 2.1 %copy-start.3 = (bf16[1,4,8,1,128,128]{5,4,3,2,1,0:T(8,128)(2,1)S(1)}, bf16[1,4,8,1,128,128]{5,4,3,2,1,0:T(8,128)(2,1)}, u32[]{:S(2)}) copy-start(bf16[1,4,8,1,128,128]{5,4,3,2,1,0:T(8,128)(2,1)} %param.9) | copy-start | bytes 3145732
  26.0 3.3 %collective-permute-start.5 = (bf16[4,11,128,128]{3,2,1,0:T(8,128)(2,1)S(1)}, bf16[4,11,128,128]{3,2,1,0:T(8,128)(2,1)S(1)}, u32[]{:S(2)}, u32[]{:S(2)}) collective-permute-start(bf16[4,11,128,128]{3,2,1,0:T(8,128)(2,1)S(1)} %stack.21.near), channel_id=1, source_target_pairs={{0,4},{4,0},{8,12},{12,8},{16,20},{20,16},{24,28},{28,24},{1,5},{5... | collective-permute-start | bytes 4325384 | tf_op jit(solution)/shard_map/ppermute | solution.py:23
  27.4 6.2 %collective-permute-start.7 = (bf16[4,11,128,128]{3,2,1,0:T(8,128)(2,1)S(1)}, bf16[4,11,128,128]{3,2,1,0:T(8,128)(2,1)S(1)}, u32[]{:S(2)}, u32[]{:S(2)}) collective-permute-start(bf16[4,11,128,128]{3,2,1,0:T(8,128)(2,1)S(1)} %get-tuple-element.42), channel_id=1, source_target_pairs={{0,4},{4,0},{8,12},{12,8},{16,20},{20,16},{24,28},{28,24},{1,5},{5... | collective-permute-start | bytes 4325384 | tf_op jit(solution)/shard_map/ppermute | solution.py:23
  28.0 1.3 %copy-start.6 = (s32[8]{0:T(128)S(1)}, s32[8]{0:T(128)}, u32[]{:S(2)}) copy-start(s32[8]{0:T(128)} %parents.5) | copy-start | bytes 100
  31.8 1.9 %collective-permute-start.6 = (f32[4,240,128]{2,1,0:T(8,128)S(1)}, f32[4,240,128]{2,1,0:T(8,128)S(1)}, u32[]{:S(2)}, u32[]{:S(2)}) collective-permute-start(f32[4,240,128]{2,1,0:T(8,128)S(1)} %get-tuple-element.40), channel_id=1, source_target_pairs={{0,4},{4,0},{8,12},{12,8},{16,20},{20,16},{24,28},{28,24},{1,5},{5... | collective-permute-start | bytes 1474568 | tf_op jit(solution)/shard_map/ppermute | solution.py:23
  32.0 13.1 %collective-permute-start.16 = (bf16[11,128,128]{2,1,0:T(8,128)(2,1)S(1)}, bf16[11,128,128]{2,1,0:T(8,128)(2,1)S(1)}, u32[]{:S(2)}, u32[]{:S(2)}) collective-permute-start(bf16[11,128,128]{2,1,0:T(8,128)(2,1)S(1)} %get-tuple-element.48), channel_id=1, source_target_pairs={{0,1},{1,2},{2,3},{3,0},{4,5},{5,6},{6,7},{7,4},{8,9},{9,10},{10,1... | collective-permute-start | bytes 1081352 | tf_op jit(solution)/shard_map/ppermute | solution.py:296
  33.8 4.5 %collective-permute-start.8 = (bf16[240,128]{1,0:T(8,128)(2,1)S(1)}, bf16[240,128]{1,0:T(8,128)(2,1)S(1)}, u32[]{:S(2)}, u32[]{:S(2)}) collective-permute-start(bf16[240,128]{1,0:T(8,128)(2,1)S(1)} %get-tuple-element.76), channel_id=1, source_target_pairs={{0,8},{4,12},{8,0},{12,4},{16,24},{20,28},{24,16},{28,20},{1,9},{5... | collective-permute-start | bytes 184328 | tf_op jit(solution)/shard_map/ppermute | solution.py:23
  35.4 5.8 %collective-permute-start.10 = (bf16[240,128]{1,0:T(8,128)(2,1)S(1)}, bf16[240,128]{1,0:T(8,128)(2,1)S(1)}, u32[]{:S(2)}, u32[]{:S(2)}) collective-permute-start(bf16[240,128]{1,0:T(8,128)(2,1)S(1)} %get-tuple-element.77), channel_id=1, source_target_pairs={{0,24},{4,28},{8,16},{12,20},{16,8},{20,12},{24,0},{28,4},{1,25},{... | collective-permute-start | bytes 184328 | tf_op jit(solution)/shard_map/ppermute | solution.py:23
  36.8 5.1 %collective-permute-start.9 = (bf16[240,128]{1,0:T(8,128)(2,1)S(1)}, bf16[240,128]{1,0:T(8,128)(2,1)S(1)}, u32[]{:S(2)}, u32[]{:S(2)}) collective-permute-start(bf16[240,128]{1,0:T(8,128)(2,1)S(1)} %get-tuple-element.78), channel_id=1, source_target_pairs={{0,16},{4,20},{8,24},{12,28},{16,0},{20,4},{24,8},{28,12},{1,17},{... | collective-permute-start | bytes 184328 | tf_op jit(solution)/shard_map/ppermute | solution.py:23
  38.5 19.3 %collective-permute-start.15 = (bf16[2,6,128,128]{3,2,1,0:T(8,128)(2,1)S(1)}, bf16[2,6,128,128]{3,2,1,0:T(8,128)(2,1)S(1)}, u32[]{:S(2)}, u32[]{:S(2)}) collective-permute-start(bf16[2,6,128,128]{3,2,1,0:T(8,128)(2,1)S(1)} %slice.95), channel_id=1, source_target_pairs={{0,16},{4,20},{8,24},{12,28},{16,0},{20,4},{24,8},{28,12},{1,17},{... | collective-permute-start | bytes 1179656 | tf_op jit(solution)/shard_map/ppermute | solution.py:23
  40.1 17.7 %collective-permute-start.14 = (bf16[2,5,128,128]{3,2,1,0:T(8,128)(2,1)S(1)}, bf16[2,5,128,128]{3,2,1,0:T(8,128)(2,1)S(1)}, u32[]{:S(2)}, u32[]{:S(2)}) collective-permute-start(bf16[2,5,128,128]{3,2,1,0:T(8,128)(2,1)S(1)} %fusion.1), channel_id=1, source_target_pairs={{0,8},{4,12},{8,0},{12,4},{16,24},{20,28},{24,16},{28,20},{1,9},{5... | collective-permute-start | bytes 983048 | tf_op jit(solution)/shard_map/ppermute | solution.py:23
  41.9 4.8 %collective-permute-start.13 = (bf16[240,128]{1,0:T(8,128)(2,1)S(1)}, bf16[240,128]{1,0:T(8,128)(2,1)S(1)}, u32[]{:S(2)}, u32[]{:S(2)}) collective-permute-start(bf16[240,128]{1,0:T(8,128)(2,1)S(1)} %fusion.7.refs_0_), channel_id=1, source_target_pairs={{0,1},{1,2},{2,3},{3,0},{4,5},{5,6},{6,7},{7,4},{8,9},{9,10},{10,1... | collective-permute-start | bytes 184328 | tf_op jit(solution)/shard_map/ppermute | solution.py:28
  43.7 5.1 %collective-permute-start.12 = (bf16[240,128]{1,0:T(8,128)(2,1)S(1)}, bf16[240,128]{1,0:T(8,128)(2,1)S(1)}, u32[]{:S(2)}, u32[]{:S(2)}) collective-permute-start(bf16[240,128]{1,0:T(8,128)(2,1)S(1)} %fusion.7.refs_0_), channel_id=1, source_target_pairs={{0,2},{1,3},{2,0},{3,1},{4,6},{5,7},{6,4},{7,5},{8,10},{9,11},{10,... | collective-permute-start | bytes 184328 | tf_op jit(solution)/shard_map/ppermute | solution.py:28
  45.1 12.7 %collective-permute-start.11 = (bf16[240,128]{1,0:T(8,128)(2,1)S(1)}, bf16[240,128]{1,0:T(8,128)(2,1)S(1)}, u32[]{:S(2)}, u32[]{:S(2)}) collective-permute-start(bf16[240,128]{1,0:T(8,128)(2,1)S(1)} %fusion.7.refs_0_), channel_id=1, source_target_pairs={{0,3},{1,0},{2,1},{3,2},{4,7},{5,4},{6,5},{7,6},{8,11},{9,8},{10,9... | collective-permute-start | bytes 184328 | tf_op jit(solution)/shard_map/ppermute | solution.py:28
  46.8 24.3 %collective-permute-start.23 = (bf16[11,128,128]{2,1,0:T(8,128)(2,1)S(1)}, bf16[11,128,128]{2,1,0:T(8,128)(2,1)S(1)}, u32[]{:S(2)}, u32[]{:S(2)}) collective-permute-start(bf16[11,128,128]{2,1,0:T(8,128)(2,1)S(1)} %get-tuple-element.61), channel_id=1, source_target_pairs={{0,2},{3,1},{4,6},{7,5},{8,10},{11,9},{12,14},{15,13},{16,18},{19,... | collective-permute-start | bytes 1081352 | tf_op jit(solution)/shard_map/ppermute | solution.py:296
  58.0 10.9 %copy-start.4 = (f32[8,128,128]{2,1,0:T(8,128)S(1)}, f32[8,128,128]{2,1,0:T(8,128)}, u32[]{:S(2)}) copy-start(f32[8,128,128]{2,1,0:T(8,128)} %lower_diagonal.1) | copy-start | bytes 1572868
  58.0 10.9 %copy-start.5 = (f32[3,128,128]{2,1,0:T(8,128)S(1)}, f32[3,128,128]{2,1,0:T(8,128)}, u32[]{:S(2)}) copy-start(f32[3,128,128]{2,1,0:T(8,128)} %upper_diagonal.1) | copy-start | bytes 589828
  58.1 5.2 %collective-permute-start.21 = (bf16[240,128]{1,0:T(8,128)(2,1)S(1)}, bf16[240,128]{1,0:T(8,128)(2,1)S(1)}, u32[]{:S(2)}, u32[]{:S(2)}) collective-permute-start(bf16[240,128]{1,0:T(8,128)(2,1)S(1)} %line.1), channel_id=1, source_target_pairs={{0,24},{4,28},{8,16},{12,20},{16,8},{20,12},{24,0},{28,4},{1,25},{... | collective-permute-start | bytes 184328 | tf_op jit(solution)/shard_map/ppermute | solution.py:23
  59.8 4.3 %collective-permute-start.20 = (bf16[240,128]{1,0:T(8,128)(2,1)S(1)}, bf16[240,128]{1,0:T(8,128)(2,1)S(1)}, u32[]{:S(2)}, u32[]{:S(2)}) collective-permute-start(bf16[240,128]{1,0:T(8,128)(2,1)S(1)} %line.1), channel_id=1, source_target_pairs={{0,16},{4,20},{8,24},{12,28},{16,0},{20,4},{24,8},{28,12},{1,17},{... | collective-permute-start | bytes 184328 | tf_op jit(solution)/shard_map/ppermute | solution.py:23
  59.8 4.3 %collective-permute-start.19 = (bf16[240,128]{1,0:T(8,128)(2,1)S(1)}, bf16[240,128]{1,0:T(8,128)(2,1)S(1)}, u32[]{:S(2)}, u32[]{:S(2)}) collective-permute-start(bf16[240,128]{1,0:T(8,128)(2,1)S(1)} %line.1), channel_id=1, source_target_pairs={{0,8},{4,12},{8,0},{12,4},{16,24},{20,28},{24,16},{28,20},{1,9},{5... | collective-permute-start | bytes 184328 | tf_op jit(solution)/shard_map/ppermute | solution.py:23
  61.6 5.4 %collective-permute-start.17 = (bf16[5,128,128]{2,1,0:T(8,128)(2,1)S(1)}, bf16[5,128,128]{2,1,0:T(8,128)(2,1)S(1)}, u32[]{:S(2)}, u32[]{:S(2)}) collective-permute-start(bf16[5,128,128]{2,1,0:T(8,128)(2,1)S(1)} %fusion.3), channel_id=1, source_target_pairs={{0,16},{4,20},{8,24},{12,28},{16,0},{20,4},{24,8},{28,12},{1,17},{... | collective-permute-start | bytes 491528 | tf_op jit(solution)/shard_map/ppermute | solution.py:23
  63.2 5.7 %collective-permute-start.18 = (bf16[6,128,128]{2,1,0:T(8,128)(2,1)S(1)}, bf16[6,128,128]{2,1,0:T(8,128)(2,1)S(1)}, u32[]{:S(2)}, u32[]{:S(2)}) collective-permute-start(bf16[6,128,128]{2,1,0:T(8,128)(2,1)S(1)} %fusion.2), channel_id=1, source_target_pairs={{0,8},{4,12},{8,0},{12,4},{16,24},{20,28},{24,16},{28,20},{1,9},{5... | collective-permute-start | bytes 589832 | tf_op jit(solution)/shard_map/ppermute | solution.py:23
  64.1 4.9 %collective-permute-start.22 = (bf16[4,240,128]{2,1,0:T(8,128)(2,1)S(1)}, bf16[4,240,128]{2,1,0:T(8,128)(2,1)S(1)}, u32[]{:S(2)}, u32[]{:S(2)}) collective-permute-start(bf16[4,240,128]{2,1,0:T(8,128)(2,1)S(1)} %pad_maximum_fusion.near), channel_id=1, source_target_pairs={{0,4},{4,0},{8,12},{12,8},{16,20},{20,16},{24,28},{28,24},{1,5},{5... | collective-permute-start | bytes 737288 | tf_op jit(solution)/shard_map/ppermute | solution.py:23
  67.1 4.1 %copy-start.7 = (s32[3,1,1]{0,2,1:T(1,128)S(1)}, s32[3,1,1]{0,2,1:T(1,128)}, u32[]{:S(2)}) copy-start(s32[3,1,1]{0,2,1:T(1,128)} %param.11) | copy-start | bytes 40
  67.1 4.1 %copy-start.8 = (s32[8,1,1]{0,2,1:T(1,128)S(1)}, s32[8,1,1]{0,2,1:T(1,128)}, u32[]{:S(2)}) copy-start(s32[8,1,1]{0,2,1:T(1,128)} %param.14) | copy-start | bytes 100

commit v4 on v3

--- a/solution.py
+++ b/solution.py
@@ -434,8 +434,7 @@
         [shape_of((depth, chunk, block), F32)],
     )
     sides = [keep + got.astype(F32) for (keep, _), got in zip(halves, tied[depth : depth + 2])]
-    part, *sides = tie(part, *sides)
-    last = returns[-1]
+    part, last, *sides = tie(part, returns[-1], *sides)
     nears = gather_near(part, "row")
     near = jnp.stack(nears)
     far = flip(near, "row", 1)

time: 72.9 us -> 69.2 us (0.949)
  the two profiles are of different devices: /device:TPU:8 before, /device:TPU:0 now
where the time goes in v4:
time: 69.2 us; the launch traced here: 69 us
  starting transfers between devices  33.3 us (48%)
  waiting for transfers between devices  22 us (32%)
  Pallas kernels  10.6 us (15%)
  local copies, waits for them, and re-layouts  1.32 us (2%)
  between operations  0.93 us (1%)
  other arithmetic  0.85 us (1%)
    ppermute x17, starting transfers between devices, flip(): return lax.ppermute(value, axis, [(i, i ^ mask) for i in range(size)])  16.5 us
    ppermute x2, waiting for transfers between devices, gather_pair(): lax.ppermute(value, axis, [(b, c) for c, b in pairs(lax.axis_size(axis),...  11.8 us
    pallas_call x10, Pallas kernels, call(): pl.pallas_call(kernel, out_shape=outs, in_specs=[SMEM] * len(scalars) + [...  10.6 us
    ppermute x2, starting transfers between devices, gather_pair(): lax.ppermute(value, axis, [(b, c) for c, b in pairs(lax.axis_size(axis),...  6.38 us
    ppermute x17, waiting for transfers between devices, flip(): return lax.ppermute(value, axis, [(i, i ^ mask) for i in range(size)])  5.66 us
    ppermute x3, starting transfers between devices, shift(): lax.ppermute(value, axis, [(i, (i + step) % size) for i in range(size)])  5.36 us
    ppermute x2, starting transfers between devices, return_pair(): return lax.ppermute(value, axis, pairs(lax.axis_size(axis), offset))  5.12 us
    ppermute x3, waiting for transfers between devices, shift(): lax.ppermute(value, axis, [(i, (i + step) % size) for i in range(size)])  2.83 us
  transfers between devices with their start and end apart: 24, of which 12 were waited for; matrix products, arithmetic and copies ran while one was open for 1% of the time, Pallas kernels for 10%

profile of v4, /device:TPU:0, one launch (start us, length us, event | category | flops | bytes accessed | tf_op | source)
XLA Modules:
  0.0 69.0 jit_solution(17894788069304690385)
XLA Ops:
  0.6 1.8 %mask.1.refs_0_ = bf16[11,128,128]{2,1,0:T(8,128)(2,1)} custom-call(s32[3]{0:T(128)} %bitcast.48, s32[8]{0:T(128)} %bitcast.50, bf16[3,128,128]{2,1,0:T(8,128)(2,1)} %bitcast.55, bf16[8,128,128]{2,1,0:T(8,128)(2,1)} %bitcast.54), custom_call_target="tpu_custom_call" | custom-call | tf_op jit(solution)/shard_map/mask/pallas_call | solution.py:41
  2.4 1.3 %collective-permute-start.4 = (bf16[11,128,128]{2,1,0:T(8,128)(2,1)}, bf16[11,128,128]{2,1,0:T(8,128)(2,1)S(1)}, u32[]{:S(2)}, u32[]{:S(2)}) collective-permute-start(bf16[11,128,128]{2,1,0:T(8,128)(2,1)} %mask.1.refs_0_), channel_id=1, source_target_pairs={{2,0},{1,3},{6,4},{5,7},{10,8},{9,11},{14,12},{13,15},{18,16},{17,... | collective-permute-start | bytes 1081352 | tf_op jit(solution)/shard_map/ppermute | solution.py:292
  3.7 5.1 %collective-permute-start.3 = (bf16[11,128,128]{2,1,0:T(8,128)(2,1)}, bf16[11,128,128]{2,1,0:T(8,128)(2,1)S(1)}, u32[]{:S(2)}, u32[]{:S(2)}) collective-permute-start(bf16[11,128,128]{2,1,0:T(8,128)(2,1)} %mask.1.refs_0_), channel_id=1, source_target_pairs={{1,0},{2,1},{3,2},{0,3},{5,4},{6,5},{7,6},{4,7},{9,8},{10,9},{11,1... | collective-permute-start | bytes 1081352 | tf_op jit(solution)/shard_map/ppermute | solution.py:292
  8.8 2.4 %collective-permute-start.2 = (bf16[11,128,128]{2,1,0:T(8,128)(2,1)}, bf16[11,128,128]{2,1,0:T(8,128)(2,1)S(1)}, u32[]{:S(2)}, u32[]{:S(2)}) collective-permute-start(bf16[11,128,128]{2,1,0:T(8,128)(2,1)} %mask.1.refs_0_), channel_id=1, source_target_pairs={{0,24},{4,28},{8,16},{12,20},{16,8},{20,12},{24,0},{28,4},{1,25},{... | collective-permute-start | bytes 1081352 | tf_op jit(solution)/shard_map/ppermute | solution.py:23
  11.3 0.5 collective-permute-start.1
  11.8 0.5 collective-permute-start
  12.3 4.9 %collective-permute-done.4.refs_2_.refs_1_ = bf16[11,128,128]{2,1,0:T(8,128)(2,1)S(1)} collective-permute-done((bf16[11,128,128]{2,1,0:T(8,128)(2,1)}, bf16[11,128,128]{2,1,0:T(8,128)(2,1)S(1)}, u32[]{:S(2)}, u32[]{:S(2)}) %collective-permute-start.4) | collective-permute-done | bytes 360480 | tf_op jit(solution)/shard_map/ppermute | solution.py:292
  17.2 6.9 %collective-permute-done.3.refs_1_.refs_0_ = bf16[11,128,128]{2,1,0:T(8,128)(2,1)S(1)} collective-permute-done((bf16[11,128,128]{2,1,0:T(8,128)(2,1)}, bf16[11,128,128]{2,1,0:T(8,128)(2,1)S(1)}, u32[]{:S(2)}, u32[]{:S(2)}) %collective-permute-start.3) | collective-permute-done | bytes 360480 | tf_op jit(solution)/shard_map/ppermute | solution.py:292
  24.1 1.0 %copy-done = bf16[11,128,128]{2,1,0:T(8,128)(2,1)S(1)} copy-done((bf16[11,128,128]{2,1,0:T(8,128)(2,1)S(1)}, bf16[11,128,128]{2,1,0:T(8,128)(2,1)}, u32[]{:S(2)}) %copy-start) | copy-done | bytes 360472
  25.1 0.3 turn.1.refs_4_.turned
  25.4 0.0 copy-start.2
  25.4 0.0 copy-start.3
  25.4 2.1 %collective-permute-done.1.refs_2_ = bf16[11,128,128]{2,1,0:T(8,128)(2,1)S(1)} collective-permute-done((bf16[11,128,128]{2,1,0:T(8,128)(2,1)}, bf16[11,128,128]{2,1,0:T(8,128)(2,1)S(1)}, u32[]{:S(2)}, u32[]{:S(2)}) %collective-permute-start.1) | collective-permute-done | bytes 360480 | tf_op jit(solution)/shard_map/ppermute | solution.py:23
  27.5 0.1 collective-permute-done.refs_1_
  27.6 0.1 stack.21.near
  27.7 0.1 collective-permute-start.5
  27.8 0.4 top.1
  28.2 1.0 %partial.1 = (f32[4,11,128,128]{3,2,1,0:T(8,128)S(1)}, bf16[4,11,128,128]{3,2,1,0:T(8,128)(2,1)S(1)}) custom-call(bf16[1024,256]{1,0:T(8,128)(2,1)S(1)} %get-tuple-element.42.top, bf16[11,128,128]{2,1,0:T(8,128)(2,1)S(1)} %collective-permute-done.3.refs_1_.refs_0_, bf16[11,128,128]{2,1,0:T(8,128)(2,1)S(1)} %collective-permute-done.4.refs_2_.refs_1_), custom_call_target="tpu_custom_call" | custom-call | tf_op jit(solution)/shard_map/partial/pallas_call | solution.py:41
  29.2 0.5 collective-permute-start.7
  29.7 0.8 %first.1.start = f32[6,384,256]{2,1,0:T(8,128)S(1)} custom-call(bf16[2,384,512]{2,1,0:T(8,128)(2,1)S(1)} %get-tuple-element.38.top, bf16[4,11,128,128]{3,2,1,0:T(8,128)(2,1)S(1)} %stack.21.near), custom_call_target="tpu_custom_call" | custom-call | tf_op jit(solution)/shard_map/first/pallas_call | solution.py:41
  30.5 0.5 collective-permute-done.5.far
  31.0 2.5 %second.1 = (f32[11,128,128]{2,1,0:T(8,128)S(1)}, bf16[11,128,128]{2,1,0:T(8,128)(2,1)S(1)}, bf16[11,128,128]{2,1,0:T(8,128)(2,1)S(1)}, f32[4,240,128]{2,1,0:T(8,128)S(1)}, f32[4,240,128]{2,1,0:T(8,128)S(1)}) custom-call(s32[8]{0:T(128)S(1)} %copy-done.6, bf16[2,384,512]{2,1,0:T(8,128)(2,1)S(1)} %get-tuple-element.38.top, ...), custom_call_target="tpu_custom_call" | custom-call | tf_op jit(solution)/shard_map/second/pallas_call | solution.py:41
  33.5 0.2 collective-permute-start.6
  33.7 1.3 %collective-permute-start.16 = (bf16[11,128,128]{2,1,0:T(8,128)(2,1)S(1)}, bf16[11,128,128]{2,1,0:T(8,128)(2,1)S(1)}, u32[]{:S(2)}, u32[]{:S(2)}) collective-permute-start(bf16[11,128,128]{2,1,0:T(8,128)(2,1)S(1)} %get-tuple-element.49), channel_id=1, source_target_pairs={{0,1},{1,2},{2,3},{3,0},{4,5},{5,6},{6,7},{7,4},{8,9},{9,10},{10,1... | collective-permute-start | bytes 1081352 | tf_op jit(solution)/shard_map/ppermute | solution.py:296
  35.0 0.0 collective-permute-done.7
  35.0 0.4 collective-permute-done.6
  35.5 0.1 fusion.8
  35.6 1.6 %collective-permute-start.8 = (bf16[240,128]{1,0:T(8,128)(2,1)S(1)}, bf16[240,128]{1,0:T(8,128)(2,1)S(1)}, u32[]{:S(2)}, u32[]{:S(2)}) collective-permute-start(bf16[240,128]{1,0:T(8,128)(2,1)S(1)} %get-tuple-element.78), channel_id=1, source_target_pairs={{0,8},{4,12},{8,0},{12,4},{16,24},{20,28},{24,16},{28,20},{1,9},{5... | collective-permute-start | bytes 184328 | tf_op jit(solution)/shard_map/ppermute | solution.py:23
  37.1 1.4 %collective-permute-start.10 = (bf16[240,128]{1,0:T(8,128)(2,1)S(1)}, bf16[240,128]{1,0:T(8,128)(2,1)S(1)}, u32[]{:S(2)}, u32[]{:S(2)}) collective-permute-start(bf16[240,128]{1,0:T(8,128)(2,1)S(1)} %get-tuple-element.79), channel_id=1, source_target_pairs={{0,24},{4,28},{8,16},{12,20},{16,8},{20,12},{24,0},{28,4},{1,25},{... | collective-permute-start | bytes 184328 | tf_op jit(solution)/shard_map/ppermute | solution.py:23
  38.5 0.6 collective-permute-start.9
  39.1 0.5 convert_add_fusion
  39.6 0.4 collective-permute-done.8
  40.0 0.1 slice.95
  40.1 0.1 slice.55
  40.2 1.6 %collective-permute-start.15 = (bf16[2,6,128,128]{3,2,1,0:T(8,128)(2,1)S(1)}, bf16[2,6,128,128]{3,2,1,0:T(8,128)(2,1)S(1)}, u32[]{:S(2)}, u32[]{:S(2)}) collective-permute-start(bf16[2,6,128,128]{3,2,1,0:T(8,128)(2,1)S(1)} %slice.95), channel_id=1, source_target_pairs={{0,16},{4,20},{8,24},{12,28},{16,0},{20,4},{24,8},{28,12},{1,17},{... | collective-permute-start | bytes 1179656 | tf_op jit(solution)/shard_map/ppermute | solution.py:23
  41.8 0.1 fusion.1
  41.9 1.0 %collective-permute-start.14 = (bf16[2,5,128,128]{3,2,1,0:T(8,128)(2,1)S(1)}, bf16[2,5,128,128]{3,2,1,0:T(8,128)(2,1)S(1)}, u32[]{:S(2)}, u32[]{:S(2)}) collective-permute-start(bf16[2,5,128,128]{3,2,1,0:T(8,128)(2,1)S(1)} %fusion.1), channel_id=1, source_target_pairs={{0,8},{4,12},{8,0},{12,4},{16,24},{20,28},{24,16},{28,20},{1,9},{5... | collective-permute-start | bytes 983048 | tf_op jit(solution)/shard_map/ppermute | solution.py:23
  42.9 0.7 %collective-permute-done.9 = bf16[240,128]{1,0:T(8,128)(2,1)S(1)} collective-permute-done((bf16[240,128]{1,0:T(8,128)(2,1)S(1)}, bf16[240,128]{1,0:T(8,128)(2,1)S(1)}, u32[]{:S(2)}, u32[]{:S(2)}) %collective-permute-start.9) | collective-permute-done | bytes 61472 | tf_op jit(solution)/shard_map/ppermute | solution.py:23
  43.7 1.3 %collective-permute-start.13 = (bf16[240,128]{1,0:T(8,128)(2,1)S(1)}, bf16[240,128]{1,0:T(8,128)(2,1)S(1)}, u32[]{:S(2)}, u32[]{:S(2)}) collective-permute-start(bf16[240,128]{1,0:T(8,128)(2,1)S(1)} %fusion.7.refs_0_), channel_id=1, source_target_pairs={{0,1},{1,2},{2,3},{3,0},{4,5},{5,6},{6,7},{7,4},{8,9},{9,10},{10,1... | collective-permute-start | bytes 184328 | tf_op jit(solution)/shard_map/ppermute | solution.py:28
  45.0 2.0 %collective-permute-start.12 = (bf16[240,128]{1,0:T(8,128)(2,1)S(1)}, bf16[240,128]{1,0:T(8,128)(2,1)S(1)}, u32[]{:S(2)}, u32[]{:S(2)}) collective-permute-start(bf16[240,128]{1,0:T(8,128)(2,1)S(1)} %fusion.7.refs_0_), channel_id=1, source_target_pairs={{0,2},{1,3},{2,0},{3,1},{4,6},{5,7},{6,4},{7,5},{8,10},{9,11},{10,... | collective-permute-start | bytes 184328 | tf_op jit(solution)/shard_map/ppermute | solution.py:28
  47.1 0.0 collective-permute-done.16.refs_0_
  47.1 2.0 %collective-permute-start.11 = (bf16[240,128]{1,0:T(8,128)(2,1)S(1)}, bf16[240,128]{1,0:T(8,128)(2,1)S(1)}, u32[]{:S(2)}, u32[]{:S(2)}) collective-permute-start(bf16[240,128]{1,0:T(8,128)(2,1)S(1)} %fusion.7.refs_0_), channel_id=1, source_target_pairs={{0,3},{1,0},{2,1},{3,2},{4,7},{5,4},{6,5},{7,6},{8,11},{9,8},{10,9... | collective-permute-start | bytes 184328 | tf_op jit(solution)/shard_map/ppermute | solution.py:28
  49.0 1.3 %collective-permute-done.13.refs_3_ = bf16[240,128]{1,0:T(8,128)(2,1)S(1)} collective-permute-done((bf16[240,128]{1,0:T(8,128)(2,1)S(1)}, bf16[240,128]{1,0:T(8,128)(2,1)S(1)}, u32[]{:S(2)}, u32[]{:S(2)}) %collective-permute-start.13) | collective-permute-done | bytes 61472 | tf_op jit(solution)/shard_map/ppermute | solution.py:28
  50.4 1.5 %collective-permute-done.12.refs_2_ = bf16[240,128]{1,0:T(8,128)(2,1)S(1)} collective-permute-done((bf16[240,128]{1,0:T(8,128)(2,1)S(1)}, bf16[240,128]{1,0:T(8,128)(2,1)S(1)}, u32[]{:S(2)}, u32[]{:S(2)}) %collective-permute-start.12) | collective-permute-done | bytes 61472 | tf_op jit(solution)/shard_map/ppermute | solution.py:28
  51.9 0.0 collective-permute-done.11.refs_1_
  51.9 0.1 convert_add_fusion.1
  52.0 0.1 fusion
  52.0 0.1 line.1
  52.1 0.0 copy-start.4
  52.1 0.0 copy-start.5
  52.1 1.7 %collective-permute-start.21 = (bf16[240,128]{1,0:T(8,128)(2,1)S(1)}, bf16[240,128]{1,0:T(8,128)(2,1)S(1)}, u32[]{:S(2)}, u32[]{:S(2)}) collective-permute-start(bf16[240,128]{1,0:T(8,128)(2,1)S(1)} %line.1), channel_id=1, source_target_pairs={{0,24},{4,28},{8,16},{12,20},{16,8},{20,12},{24,0},{28,4},{1,25},{... | collective-permute-start | bytes 184328 | tf_op jit(solution)/shard_map/ppermute | solution.py:23
  53.9 0.9 %collective-permute-start.20 = (bf16[240,128]{1,0:T(8,128)(2,1)S(1)}, bf16[240,128]{1,0:T(8,128)(2,1)S(1)}, u32[]{:S(2)}, u32[]{:S(2)}) collective-permute-start(bf16[240,128]{1,0:T(8,128)(2,1)S(1)} %line.1), channel_id=1, source_target_pairs={{0,16},{4,20},{8,24},{12,28},{16,0},{20,4},{24,8},{28,12},{1,17},{... | collective-permute-start | bytes 184328 | tf_op jit(solution)/shard_map/ppermute | solution.py:23
  54.8 0.9 %collective-permute-start.19 = (bf16[240,128]{1,0:T(8,128)(2,1)S(1)}, bf16[240,128]{1,0:T(8,128)(2,1)S(1)}, u32[]{:S(2)}, u32[]{:S(2)}) collective-permute-start(bf16[240,128]{1,0:T(8,128)(2,1)S(1)} %line.1), channel_id=1, source_target_pairs={{0,8},{4,12},{8,0},{12,4},{16,24},{20,28},{24,16},{28,20},{1,9},{5... | collective-permute-start | bytes 184328 | tf_op jit(solution)/shard_map/ppermute | solution.py:23
  55.7 0.7 collective-permute-start.17
  56.4 1.7 %collective-permute-start.18 = (bf16[6,128,128]{2,1,0:T(8,128)(2,1)S(1)}, bf16[6,128,128]{2,1,0:T(8,128)(2,1)S(1)}, u32[]{:S(2)}, u32[]{:S(2)}) collective-permute-start(bf16[6,128,128]{2,1,0:T(8,128)(2,1)S(1)} %fusion.2), channel_id=1, source_target_pairs={{0,8},{4,12},{8,0},{12,4},{16,24},{20,28},{24,16},{28,20},{1,9},{5... | collective-permute-start | bytes 589832 | tf_op jit(solution)/shard_map/ppermute | solution.py:23
  58.1 3.8 %collective-permute-start.23 = (bf16[11,128,128]{2,1,0:T(8,128)(2,1)S(1)}, bf16[11,128,128]{2,1,0:T(8,128)(2,1)S(1)}, u32[]{:S(2)}, u32[]{:S(2)}) collective-permute-start(bf16[11,128,128]{2,1,0:T(8,128)(2,1)S(1)} %get-tuple-element.63), channel_id=1, source_target_pairs={{0,2},{3,1},{4,6},{7,5},{8,10},{11,9},{12,14},{15,13},{16,18},{19,... | collective-permute-start | bytes 1081352 | tf_op jit(solution)/shard_map/ppermute | solution.py:296
  62.0 0.1 collective-permute-start.22
  62.1 0.0 copy-start.7
  62.2 0.0 copy-start.8
  62.2 0.0 collective-permute-done.18
  62.2 1.4 %collective-permute-done.22.far = bf16[4,240,128]{2,1,0:T(8,128)(2,1)S(1)} collective-permute-done((bf16[4,240,128]{2,1,0:T(8,128)(2,1)S(1)}, bf16[4,240,128]{2,1,0:T(8,128)(2,1)S(1)}, u32[]{:S(2)}, u32[]{:S(2)}) %collective-permute-start.22) | collective-permute-done | bytes 245792 | tf_op jit(solution)/shard_map/ppermute | solution.py:23
  63.6 2.1 %blocks.1 = (f32[3,128,128]{2,1,0:T(8,128)}, f32[8,128,128]{2,1,0:T(8,128)}, f32[8,128,128]{2,1,0:T(8,128)}) custom-call(s32[8]{0:T(128)S(1)} %copy-done.6, bf16[4,240,128]{2,1,0:T(8,128)(2,1)S(1)} %pad_maximum_fusion.near, bf16[4,240,128]{2,1,0:T(8,128)(2,1)S(1)} %collective-permute-done.22.far, f32[3,128,128]{2,1,0:T(8,128)S(1)} %copy-done.5, ...), custom_call_target="tpu_custom_call" | custom-call | tf_op jit(solution)/shard_map/blocks/pallas_call | solution.py:41
  65.7 1.7 %collective-permute-done.23.refs_1_ = bf16[11,128,128]{2,1,0:T(8,128)(2,1)S(1)} collective-permute-done((bf16[11,128,128]{2,1,0:T(8,128)(2,1)S(1)}, bf16[11,128,128]{2,1,0:T(8,128)(2,1)S(1)}, u32[]{:S(2)}, u32[]{:S(2)}) %collective-permute-start.23) | collective-permute-done | bytes 360480 | tf_op jit(solution)/shard_map/ppermute | solution.py:296
  67.5 1.5 %columns.1 = (bf16[3,128,128]{2,1,0:T(8,128)(2,1)}, bf16[8,128,128]{2,1,0:T(8,128)(2,1)}) custom-call(s32[8]{0:T(128)S(1)} %copy-done.6, s32[3]{0:T(128)S(1)} %bitcast.49, s32[8]{0:T(128)S(1)} %bitcast.51, bf16[8,128,128]{2,1,0:T(8,128)(2,1)S(1)} %copy-done.2, f32[11,128,128]{2,1,0:T(8,128)S(1)} %get-tuple-element.39.own, ...), custom_call_target="tpu_custom_call" | custom-call | tf_op jit(solution)/shard_map/columns/pallas_call | solution.py:41
  (26 shorter events, 0.2 us)
Async XLA Ops:
  2.4 14.8 %collective-permute-start.4 = (bf16[11,128,128]{2,1,0:T(8,128)(2,1)}, bf16[11,128,128]{2,1,0:T(8,128)(2,1)S(1)}, u32[]{:S(2)}, u32[]{:S(2)}) collective-permute-start(bf16[11,128,128]{2,1,0:T(8,128)(2,1)} %mask.1.refs_0_), channel_id=1, source_target_pairs={{2,0},{1,3},{6,4},{5,7},{10,8},{9,11},{14,12},{13,15},{18,16},{17,... | collective-permute-start | bytes 1081352 | tf_op jit(solution)/shard_map/ppermute | solution.py:292
  3.7 20.4 %collective-permute-start.3 = (bf16[11,128,128]{2,1,0:T(8,128)(2,1)}, bf16[11,128,128]{2,1,0:T(8,128)(2,1)S(1)}, u32[]{:S(2)}, u32[]{:S(2)}) collective-permute-start(bf16[11,128,128]{2,1,0:T(8,128)(2,1)} %mask.1.refs_0_), channel_id=1, source_target_pairs={{1,0},{2,1},{3,2},{0,3},{5,4},{6,5},{7,6},{4,7},{9,8},{10,9},{11,1... | collective-permute-start | bytes 1081352 | tf_op jit(solution)/shard_map/ppermute | solution.py:292
  8.8 16.6 %collective-permute-start.2 = (bf16[11,128,128]{2,1,0:T(8,128)(2,1)}, bf16[11,128,128]{2,1,0:T(8,128)(2,1)S(1)}, u32[]{:S(2)}, u32[]{:S(2)}) collective-permute-start(bf16[11,128,128]{2,1,0:T(8,128)(2,1)} %mask.1.refs_0_), channel_id=1, source_target_pairs={{0,24},{4,28},{8,16},{12,20},{16,8},{20,12},{24,0},{28,4},{1,25},{... | collective-permute-start | bytes 1081352 | tf_op jit(solution)/shard_map/ppermute | solution.py:23
  11.3 16.3 %collective-permute-start.1 = (bf16[11,128,128]{2,1,0:T(8,128)(2,1)}, bf16[11,128,128]{2,1,0:T(8,128)(2,1)S(1)}, u32[]{:S(2)}, u32[]{:S(2)}) collective-permute-start(bf16[11,128,128]{2,1,0:T(8,128)(2,1)} %mask.1.refs_0_), channel_id=1, source_target_pairs={{0,16},{4,20},{8,24},{12,28},{16,0},{20,4},{24,8},{28,12},{1,17},{... | collective-permute-start | bytes 1081352 | tf_op jit(solution)/shard_map/ppermute | solution.py:23
  11.8 15.9 %collective-permute-start = (bf16[11,128,128]{2,1,0:T(8,128)(2,1)}, bf16[11,128,128]{2,1,0:T(8,128)(2,1)S(1)}, u32[]{:S(2)}, u32[]{:S(2)}) collective-permute-start(bf16[11,128,128]{2,1,0:T(8,128)(2,1)} %mask.1.refs_0_), channel_id=1, source_target_pairs={{0,8},{4,12},{8,0},{12,4},{16,24},{20,28},{24,16},{28,20},{1,9},{5... | collective-permute-start | bytes 1081352 | tf_op jit(solution)/shard_map/ppermute | solution.py:23
  24.1 1.0 %copy-start = (bf16[11,128,128]{2,1,0:T(8,128)(2,1)S(1)}, bf16[11,128,128]{2,1,0:T(8,128)(2,1)}, u32[]{:S(2)}) copy-start(bf16[11,128,128]{2,1,0:T(8,128)(2,1)} %mask.1.refs_0_) | copy-start | bytes 1081348
  25.1 2.6 %copy-start.1 = (bf16[11,128,128]{2,1,0:T(8,128)(2,1)S(1)}, bf16[11,128,128]{2,1,0:T(8,128)(2,1)}, u32[]{:S(2)}) copy-start(bf16[11,128,128]{2,1,0:T(8,128)(2,1)} %mask.1.refs_0_) | copy-start | bytes 1081348
  25.4 2.4 %copy-start.2 = (bf16[8,128,128]{2,1,0:T(8,128)(2,1)S(1)}, bf16[8,128,128]{2,1,0:T(8,128)(2,1)}, u32[]{:S(2)}) copy-start(bf16[8,128,128]{2,1,0:T(8,128)(2,1)} %panel.5) | copy-start | bytes 786436
  25.4 2.4 %copy-start.3 = (bf16[1,4,8,1,128,128]{5,4,3,2,1,0:T(8,128)(2,1)S(1)}, bf16[1,4,8,1,128,128]{5,4,3,2,1,0:T(8,128)(2,1)}, u32[]{:S(2)}) copy-start(bf16[1,4,8,1,128,128]{5,4,3,2,1,0:T(8,128)(2,1)} %param.9) | copy-start | bytes 3145732
  27.7 3.3 %collective-permute-start.5 = (bf16[4,11,128,128]{3,2,1,0:T(8,128)(2,1)S(1)}, bf16[4,11,128,128]{3,2,1,0:T(8,128)(2,1)S(1)}, u32[]{:S(2)}, u32[]{:S(2)}) collective-permute-start(bf16[4,11,128,128]{3,2,1,0:T(8,128)(2,1)S(1)} %stack.21.near), channel_id=1, source_target_pairs={{0,4},{4,0},{8,12},{12,8},{16,20},{20,16},{24,28},{28,24},{1,5},{5... | collective-permute-start | bytes 4325384 | tf_op jit(solution)/shard_map/ppermute | solution.py:23
  29.2 5.8 %collective-permute-start.7 = (bf16[4,11,128,128]{3,2,1,0:T(8,128)(2,1)S(1)}, bf16[4,11,128,128]{3,2,1,0:T(8,128)(2,1)S(1)}, u32[]{:S(2)}, u32[]{:S(2)}) collective-permute-start(bf16[4,11,128,128]{3,2,1,0:T(8,128)(2,1)S(1)} %get-tuple-element.43), channel_id=1, source_target_pairs={{0,4},{4,0},{8,12},{12,8},{16,20},{20,16},{24,28},{28,24},{1,5},{5... | collective-permute-start | bytes 4325384 | tf_op jit(solution)/shard_map/ppermute | solution.py:23
  29.7 1.3 %copy-start.6 = (s32[8]{0:T(128)S(1)}, s32[8]{0:T(128)}, u32[]{:S(2)}) copy-start(s32[8]{0:T(128)} %parents.5) | copy-start | bytes 100
  33.5 1.9 %collective-permute-start.6 = (f32[4,240,128]{2,1,0:T(8,128)S(1)}, f32[4,240,128]{2,1,0:T(8,128)S(1)}, u32[]{:S(2)}, u32[]{:S(2)}) collective-permute-start(f32[4,240,128]{2,1,0:T(8,128)S(1)} %get-tuple-element.41), channel_id=1, source_target_pairs={{0,4},{4,0},{8,12},{12,8},{16,20},{20,16},{24,28},{28,24},{1,5},{5... | collective-permute-start | bytes 1474568 | tf_op jit(solution)/shard_map/ppermute | solution.py:23
  33.7 13.3 %collective-permute-start.16 = (bf16[11,128,128]{2,1,0:T(8,128)(2,1)S(1)}, bf16[11,128,128]{2,1,0:T(8,128)(2,1)S(1)}, u32[]{:S(2)}, u32[]{:S(2)}) collective-permute-start(bf16[11,128,128]{2,1,0:T(8,128)(2,1)S(1)} %get-tuple-element.49), channel_id=1, source_target_pairs={{0,1},{1,2},{2,3},{3,0},{4,5},{5,6},{6,7},{7,4},{8,9},{9,10},{10,1... | collective-permute-start | bytes 1081352 | tf_op jit(solution)/shard_map/ppermute | solution.py:296
  35.6 4.5 %collective-permute-start.8 = (bf16[240,128]{1,0:T(8,128)(2,1)S(1)}, bf16[240,128]{1,0:T(8,128)(2,1)S(1)}, u32[]{:S(2)}, u32[]{:S(2)}) collective-permute-start(bf16[240,128]{1,0:T(8,128)(2,1)S(1)} %get-tuple-element.78), channel_id=1, source_target_pairs={{0,8},{4,12},{8,0},{12,4},{16,24},{20,28},{24,16},{28,20},{1,9},{5... | collective-permute-start | bytes 184328 | tf_op jit(solution)/shard_map/ppermute | solution.py:23
  37.1 5.8 %collective-permute-start.10 = (bf16[240,128]{1,0:T(8,128)(2,1)S(1)}, bf16[240,128]{1,0:T(8,128)(2,1)S(1)}, u32[]{:S(2)}, u32[]{:S(2)}) collective-permute-start(bf16[240,128]{1,0:T(8,128)(2,1)S(1)} %get-tuple-element.79), channel_id=1, source_target_pairs={{0,24},{4,28},{8,16},{12,20},{16,8},{20,12},{24,0},{28,4},{1,25},{... | collective-permute-start | bytes 184328 | tf_op jit(solution)/shard_map/ppermute | solution.py:23
  38.5 5.1 %collective-permute-start.9 = (bf16[240,128]{1,0:T(8,128)(2,1)S(1)}, bf16[240,128]{1,0:T(8,128)(2,1)S(1)}, u32[]{:S(2)}, u32[]{:S(2)}) collective-permute-start(bf16[240,128]{1,0:T(8,128)(2,1)S(1)} %get-tuple-element.80), channel_id=1, source_target_pairs={{0,16},{4,20},{8,24},{12,28},{16,0},{20,4},{24,8},{28,12},{1,17},{... | collective-permute-start | bytes 184328 | tf_op jit(solution)/shard_map/ppermute | solution.py:23
  40.2 11.7 %collective-permute-start.15 = (bf16[2,6,128,128]{3,2,1,0:T(8,128)(2,1)S(1)}, bf16[2,6,128,128]{3,2,1,0:T(8,128)(2,1)S(1)}, u32[]{:S(2)}, u32[]{:S(2)}) collective-permute-start(bf16[2,6,128,128]{3,2,1,0:T(8,128)(2,1)S(1)} %slice.95), channel_id=1, source_target_pairs={{0,16},{4,20},{8,24},{12,28},{16,0},{20,4},{24,8},{28,12},{1,17},{... | collective-permute-start | bytes 1179656 | tf_op jit(solution)/shard_map/ppermute | solution.py:23
  41.9 10.0 %collective-permute-start.14 = (bf16[2,5,128,128]{3,2,1,0:T(8,128)(2,1)S(1)}, bf16[2,5,128,128]{3,2,1,0:T(8,128)(2,1)S(1)}, u32[]{:S(2)}, u32[]{:S(2)}) collective-permute-start(bf16[2,5,128,128]{3,2,1,0:T(8,128)(2,1)S(1)} %fusion.1), channel_id=1, source_target_pairs={{0,8},{4,12},{8,0},{12,4},{16,24},{20,28},{24,16},{28,20},{1,9},{5... | collective-permute-start | bytes 983048 | tf_op jit(solution)/shard_map/ppermute | solution.py:23
  43.7 6.7 %collective-permute-start.13 = (bf16[240,128]{1,0:T(8,128)(2,1)S(1)}, bf16[240,128]{1,0:T(8,128)(2,1)S(1)}, u32[]{:S(2)}, u32[]{:S(2)}) collective-permute-start(bf16[240,128]{1,0:T(8,128)(2,1)S(1)} %fusion.7.refs_0_), channel_id=1, source_target_pairs={{0,1},{1,2},{2,3},{3,0},{4,5},{5,6},{6,7},{7,4},{8,9},{9,10},{10,1... | collective-permute-start | bytes 184328 | tf_op jit(solution)/shard_map/ppermute | solution.py:28
  45.0 6.9 %collective-permute-start.12 = (bf16[240,128]{1,0:T(8,128)(2,1)S(1)}, bf16[240,128]{1,0:T(8,128)(2,1)S(1)}, u32[]{:S(2)}, u32[]{:S(2)}) collective-permute-start(bf16[240,128]{1,0:T(8,128)(2,1)S(1)} %fusion.7.refs_0_), channel_id=1, source_target_pairs={{0,2},{1,3},{2,0},{3,1},{4,6},{5,7},{6,4},{7,5},{8,10},{9,11},{10,... | collective-permute-start | bytes 184328 | tf_op jit(solution)/shard_map/ppermute | solution.py:28
  47.1 4.8 %collective-permute-start.11 = (bf16[240,128]{1,0:T(8,128)(2,1)S(1)}, bf16[240,128]{1,0:T(8,128)(2,1)S(1)}, u32[]{:S(2)}, u32[]{:S(2)}) collective-permute-start(bf16[240,128]{1,0:T(8,128)(2,1)S(1)} %fusion.7.refs_0_), channel_id=1, source_target_pairs={{0,3},{1,0},{2,1},{3,2},{4,7},{5,4},{6,5},{7,6},{8,11},{9,8},{10,9... | collective-permute-start | bytes 184328 | tf_op jit(solution)/shard_map/ppermute | solution.py:28
  52.1 11.5 %copy-start.4 = (f32[8,128,128]{2,1,0:T(8,128)S(1)}, f32[8,128,128]{2,1,0:T(8,128)}, u32[]{:S(2)}) copy-start(f32[8,128,128]{2,1,0:T(8,128)} %lower_diagonal.1) | copy-start | bytes 1572868
  52.1 11.5 %copy-start.5 = (f32[3,128,128]{2,1,0:T(8,128)S(1)}, f32[3,128,128]{2,1,0:T(8,128)}, u32[]{:S(2)}) copy-start(f32[3,128,128]{2,1,0:T(8,128)} %upper_diagonal.1) | copy-start | bytes 589828
  52.1 6.0 %collective-permute-start.21 = (bf16[240,128]{1,0:T(8,128)(2,1)S(1)}, bf16[240,128]{1,0:T(8,128)(2,1)S(1)}, u32[]{:S(2)}, u32[]{:S(2)}) collective-permute-start(bf16[240,128]{1,0:T(8,128)(2,1)S(1)} %line.1), channel_id=1, source_target_pairs={{0,24},{4,28},{8,16},{12,20},{16,8},{20,12},{24,0},{28,4},{1,25},{... | collective-permute-start | bytes 184328 | tf_op jit(solution)/shard_map/ppermute | solution.py:23
  53.9 8.1 %collective-permute-start.20 = (bf16[240,128]{1,0:T(8,128)(2,1)S(1)}, bf16[240,128]{1,0:T(8,128)(2,1)S(1)}, u32[]{:S(2)}, u32[]{:S(2)}) collective-permute-start(bf16[240,128]{1,0:T(8,128)(2,1)S(1)} %line.1), channel_id=1, source_target_pairs={{0,16},{4,20},{8,24},{12,28},{16,0},{20,4},{24,8},{28,12},{1,17},{... | collective-permute-start | bytes 184328 | tf_op jit(solution)/shard_map/ppermute | solution.py:23
  54.8 7.2 %collective-permute-start.19 = (bf16[240,128]{1,0:T(8,128)(2,1)S(1)}, bf16[240,128]{1,0:T(8,128)(2,1)S(1)}, u32[]{:S(2)}, u32[]{:S(2)}) collective-permute-start(bf16[240,128]{1,0:T(8,128)(2,1)S(1)} %line.1), channel_id=1, source_target_pairs={{0,8},{4,12},{8,0},{12,4},{16,24},{20,28},{24,16},{28,20},{1,9},{5... | collective-permute-start | bytes 184328 | tf_op jit(solution)/shard_map/ppermute | solution.py:23
  55.7 6.4 %collective-permute-start.17 = (bf16[5,128,128]{2,1,0:T(8,128)(2,1)S(1)}, bf16[5,128,128]{2,1,0:T(8,128)(2,1)S(1)}, u32[]{:S(2)}, u32[]{:S(2)}) collective-permute-start(bf16[5,128,128]{2,1,0:T(8,128)(2,1)S(1)} %fusion.3), channel_id=1, source_target_pairs={{0,16},{4,20},{8,24},{12,28},{16,0},{20,4},{24,8},{28,12},{1,17},{... | collective-permute-start | bytes 491528 | tf_op jit(solution)/shard_map/ppermute | solution.py:23
  56.4 5.7 %collective-permute-start.18 = (bf16[6,128,128]{2,1,0:T(8,128)(2,1)S(1)}, bf16[6,128,128]{2,1,0:T(8,128)(2,1)S(1)}, u32[]{:S(2)}, u32[]{:S(2)}) collective-permute-start(bf16[6,128,128]{2,1,0:T(8,128)(2,1)S(1)} %fusion.2), channel_id=1, source_target_pairs={{0,8},{4,12},{8,0},{12,4},{16,24},{20,28},{24,16},{28,20},{1,9},{5... | collective-permute-start | bytes 589832 | tf_op jit(solution)/shard_map/ppermute | solution.py:23
  58.1 9.3 %collective-permute-start.23 = (bf16[11,128,128]{2,1,0:T(8,128)(2,1)S(1)}, bf16[11,128,128]{2,1,0:T(8,128)(2,1)S(1)}, u32[]{:S(2)}, u32[]{:S(2)}) collective-permute-start(bf16[11,128,128]{2,1,0:T(8,128)(2,1)S(1)} %get-tuple-element.63), channel_id=1, source_target_pairs={{0,2},{3,1},{4,6},{7,5},{8,10},{11,9},{12,14},{15,13},{16,18},{19,... | collective-permute-start | bytes 1081352 | tf_op jit(solution)/shard_map/ppermute | solution.py:296
  62.0 1.6 %collective-permute-start.22 = (bf16[4,240,128]{2,1,0:T(8,128)(2,1)S(1)}, bf16[4,240,128]{2,1,0:T(8,128)(2,1)S(1)}, u32[]{:S(2)}, u32[]{:S(2)}) collective-permute-start(bf16[4,240,128]{2,1,0:T(8,128)(2,1)S(1)} %pad_maximum_fusion.near), channel_id=1, source_target_pairs={{0,4},{4,0},{8,12},{12,8},{16,20},{20,16},{24,28},{28,24},{1,5},{5... | collective-permute-start | bytes 737288 | tf_op jit(solution)/shard_map/ppermute | solution.py:23
  62.1 5.3 %copy-start.7 = (s32[3,1,1]{0,2,1:T(1,128)S(1)}, s32[3,1,1]{0,2,1:T(1,128)}, u32[]{:S(2)}) copy-start(s32[3,1,1]{0,2,1:T(1,128)} %param.11) | copy-start | bytes 40
  62.2 5.3 %copy-start.8 = (s32[8,1,1]{0,2,1:T(1,128)S(1)}, s32[8,1,1]{0,2,1:T(1,128)}, u32[]{:S(2)}) copy-start(s32[8,1,1]{0,2,1:T(1,128)} %param.14) | copy-start | bytes 100

commit v5 on v4

--- a/solution.py
+++ b/solution.py
@@ -51,7 +51,7 @@
 
 
 def stack_kernel(*refs):
-    for i, piece in enumerate(refs[:-2]):
+    for i, piece in enumerate(refs[:-3]):
         refs[-1][i] = piece[...]
 
 
@@ -107,18 +107,16 @@
                 away[i, k] = far.astype(away.dtype)
 
 
-def dot_pair(left, pieces, first, second):
-    right = [
-        jnp.concatenate([pieces[i, first], pieces[i, second]], axis=1)
-        for i in range(pieces.shape[0])
-    ]
+def dot_pair(left, own, others, first, second):
+    pieces = [own, *[others.at[i] for i in range(others.shape[0])]]
+    right = [jnp.concatenate([piece[first], piece[second]], axis=1) for piece in pieces]
     return jnp.dot(left, jnp.concatenate(right), preferred_element_type=F32)
 
 
-def first_kernel(top, near, out):
-    total = near.shape[1]
+def first_kernel(top, own, near, out):
+    total = own.shape[0]
     for first in range(0, total, 2):
-        out[first // 2] = dot_pair(top[0], near, first, min(first + 1, total - 1))
+        out[first // 2] = dot_pair(top[0], own, near, first, min(first + 1, total - 1))
 
 
 def triangle(block):
@@ -128,7 +126,7 @@
 
 
 def pack(squares, packed, start):
-    total, block = squares.shape[:2]
+    total, block = len(squares), squares[0].shape[0]
     above, diagonal = triangle(block)
     for p in range(total // 2):
         first, second = [squares[k] + squares[k].T for k in (2 * p, 2 * p + 1)]
@@ -153,8 +151,8 @@
     return squares
 
 
-def second_kernel(uppers, parents, top, far, start, turned, *refs):
-    own, returns, (sums_keep, sums_away, both, squares, packed) = refs[0], refs[1:-5], refs[-5:]
+def second_kernel(uppers, parents, top, far_own, far, start, turned, *refs):
+    own, returns, (sums_keep, sums_away, both, packed) = refs[0], refs[1:-4], refs[-4:]
     total, block, reach = turned.shape
     lowers = total - uppers
     half, chunk, _ = sums_keep.shape
@@ -162,7 +160,7 @@
 
     for first in range(0, total, 2):
         second = min(first + 1, total - 1)
-        value = start[first // 2] + dot_pair(top[1], far, first, second)
+        value = start[first // 2] + dot_pair(top[1], far_own, far, first, second)
         for lane, k in enumerate(range(first, second + 1)):
             part = value[:, lane * block : (lane + 1) * block]
             own[k] = part[:block]
@@ -178,14 +176,14 @@
         return value[:, :block] + value[:, block:]
 
     base = (total + 1) // 2 * block
-    for k in range(uppers):
-        squares[k] = fold(turned[k], k)
+    squares = [fold(turned[k], k) for k in range(uppers)]
+    crossed = [fold(turned[uppers + m], parents[m]) for m in range(lowers)]
     for m in range(lowers):
-        own_row, parent = turned[uppers + m], parents[m]
-        value = fold(jnp.concatenate([own_row, turned[parent]], axis=0), uppers + m)
-        squares[uppers + m] = value[:block]
+        rows = jnp.concatenate([turned[uppers + m], turned[parents[m]]], axis=0)
+        value = fold(rows, uppers + m)
+        squares.append(value[:block])
         place = base + m * block
-        packed[place : place + block] = value[block:] + fold(own_row, parent).T
+        packed[place : place + block] = value[block:] + crossed[m].T
     end = base + lowers * block
     packed[end:] = jnp.zeros((packed.shape[0] - end, block), F32)
     pack(squares, packed, end)
@@ -356,12 +354,13 @@
         (masked, *pieces),
         [shape_of((total, block, (reach + 1) * block), bf16)],
     )
+    far_own = flip(masked, "row", 1)
     (near,) = call(
         stack_kernel,
         "stack",
         (),
-        (*gather_near(masked, "row"), turned),
-        [shape_of((half, total, block, block), bf16)],
+        (*gather_near(masked, "row")[1:], turned, far_own),
+        [shape_of((half - 1, total, block, block), bf16)],
     )
     far = flip(near, "row", 1)
     top, top_turned, panel_turned = call(
@@ -390,20 +389,19 @@
         first_kernel,
         "first",
         (),
-        (top, near),
+        (top, masked, near),
         [shape_of((columns_n, (reach + 1) * block, 2 * block), F32)],
     )
     own, *rest = call(
         functools.partial(second_kernel, uppers),
         "second",
         (parents,),
-        (top, far, start, turned),
+        (top, far_own, far, start, turned),
         [shape_of((total, block, block), F32)]
         + [shape_of((total, block, block), WIRE)] * reach
         + [shape_of((half, chunk, block), F32)] * 2,
         [
             shape_of((total, (reach + 1) * block, 2 * block), bf16),
-            shape_of((total, block, block), F32),
             shape_of((width * chunk, block), F32),
         ],
     )

time: 69.2 us -> 68.9 us (level)
    ppermute x17 -> x18, waiting for transfers between devices: 5.66 us -> 4.87 us  [flip(): return lax.ppermute(value, axis, [(i, i ^ mask) for i in range(size)])]
    ppermute x17 -> x18, starting transfers between devices: 16.5 us -> 16.5 us  [flip(): return lax.ppermute(value, axis, [(i, i ^ mask) for i in range(size)])]
  transfers between devices with their start and end apart: 24 -> 25, of which waited for: 12 -> 13; matrix products, arithmetic and copies ran while one was open for 1% -> 1% of each run, Pallas kernels for 10% -> 10%
where the time goes in v5:
time: 68.9 us; the launch traced here: 68.7 us
  starting transfers between devices  33.4 us (48%)
  waiting for transfers between devices  21.6 us (31%)
  Pallas kernels  10.6 us (15%)
  local copies, waits for them, and re-layouts  1.32 us (2%)
  between operations  0.94 us (1%)
  other arithmetic  0.85 us (1%)
    ppermute x18, starting transfers between devices, flip(): return lax.ppermute(value, axis, [(i, i ^ mask) for i in range(size)])  16.5 us
    ppermute x2, waiting for transfers between devices, gather_pair(): lax.ppermute(value, axis, [(b, c) for c, b in pairs(lax.axis_size(axis),...  11.8 us
    pallas_call x10, Pallas kernels, call(): pl.pallas_call(kernel, out_shape=outs, in_specs=[SMEM] * len(scalars) + [...  10.6 us
    ppermute x2, starting transfers between devices, gather_pair(): lax.ppermute(value, axis, [(b, c) for c, b in pairs(lax.axis_size(axis),...  6.38 us
    ppermute x3, starting transfers between devices, shift(): lax.ppermute(value, axis, [(i, (i + step) % size) for i in range(size)])  5.36 us
    ppermute x2, starting transfers between devices, return_pair(): return lax.ppermute(value, axis, pairs(lax.axis_size(axis), offset))  5.1 us
    ppermute x18, waiting for transfers between devices, flip(): return lax.ppermute(value, axis, [(i, i ^ mask) for i in range(size)])  4.87 us
    ppermute x3, waiting for transfers between devices, shift(): lax.ppermute(value, axis, [(i, (i + step) % size) for i in range(size)])  3.11 us
  transfers between devices with their start and end apart: 25, of which 13 were waited for; matrix products, arithmetic and copies ran while one was open for 1% of the time, Pallas kernels for 10%

profile of v5, /device:TPU:0, one launch (start us, length us, event | category | flops | bytes accessed | tf_op | source)
XLA Modules:
  0.0 68.7 jit_solution(13309072236385847429)
XLA Ops:
  0.6 1.8 %mask.1.refs_0_.own = bf16[11,128,128]{2,1,0:T(8,128)(2,1)} custom-call(s32[3]{0:T(128)} %bitcast.48, s32[8]{0:T(128)} %bitcast.50, bf16[3,128,128]{2,1,0:T(8,128)(2,1)} %bitcast.55, bf16[8,128,128]{2,1,0:T(8,128)(2,1)} %bitcast.54), custom_call_target="tpu_custom_call" | custom-call | tf_op jit(solution)/shard_map/mask/pallas_call | solution.py:41
  2.4 1.3 %collective-permute-start.5 = (bf16[11,128,128]{2,1,0:T(8,128)(2,1)}, bf16[11,128,128]{2,1,0:T(8,128)(2,1)S(1)}, u32[]{:S(2)}, u32[]{:S(2)}) collective-permute-start(bf16[11,128,128]{2,1,0:T(8,128)(2,1)} %mask.1.refs_0_.own), channel_id=1, source_target_pairs={{2,0},{1,3},{6,4},{5,7},{10,8},{9,11},{14,12},{13,15},{18,16},{17,... | collective-permute-start | bytes 1081352 | tf_op jit(solution)/shard_map/ppermute | solution.py:290
  3.7 5.1 %collective-permute-start.4 = (bf16[11,128,128]{2,1,0:T(8,128)(2,1)}, bf16[11,128,128]{2,1,0:T(8,128)(2,1)S(1)}, u32[]{:S(2)}, u32[]{:S(2)}) collective-permute-start(bf16[11,128,128]{2,1,0:T(8,128)(2,1)} %mask.1.refs_0_.own), channel_id=1, source_target_pairs={{1,0},{2,1},{3,2},{0,3},{5,4},{6,5},{7,6},{4,7},{9,8},{10,9},{11,1... | collective-permute-start | bytes 1081352 | tf_op jit(solution)/shard_map/ppermute | solution.py:290
  8.8 2.4 %collective-permute-start.3 = (bf16[11,128,128]{2,1,0:T(8,128)(2,1)}, bf16[11,128,128]{2,1,0:T(8,128)(2,1)S(1)}, u32[]{:S(2)}, u32[]{:S(2)}) collective-permute-start(bf16[11,128,128]{2,1,0:T(8,128)(2,1)} %mask.1.refs_0_.own), channel_id=1, source_target_pairs={{0,24},{4,28},{8,16},{12,20},{16,8},{20,12},{24,0},{28,4},{1,25},{... | collective-permute-start | bytes 1081352 | tf_op jit(solution)/shard_map/ppermute | solution.py:23
  11.3 0.5 collective-permute-start.2
  11.8 0.5 collective-permute-start.1
  12.3 4.9 %collective-permute-done.5.refs_2_.refs_1_ = bf16[11,128,128]{2,1,0:T(8,128)(2,1)S(1)} collective-permute-done((bf16[11,128,128]{2,1,0:T(8,128)(2,1)}, bf16[11,128,128]{2,1,0:T(8,128)(2,1)S(1)}, u32[]{:S(2)}, u32[]{:S(2)}) %collective-permute-start.5) | collective-permute-done | bytes 360480 | tf_op jit(solution)/shard_map/ppermute | solution.py:290
  17.2 0.0 collective-permute-start
  17.2 6.8 %collective-permute-done.4.refs_1_.refs_0_ = bf16[11,128,128]{2,1,0:T(8,128)(2,1)S(1)} collective-permute-done((bf16[11,128,128]{2,1,0:T(8,128)(2,1)}, bf16[11,128,128]{2,1,0:T(8,128)(2,1)S(1)}, u32[]{:S(2)}, u32[]{:S(2)}) %collective-permute-start.4) | collective-permute-done | bytes 360480 | tf_op jit(solution)/shard_map/ppermute | solution.py:290
  24.1 1.0 %copy-done = bf16[11,128,128]{2,1,0:T(8,128)(2,1)S(1)} copy-done((bf16[11,128,128]{2,1,0:T(8,128)(2,1)S(1)}, bf16[11,128,128]{2,1,0:T(8,128)(2,1)}, u32[]{:S(2)}) %copy-start) | copy-done | bytes 360472
  25.1 0.3 turn.1.refs_3_.turned
  25.4 0.0 copy-start.2
  25.4 0.0 copy-start.3
  25.4 2.1 %collective-permute-done.2.refs_1_ = bf16[11,128,128]{2,1,0:T(8,128)(2,1)S(1)} collective-permute-done((bf16[11,128,128]{2,1,0:T(8,128)(2,1)}, bf16[11,128,128]{2,1,0:T(8,128)(2,1)S(1)}, u32[]{:S(2)}, u32[]{:S(2)}) %collective-permute-start.2) | collective-permute-done | bytes 360480 | tf_op jit(solution)/shard_map/ppermute | solution.py:23
  27.5 0.1 collective-permute-done.1.refs_0_
  27.6 0.1 stack.21.near
  27.7 0.0 copy-start.1
  27.7 0.1 collective-permute-start.6
  27.8 0.4 top.1
  28.2 1.0 %partial.1 = (f32[4,11,128,128]{3,2,1,0:T(8,128)S(1)}, bf16[4,11,128,128]{3,2,1,0:T(8,128)(2,1)S(1)}) custom-call(bf16[1024,256]{1,0:T(8,128)(2,1)S(1)} %get-tuple-element.42.top, bf16[11,128,128]{2,1,0:T(8,128)(2,1)S(1)} %collective-permute-done.4.refs_1_.refs_0_, bf16[11,128,128]{2,1,0:T(8,128)(2,1)S(1)} %collective-permute-done.5.refs_2_.refs_1_), custom_call_target="tpu_custom_call" | custom-call | tf_op jit(solution)/shard_map/partial/pallas_call | solution.py:41
  29.2 0.5 collective-permute-start.8
  29.7 0.8 %first.1.start = f32[6,384,256]{2,1,0:T(8,128)S(1)} custom-call(bf16[2,384,512]{2,1,0:T(8,128)(2,1)S(1)} %get-tuple-element.38.top, bf16[11,128,128]{2,1,0:T(8,128)(2,1)S(1)} %copy-done.1, bf16[3,11,128,128]{3,2,1,0:T(8,128)(2,1)S(1)} %stack.21.near), custom_call_target="tpu_custom_call" | custom-call | tf_op jit(solution)/shard_map/first/pallas_call | solution.py:41
  30.5 0.0 collective-permute-done.6.far
  30.5 2.5 %second.1 = (f32[11,128,128]{2,1,0:T(8,128)S(1)}, bf16[11,128,128]{2,1,0:T(8,128)(2,1)S(1)}, bf16[11,128,128]{2,1,0:T(8,128)(2,1)S(1)}, f32[4,240,128]{2,1,0:T(8,128)S(1)}, f32[4,240,128]{2,1,0:T(8,128)S(1)}) custom-call(s32[8]{0:T(128)S(1)} %copy-done.6, bf16[2,384,512]{2,1,0:T(8,128)(2,1)S(1)} %get-tuple-element.38.top, ...), custom_call_target="tpu_custom_call" | custom-call | tf_op jit(solution)/shard_map/second/pallas_call | solution.py:41
  33.1 0.2 collective-permute-start.7
  33.3 1.3 %collective-permute-start.17 = (bf16[11,128,128]{2,1,0:T(8,128)(2,1)S(1)}, bf16[11,128,128]{2,1,0:T(8,128)(2,1)S(1)}, u32[]{:S(2)}, u32[]{:S(2)}) collective-permute-start(bf16[11,128,128]{2,1,0:T(8,128)(2,1)S(1)} %get-tuple-element.49), channel_id=1, source_target_pairs={{0,1},{1,2},{2,3},{3,0},{4,5},{5,6},{6,7},{7,4},{8,9},{9,10},{10,1... | collective-permute-start | bytes 1081352 | tf_op jit(solution)/shard_map/ppermute | solution.py:294
  34.5 0.5 collective-permute-done.7
  35.0 0.1 fusion.8
  35.1 1.6 %collective-permute-start.9 = (bf16[240,128]{1,0:T(8,128)(2,1)S(1)}, bf16[240,128]{1,0:T(8,128)(2,1)S(1)}, u32[]{:S(2)}, u32[]{:S(2)}) collective-permute-start(bf16[240,128]{1,0:T(8,128)(2,1)S(1)} %get-tuple-element.78), channel_id=1, source_target_pairs={{0,8},{4,12},{8,0},{12,4},{16,24},{20,28},{24,16},{28,20},{1,9},{5... | collective-permute-start | bytes 184328 | tf_op jit(solution)/shard_map/ppermute | solution.py:23
  36.7 1.4 %collective-permute-start.11 = (bf16[240,128]{1,0:T(8,128)(2,1)S(1)}, bf16[240,128]{1,0:T(8,128)(2,1)S(1)}, u32[]{:S(2)}, u32[]{:S(2)}) collective-permute-start(bf16[240,128]{1,0:T(8,128)(2,1)S(1)} %get-tuple-element.79), channel_id=1, source_target_pairs={{0,24},{4,28},{8,16},{12,20},{16,8},{20,12},{24,0},{28,4},{1,25},{... | collective-permute-start | bytes 184328 | tf_op jit(solution)/shard_map/ppermute | solution.py:23
  38.0 0.6 collective-permute-start.10
  38.6 0.5 convert_add_fusion
  39.2 0.2 collective-permute-done.9
  39.4 0.1 slice.95
  39.4 0.1 slice.55
  39.6 1.8 %collective-permute-start.16 = (bf16[2,6,128,128]{3,2,1,0:T(8,128)(2,1)S(1)}, bf16[2,6,128,128]{3,2,1,0:T(8,128)(2,1)S(1)}, u32[]{:S(2)}, u32[]{:S(2)}) collective-permute-start(bf16[2,6,128,128]{3,2,1,0:T(8,128)(2,1)S(1)} %slice.95), channel_id=1, source_target_pairs={{0,16},{4,20},{8,24},{12,28},{16,0},{20,4},{24,8},{28,12},{1,17},{... | collective-permute-start | bytes 1179656 | tf_op jit(solution)/shard_map/ppermute | solution.py:23
  41.4 0.1 fusion.1
  41.4 1.2 %collective-permute-start.15 = (bf16[2,5,128,128]{3,2,1,0:T(8,128)(2,1)S(1)}, bf16[2,5,128,128]{3,2,1,0:T(8,128)(2,1)S(1)}, u32[]{:S(2)}, u32[]{:S(2)}) collective-permute-start(bf16[2,5,128,128]{3,2,1,0:T(8,128)(2,1)S(1)} %fusion.1), channel_id=1, source_target_pairs={{0,8},{4,12},{8,0},{12,4},{16,24},{20,28},{24,16},{28,20},{1,9},{5... | collective-permute-start | bytes 983048 | tf_op jit(solution)/shard_map/ppermute | solution.py:23
  42.6 0.6 collective-permute-done.10
  43.2 1.3 %collective-permute-start.14 = (bf16[240,128]{1,0:T(8,128)(2,1)S(1)}, bf16[240,128]{1,0:T(8,128)(2,1)S(1)}, u32[]{:S(2)}, u32[]{:S(2)}) collective-permute-start(bf16[240,128]{1,0:T(8,128)(2,1)S(1)} %fusion.7.refs_0_), channel_id=1, source_target_pairs={{0,1},{1,2},{2,3},{3,0},{4,5},{5,6},{6,7},{7,4},{8,9},{9,10},{10,1... | collective-permute-start | bytes 184328 | tf_op jit(solution)/shard_map/ppermute | solution.py:28
  44.6 2.6 %collective-permute-start.13 = (bf16[240,128]{1,0:T(8,128)(2,1)S(1)}, bf16[240,128]{1,0:T(8,128)(2,1)S(1)}, u32[]{:S(2)}, u32[]{:S(2)}) collective-permute-start(bf16[240,128]{1,0:T(8,128)(2,1)S(1)} %fusion.7.refs_0_), channel_id=1, source_target_pairs={{0,2},{1,3},{2,0},{3,1},{4,6},{5,7},{6,4},{7,5},{8,10},{9,11},{10,... | collective-permute-start | bytes 184328 | tf_op jit(solution)/shard_map/ppermute | solution.py:28
  47.1 1.5 %collective-permute-start.12 = (bf16[240,128]{1,0:T(8,128)(2,1)S(1)}, bf16[240,128]{1,0:T(8,128)(2,1)S(1)}, u32[]{:S(2)}, u32[]{:S(2)}) collective-permute-start(bf16[240,128]{1,0:T(8,128)(2,1)S(1)} %fusion.7.refs_0_), channel_id=1, source_target_pairs={{0,3},{1,0},{2,1},{3,2},{4,7},{5,4},{6,5},{7,6},{8,11},{9,8},{10,9... | collective-permute-start | bytes 184328 | tf_op jit(solution)/shard_map/ppermute | solution.py:28
  48.6 1.3 %collective-permute-done.14.refs_3_ = bf16[240,128]{1,0:T(8,128)(2,1)S(1)} collective-permute-done((bf16[240,128]{1,0:T(8,128)(2,1)S(1)}, bf16[240,128]{1,0:T(8,128)(2,1)S(1)}, u32[]{:S(2)}, u32[]{:S(2)}) %collective-permute-start.14) | collective-permute-done | bytes 61472 | tf_op jit(solution)/shard_map/ppermute | solution.py:28
  49.9 1.6 %collective-permute-done.13.refs_2_ = bf16[240,128]{1,0:T(8,128)(2,1)S(1)} collective-permute-done((bf16[240,128]{1,0:T(8,128)(2,1)S(1)}, bf16[240,128]{1,0:T(8,128)(2,1)S(1)}, u32[]{:S(2)}, u32[]{:S(2)}) %collective-permute-start.13) | collective-permute-done | bytes 61472 | tf_op jit(solution)/shard_map/ppermute | solution.py:28
  51.5 0.2 collective-permute-done.12.refs_1_
  51.7 0.1 convert_add_fusion.1
  51.8 0.1 fusion
  51.9 0.1 line.1
  51.9 0.0 copy-start.4
  51.9 0.0 copy-start.5
  52.0 1.5 %collective-permute-start.22 = (bf16[240,128]{1,0:T(8,128)(2,1)S(1)}, bf16[240,128]{1,0:T(8,128)(2,1)S(1)}, u32[]{:S(2)}, u32[]{:S(2)}) collective-permute-start(bf16[240,128]{1,0:T(8,128)(2,1)S(1)} %line.1), channel_id=1, source_target_pairs={{0,24},{4,28},{8,16},{12,20},{16,8},{20,12},{24,0},{28,4},{1,25},{... | collective-permute-start | bytes 184328 | tf_op jit(solution)/shard_map/ppermute | solution.py:23
  53.4 1.2 %collective-permute-start.21 = (bf16[240,128]{1,0:T(8,128)(2,1)S(1)}, bf16[240,128]{1,0:T(8,128)(2,1)S(1)}, u32[]{:S(2)}, u32[]{:S(2)}) collective-permute-start(bf16[240,128]{1,0:T(8,128)(2,1)S(1)} %line.1), channel_id=1, source_target_pairs={{0,16},{4,20},{8,24},{12,28},{16,0},{20,4},{24,8},{28,12},{1,17},{... | collective-permute-start | bytes 184328 | tf_op jit(solution)/shard_map/ppermute | solution.py:23
  54.6 0.9 %collective-permute-start.20 = (bf16[240,128]{1,0:T(8,128)(2,1)S(1)}, bf16[240,128]{1,0:T(8,128)(2,1)S(1)}, u32[]{:S(2)}, u32[]{:S(2)}) collective-permute-start(bf16[240,128]{1,0:T(8,128)(2,1)S(1)} %line.1), channel_id=1, source_target_pairs={{0,8},{4,12},{8,0},{12,4},{16,24},{20,28},{24,16},{28,20},{1,9},{5... | collective-permute-start | bytes 184328 | tf_op jit(solution)/shard_map/ppermute | solution.py:23
  55.5 0.5 collective-permute-start.18
  56.1 1.6 %collective-permute-start.19 = (bf16[6,128,128]{2,1,0:T(8,128)(2,1)S(1)}, bf16[6,128,128]{2,1,0:T(8,128)(2,1)S(1)}, u32[]{:S(2)}, u32[]{:S(2)}) collective-permute-start(bf16[6,128,128]{2,1,0:T(8,128)(2,1)S(1)} %fusion.2), channel_id=1, source_target_pairs={{0,8},{4,12},{8,0},{12,4},{16,24},{20,28},{24,16},{28,20},{1,9},{5... | collective-permute-start | bytes 589832 | tf_op jit(solution)/shard_map/ppermute | solution.py:23
  57.7 3.8 %collective-permute-start.24 = (bf16[11,128,128]{2,1,0:T(8,128)(2,1)S(1)}, bf16[11,128,128]{2,1,0:T(8,128)(2,1)S(1)}, u32[]{:S(2)}, u32[]{:S(2)}) collective-permute-start(bf16[11,128,128]{2,1,0:T(8,128)(2,1)S(1)} %get-tuple-element.63), channel_id=1, source_target_pairs={{0,2},{3,1},{4,6},{7,5},{8,10},{11,9},{12,14},{15,13},{16,18},{19,... | collective-permute-start | bytes 1081352 | tf_op jit(solution)/shard_map/ppermute | solution.py:294
  61.6 0.1 collective-permute-start.23
  61.7 0.0 copy-start.7
  61.7 0.0 copy-start.8
  61.7 0.1 collective-permute-done.19
  61.9 1.3 %collective-permute-done.23.far = bf16[4,240,128]{2,1,0:T(8,128)(2,1)S(1)} collective-permute-done((bf16[4,240,128]{2,1,0:T(8,128)(2,1)S(1)}, bf16[4,240,128]{2,1,0:T(8,128)(2,1)S(1)}, u32[]{:S(2)}, u32[]{:S(2)}) %collective-permute-start.23) | collective-permute-done | bytes 245792 | tf_op jit(solution)/shard_map/ppermute | solution.py:23
  63.1 2.1 %blocks.1 = (f32[3,128,128]{2,1,0:T(8,128)}, f32[8,128,128]{2,1,0:T(8,128)}, f32[8,128,128]{2,1,0:T(8,128)}) custom-call(s32[8]{0:T(128)S(1)} %copy-done.6, bf16[4,240,128]{2,1,0:T(8,128)(2,1)S(1)} %pad_maximum_fusion.near, bf16[4,240,128]{2,1,0:T(8,128)(2,1)S(1)} %collective-permute-done.23.far, f32[3,128,128]{2,1,0:T(8,128)S(1)} %copy-done.5, ...), custom_call_target="tpu_custom_call" | custom-call | tf_op jit(solution)/shard_map/blocks/pallas_call | solution.py:41
  65.3 1.9 %collective-permute-done.24.refs_1_ = bf16[11,128,128]{2,1,0:T(8,128)(2,1)S(1)} collective-permute-done((bf16[11,128,128]{2,1,0:T(8,128)(2,1)S(1)}, bf16[11,128,128]{2,1,0:T(8,128)(2,1)S(1)}, u32[]{:S(2)}, u32[]{:S(2)}) %collective-permute-start.24) | collective-permute-done | bytes 360480 | tf_op jit(solution)/shard_map/ppermute | solution.py:294
  67.1 1.5 %columns.1 = (bf16[3,128,128]{2,1,0:T(8,128)(2,1)}, bf16[8,128,128]{2,1,0:T(8,128)(2,1)}) custom-call(s32[8]{0:T(128)S(1)} %copy-done.6, s32[3]{0:T(128)S(1)} %bitcast.49, s32[8]{0:T(128)S(1)} %bitcast.51, bf16[8,128,128]{2,1,0:T(8,128)(2,1)S(1)} %copy-done.2, f32[11,128,128]{2,1,0:T(8,128)S(1)} %get-tuple-element.39.own, ...), custom_call_target="tpu_custom_call" | custom-call | tf_op jit(solution)/shard_map/columns/pallas_call | solution.py:41
  (28 shorter events, 0.3 us)
Async XLA Ops:
  2.4 14.8 %collective-permute-start.5 = (bf16[11,128,128]{2,1,0:T(8,128)(2,1)}, bf16[11,128,128]{2,1,0:T(8,128)(2,1)S(1)}, u32[]{:S(2)}, u32[]{:S(2)}) collective-permute-start(bf16[11,128,128]{2,1,0:T(8,128)(2,1)} %mask.1.refs_0_.own), channel_id=1, source_target_pairs={{2,0},{1,3},{6,4},{5,7},{10,8},{9,11},{14,12},{13,15},{18,16},{17,... | collective-permute-start | bytes 1081352 | tf_op jit(solution)/shard_map/ppermute | solution.py:290
  3.7 20.4 %collective-permute-start.4 = (bf16[11,128,128]{2,1,0:T(8,128)(2,1)}, bf16[11,128,128]{2,1,0:T(8,128)(2,1)S(1)}, u32[]{:S(2)}, u32[]{:S(2)}) collective-permute-start(bf16[11,128,128]{2,1,0:T(8,128)(2,1)} %mask.1.refs_0_.own), channel_id=1, source_target_pairs={{1,0},{2,1},{3,2},{0,3},{5,4},{6,5},{7,6},{4,7},{9,8},{10,9},{11,1... | collective-permute-start | bytes 1081352 | tf_op jit(solution)/shard_map/ppermute | solution.py:290
  8.8 16.6 %collective-permute-start.3 = (bf16[11,128,128]{2,1,0:T(8,128)(2,1)}, bf16[11,128,128]{2,1,0:T(8,128)(2,1)S(1)}, u32[]{:S(2)}, u32[]{:S(2)}) collective-permute-start(bf16[11,128,128]{2,1,0:T(8,128)(2,1)} %mask.1.refs_0_.own), channel_id=1, source_target_pairs={{0,24},{4,28},{8,16},{12,20},{16,8},{20,12},{24,0},{28,4},{1,25},{... | collective-permute-start | bytes 1081352 | tf_op jit(solution)/shard_map/ppermute | solution.py:23
  11.3 16.3 %collective-permute-start.2 = (bf16[11,128,128]{2,1,0:T(8,128)(2,1)}, bf16[11,128,128]{2,1,0:T(8,128)(2,1)S(1)}, u32[]{:S(2)}, u32[]{:S(2)}) collective-permute-start(bf16[11,128,128]{2,1,0:T(8,128)(2,1)} %mask.1.refs_0_.own), channel_id=1, source_target_pairs={{0,16},{4,20},{8,24},{12,28},{16,0},{20,4},{24,8},{28,12},{1,17},{... | collective-permute-start | bytes 1081352 | tf_op jit(solution)/shard_map/ppermute | solution.py:23
  11.8 15.9 %collective-permute-start.1 = (bf16[11,128,128]{2,1,0:T(8,128)(2,1)}, bf16[11,128,128]{2,1,0:T(8,128)(2,1)S(1)}, u32[]{:S(2)}, u32[]{:S(2)}) collective-permute-start(bf16[11,128,128]{2,1,0:T(8,128)(2,1)} %mask.1.refs_0_.own), channel_id=1, source_target_pairs={{0,8},{4,12},{8,0},{12,4},{16,24},{20,28},{24,16},{28,20},{1,9},{5... | collective-permute-start | bytes 1081352 | tf_op jit(solution)/shard_map/ppermute | solution.py:23
  17.2 10.4 %collective-permute-start = (bf16[11,128,128]{2,1,0:T(8,128)(2,1)}, bf16[11,128,128]{2,1,0:T(8,128)(2,1)S(1)}, u32[]{:S(2)}, u32[]{:S(2)}) collective-permute-start(bf16[11,128,128]{2,1,0:T(8,128)(2,1)} %mask.1.refs_0_.own), channel_id=1, source_target_pairs={{0,4},{4,0},{8,12},{12,8},{16,20},{20,16},{24,28},{28,24},{1,5},{5... | collective-permute-start | bytes 1081352 | tf_op jit(solution)/shard_map/ppermute | solution.py:23
  24.1 1.0 %copy-start = (bf16[11,128,128]{2,1,0:T(8,128)(2,1)S(1)}, bf16[11,128,128]{2,1,0:T(8,128)(2,1)}, u32[]{:S(2)}) copy-start(bf16[11,128,128]{2,1,0:T(8,128)(2,1)} %mask.1.refs_0_.own) | copy-start | bytes 1081348
  25.4 2.4 %copy-start.2 = (bf16[8,128,128]{2,1,0:T(8,128)(2,1)S(1)}, bf16[8,128,128]{2,1,0:T(8,128)(2,1)}, u32[]{:S(2)}) copy-start(bf16[8,128,128]{2,1,0:T(8,128)(2,1)} %panel.5) | copy-start | bytes 786436
  25.4 2.4 %copy-start.3 = (bf16[1,4,8,1,128,128]{5,4,3,2,1,0:T(8,128)(2,1)S(1)}, bf16[1,4,8,1,128,128]{5,4,3,2,1,0:T(8,128)(2,1)}, u32[]{:S(2)}) copy-start(bf16[1,4,8,1,128,128]{5,4,3,2,1,0:T(8,128)(2,1)} %param.9) | copy-start | bytes 3145732
  27.7 2.0 %copy-start.1 = (bf16[11,128,128]{2,1,0:T(8,128)(2,1)S(1)}, bf16[11,128,128]{2,1,0:T(8,128)(2,1)}, u32[]{:S(2)}) copy-start(bf16[11,128,128]{2,1,0:T(8,128)(2,1)} %mask.1.refs_0_.own) | copy-start | bytes 1081348
  27.7 2.8 %collective-permute-start.6 = (bf16[3,11,128,128]{3,2,1,0:T(8,128)(2,1)S(1)}, bf16[3,11,128,128]{3,2,1,0:T(8,128)(2,1)S(1)}, u32[]{:S(2)}, u32[]{:S(2)}) collective-permute-start(bf16[3,11,128,128]{3,2,1,0:T(8,128)(2,1)S(1)} %stack.21.near), channel_id=1, source_target_pairs={{0,4},{4,0},{8,12},{12,8},{16,20},{20,16},{24,28},{28,24},{1,5},{5... | collective-permute-start | bytes 3244040 | tf_op jit(solution)/shard_map/ppermute | solution.py:23
  29.2 5.4 %collective-permute-start.8 = (bf16[4,11,128,128]{3,2,1,0:T(8,128)(2,1)S(1)}, bf16[4,11,128,128]{3,2,1,0:T(8,128)(2,1)S(1)}, u32[]{:S(2)}, u32[]{:S(2)}) collective-permute-start(bf16[4,11,128,128]{3,2,1,0:T(8,128)(2,1)S(1)} %get-tuple-element.43), channel_id=1, source_target_pairs={{0,4},{4,0},{8,12},{12,8},{16,20},{20,16},{24,28},{28,24},{1,5},{5... | collective-permute-start | bytes 4325384 | tf_op jit(solution)/shard_map/ppermute | solution.py:23
  29.7 0.8 %copy-start.6 = (s32[8]{0:T(128)S(1)}, s32[8]{0:T(128)}, u32[]{:S(2)}) copy-start(s32[8]{0:T(128)} %parents.5) | copy-start | bytes 100
  33.1 1.9 %collective-permute-start.7 = (f32[4,240,128]{2,1,0:T(8,128)S(1)}, f32[4,240,128]{2,1,0:T(8,128)S(1)}, u32[]{:S(2)}, u32[]{:S(2)}) collective-permute-start(f32[4,240,128]{2,1,0:T(8,128)S(1)} %get-tuple-element.41), channel_id=1, source_target_pairs={{0,4},{4,0},{8,12},{12,8},{16,20},{20,16},{24,28},{28,24},{1,5},{5... | collective-permute-start | bytes 1474568 | tf_op jit(solution)/shard_map/ppermute | solution.py:23
  33.3 13.9 %collective-permute-start.17 = (bf16[11,128,128]{2,1,0:T(8,128)(2,1)S(1)}, bf16[11,128,128]{2,1,0:T(8,128)(2,1)S(1)}, u32[]{:S(2)}, u32[]{:S(2)}) collective-permute-start(bf16[11,128,128]{2,1,0:T(8,128)(2,1)S(1)} %get-tuple-element.49), channel_id=1, source_target_pairs={{0,1},{1,2},{2,3},{3,0},{4,5},{5,6},{6,7},{7,4},{8,9},{9,10},{10,1... | collective-permute-start | bytes 1081352 | tf_op jit(solution)/shard_map/ppermute | solution.py:294
  35.1 4.3 %collective-permute-start.9 = (bf16[240,128]{1,0:T(8,128)(2,1)S(1)}, bf16[240,128]{1,0:T(8,128)(2,1)S(1)}, u32[]{:S(2)}, u32[]{:S(2)}) collective-permute-start(bf16[240,128]{1,0:T(8,128)(2,1)S(1)} %get-tuple-element.78), channel_id=1, source_target_pairs={{0,8},{4,12},{8,0},{12,4},{16,24},{20,28},{24,16},{28,20},{1,9},{5... | collective-permute-start | bytes 184328 | tf_op jit(solution)/shard_map/ppermute | solution.py:23
  36.7 6.0 %collective-permute-start.11 = (bf16[240,128]{1,0:T(8,128)(2,1)S(1)}, bf16[240,128]{1,0:T(8,128)(2,1)S(1)}, u32[]{:S(2)}, u32[]{:S(2)}) collective-permute-start(bf16[240,128]{1,0:T(8,128)(2,1)S(1)} %get-tuple-element.79), channel_id=1, source_target_pairs={{0,24},{4,28},{8,16},{12,20},{16,8},{20,12},{24,0},{28,4},{1,25},{... | collective-permute-start | bytes 184328 | tf_op jit(solution)/shard_map/ppermute | solution.py:23
  38.0 5.1 %collective-permute-start.10 = (bf16[240,128]{1,0:T(8,128)(2,1)S(1)}, bf16[240,128]{1,0:T(8,128)(2,1)S(1)}, u32[]{:S(2)}, u32[]{:S(2)}) collective-permute-start(bf16[240,128]{1,0:T(8,128)(2,1)S(1)} %get-tuple-element.80), channel_id=1, source_target_pairs={{0,16},{4,20},{8,24},{12,28},{16,0},{20,4},{24,8},{28,12},{1,17},{... | collective-permute-start | bytes 184328 | tf_op jit(solution)/shard_map/ppermute | solution.py:23
  39.6 12.1 %collective-permute-start.16 = (bf16[2,6,128,128]{3,2,1,0:T(8,128)(2,1)S(1)}, bf16[2,6,128,128]{3,2,1,0:T(8,128)(2,1)S(1)}, u32[]{:S(2)}, u32[]{:S(2)}) collective-permute-start(bf16[2,6,128,128]{3,2,1,0:T(8,128)(2,1)S(1)} %slice.95), channel_id=1, source_target_pairs={{0,16},{4,20},{8,24},{12,28},{16,0},{20,4},{24,8},{28,12},{1,17},{... | collective-permute-start | bytes 1179656 | tf_op jit(solution)/shard_map/ppermute | solution.py:23
  41.4 10.3 %collective-permute-start.15 = (bf16[2,5,128,128]{3,2,1,0:T(8,128)(2,1)S(1)}, bf16[2,5,128,128]{3,2,1,0:T(8,128)(2,1)S(1)}, u32[]{:S(2)}, u32[]{:S(2)}) collective-permute-start(bf16[2,5,128,128]{3,2,1,0:T(8,128)(2,1)S(1)} %fusion.1), channel_id=1, source_target_pairs={{0,8},{4,12},{8,0},{12,4},{16,24},{20,28},{24,16},{28,20},{1,9},{5... | collective-permute-start | bytes 983048 | tf_op jit(solution)/shard_map/ppermute | solution.py:23
  43.2 6.7 %collective-permute-start.14 = (bf16[240,128]{1,0:T(8,128)(2,1)S(1)}, bf16[240,128]{1,0:T(8,128)(2,1)S(1)}, u32[]{:S(2)}, u32[]{:S(2)}) collective-permute-start(bf16[240,128]{1,0:T(8,128)(2,1)S(1)} %fusion.7.refs_0_), channel_id=1, source_target_pairs={{0,1},{1,2},{2,3},{3,0},{4,5},{5,6},{6,7},{7,4},{8,9},{9,10},{10,1... | collective-permute-start | bytes 184328 | tf_op jit(solution)/shard_map/ppermute | solution.py:28
  44.6 7.0 %collective-permute-start.13 = (bf16[240,128]{1,0:T(8,128)(2,1)S(1)}, bf16[240,128]{1,0:T(8,128)(2,1)S(1)}, u32[]{:S(2)}, u32[]{:S(2)}) collective-permute-start(bf16[240,128]{1,0:T(8,128)(2,1)S(1)} %fusion.7.refs_0_), channel_id=1, source_target_pairs={{0,2},{1,3},{2,0},{3,1},{4,6},{5,7},{6,4},{7,5},{8,10},{9,11},{10,... | collective-permute-start | bytes 184328 | tf_op jit(solution)/shard_map/ppermute | solution.py:28
  47.1 4.6 %collective-permute-start.12 = (bf16[240,128]{1,0:T(8,128)(2,1)S(1)}, bf16[240,128]{1,0:T(8,128)(2,1)S(1)}, u32[]{:S(2)}, u32[]{:S(2)}) collective-permute-start(bf16[240,128]{1,0:T(8,128)(2,1)S(1)} %fusion.7.refs_0_), channel_id=1, source_target_pairs={{0,3},{1,0},{2,1},{3,2},{4,7},{5,4},{6,5},{7,6},{8,11},{9,8},{10,9... | collective-permute-start | bytes 184328 | tf_op jit(solution)/shard_map/ppermute | solution.py:28
  51.9 11.2 %copy-start.4 = (f32[8,128,128]{2,1,0:T(8,128)S(1)}, f32[8,128,128]{2,1,0:T(8,128)}, u32[]{:S(2)}) copy-start(f32[8,128,128]{2,1,0:T(8,128)} %lower_diagonal.1) | copy-start | bytes 1572868
  51.9 11.2 %copy-start.5 = (f32[3,128,128]{2,1,0:T(8,128)S(1)}, f32[3,128,128]{2,1,0:T(8,128)}, u32[]{:S(2)}) copy-start(f32[3,128,128]{2,1,0:T(8,128)} %upper_diagonal.1) | copy-start | bytes 589828
  52.0 5.7 %collective-permute-start.22 = (bf16[240,128]{1,0:T(8,128)(2,1)S(1)}, bf16[240,128]{1,0:T(8,128)(2,1)S(1)}, u32[]{:S(2)}, u32[]{:S(2)}) collective-permute-start(bf16[240,128]{1,0:T(8,128)(2,1)S(1)} %line.1), channel_id=1, source_target_pairs={{0,24},{4,28},{8,16},{12,20},{16,8},{20,12},{24,0},{28,4},{1,25},{... | collective-permute-start | bytes 184328 | tf_op jit(solution)/shard_map/ppermute | solution.py:23
  53.4 8.1 %collective-permute-start.21 = (bf16[240,128]{1,0:T(8,128)(2,1)S(1)}, bf16[240,128]{1,0:T(8,128)(2,1)S(1)}, u32[]{:S(2)}, u32[]{:S(2)}) collective-permute-start(bf16[240,128]{1,0:T(8,128)(2,1)S(1)} %line.1), channel_id=1, source_target_pairs={{0,16},{4,20},{8,24},{12,28},{16,0},{20,4},{24,8},{28,12},{1,17},{... | collective-permute-start | bytes 184328 | tf_op jit(solution)/shard_map/ppermute | solution.py:23
  54.6 6.9 %collective-permute-start.20 = (bf16[240,128]{1,0:T(8,128)(2,1)S(1)}, bf16[240,128]{1,0:T(8,128)(2,1)S(1)}, u32[]{:S(2)}, u32[]{:S(2)}) collective-permute-start(bf16[240,128]{1,0:T(8,128)(2,1)S(1)} %line.1), channel_id=1, source_target_pairs={{0,8},{4,12},{8,0},{12,4},{16,24},{20,28},{24,16},{28,20},{1,9},{5... | collective-permute-start | bytes 184328 | tf_op jit(solution)/shard_map/ppermute | solution.py:23
  55.5 6.1 %collective-permute-start.18 = (bf16[5,128,128]{2,1,0:T(8,128)(2,1)S(1)}, bf16[5,128,128]{2,1,0:T(8,128)(2,1)S(1)}, u32[]{:S(2)}, u32[]{:S(2)}) collective-permute-start(bf16[5,128,128]{2,1,0:T(8,128)(2,1)S(1)} %fusion.3), channel_id=1, source_target_pairs={{0,16},{4,20},{8,24},{12,28},{16,0},{20,4},{24,8},{28,12},{1,17},{... | collective-permute-start | bytes 491528 | tf_op jit(solution)/shard_map/ppermute | solution.py:23
  56.1 5.7 %collective-permute-start.19 = (bf16[6,128,128]{2,1,0:T(8,128)(2,1)S(1)}, bf16[6,128,128]{2,1,0:T(8,128)(2,1)S(1)}, u32[]{:S(2)}, u32[]{:S(2)}) collective-permute-start(bf16[6,128,128]{2,1,0:T(8,128)(2,1)S(1)} %fusion.2), channel_id=1, source_target_pairs={{0,8},{4,12},{8,0},{12,4},{16,24},{20,28},{24,16},{28,20},{1,9},{5... | collective-permute-start | bytes 589832 | tf_op jit(solution)/shard_map/ppermute | solution.py:23
  57.7 9.5 %collective-permute-start.24 = (bf16[11,128,128]{2,1,0:T(8,128)(2,1)S(1)}, bf16[11,128,128]{2,1,0:T(8,128)(2,1)S(1)}, u32[]{:S(2)}, u32[]{:S(2)}) collective-permute-start(bf16[11,128,128]{2,1,0:T(8,128)(2,1)S(1)} %get-tuple-element.63), channel_id=1, source_target_pairs={{0,2},{3,1},{4,6},{7,5},{8,10},{11,9},{12,14},{15,13},{16,18},{19,... | collective-permute-start | bytes 1081352 | tf_op jit(solution)/shard_map/ppermute | solution.py:294
  61.6 1.6 %collective-permute-start.23 = (bf16[4,240,128]{2,1,0:T(8,128)(2,1)S(1)}, bf16[4,240,128]{2,1,0:T(8,128)(2,1)S(1)}, u32[]{:S(2)}, u32[]{:S(2)}) collective-permute-start(bf16[4,240,128]{2,1,0:T(8,128)(2,1)S(1)} %pad_maximum_fusion.near), channel_id=1, source_target_pairs={{0,4},{4,0},{8,12},{12,8},{16,20},{20,16},{24,28},{28,24},{1,5},{5... | collective-permute-start | bytes 737288 | tf_op jit(solution)/shard_map/ppermute | solution.py:23
  61.7 5.4 %copy-start.7 = (s32[3,1,1]{0,2,1:T(1,128)S(1)}, s32[3,1,1]{0,2,1:T(1,128)}, u32[]{:S(2)}) copy-start(s32[3,1,1]{0,2,1:T(1,128)} %param.11) | copy-start | bytes 40
  61.7 5.4 %copy-start.8 = (s32[8,1,1]{0,2,1:T(1,128)S(1)}, s32[8,1,1]{0,2,1:T(1,128)}, u32[]{:S(2)}) copy-start(s32[8,1,1]{0,2,1:T(1,128)} %param.14) | copy-start | bytes 100

commit v6 on v5

--- a/solution.py
+++ b/solution.py
@@ -419,7 +419,7 @@
     for piece in pieces:
         part = part + piece.astype(F32)
     part = part.astype(WIRE)
-    early = [return_pair(returns[o - 1], "col", o) for o in range(1, reach)]
+    early = [return_pair(returns[o - 1], "col", o) for o in range(2, reach + 1)]
     parts = gather_shifts(part, "col")
     tied = tie(*parts, *[got for _, got in halves], *early)
     early = tied[depth + 2 :]
@@ -432,11 +432,11 @@
         [shape_of((depth, chunk, block), F32)],
     )
     sides = [keep + got.astype(F32) for (keep, _), got in zip(halves, tied[depth : depth + 2])]
-    part, last, *sides = tie(part, returns[-1], *sides)
+    part, last, *sides = tie(part, returns[0], *sides)
     nears = gather_near(part, "row")
     near = jnp.stack(nears)
     far = flip(near, "row", 1)
-    got = [*early, return_pair(last, "col", reach)]
+    got = [*early, return_pair(last, "col", 1)]
     front, back = sides
     for i in range(1, len(bits)):
         keep, across = halve(front, "row", bits[i], bits[i:])

time: 68.9 us -> 71.3 us (1.035)
  waiting for transfers between devices: 21.6 us -> 25.5 us
  starting transfers between devices: 33.4 us -> 31.9 us
    ppermute x18, waiting for transfers between devices: 4.87 us -> 6.99 us  [flip(): return lax.ppermute(value, axis, [(i, i ^ mask) for i in range(size)])]
    ppermute x2, waiting for transfers between devices: 1.85 us -> 3.35 us  [return_pair(): return lax.ppermute(value, axis, pairs(lax.axis_size(axis), offset))]
    ppermute x3, starting transfers between devices: 5.36 us -> 3.87 us  [shift(): lax.ppermute(value, axis, [(i, (i + step) % size) for i in range(size)])]
where the time goes in v6:
time: 71.3 us; the launch traced here: 71.1 us
  starting transfers between devices  31.9 us (45%)
  waiting for transfers between devices  25.5 us (36%)
  Pallas kernels  10.6 us (15%)
  local copies, waits for them, and re-layouts  1.32 us (2%)
  between operations  0.96 us (1%)
  other arithmetic  0.85 us (1%)
    ppermute x18, starting transfers between devices, flip(): return lax.ppermute(value, axis, [(i, i ^ mask) for i in range(size)])  16.3 us
    ppermute x2, waiting for transfers between devices, gather_pair(): lax.ppermute(value, axis, [(b, c) for c, b in pairs(lax.axis_size(axis),...  11.8 us
    pallas_call x10, Pallas kernels, call(): pl.pallas_call(kernel, out_shape=outs, in_specs=[SMEM] * len(scalars) + [...  10.6 us
    ppermute x18, waiting for transfers between devices, flip(): return lax.ppermute(value, axis, [(i, i ^ mask) for i in range(size)])  6.99 us
    ppermute x2, starting transfers between devices, gather_pair(): lax.ppermute(value, axis, [(b, c) for c, b in pairs(lax.axis_size(axis),...  6.38 us
    ppermute x2, starting transfers between devices, return_pair(): return lax.ppermute(value, axis, pairs(lax.axis_size(axis), offset))  5.3 us
    ppermute x3, starting transfers between devices, shift(): lax.ppermute(value, axis, [(i, (i + step) % size) for i in range(size)])  3.87 us
    ppermute x3, waiting for transfers between devices, shift(): lax.ppermute(value, axis, [(i, (i + step) % size) for i in range(size)])  3.42 us
  transfers between devices with their start and end apart: 25, of which 13 were waited for; matrix products, arithmetic and copies ran while one was open for 1% of the time, Pallas kernels for 10%

profile of v6, /device:TPU:0, one launch (start us, length us, event | category | flops | bytes accessed | tf_op | source)
XLA Modules:
  0.0 71.1 jit_solution(17046411226629008)
XLA Ops:
  0.6 1.8 %mask.1.refs_0_.own = bf16[11,128,128]{2,1,0:T(8,128)(2,1)} custom-call(s32[3]{0:T(128)} %bitcast.48, s32[8]{0:T(128)} %bitcast.50, bf16[3,128,128]{2,1,0:T(8,128)(2,1)} %bitcast.55, bf16[8,128,128]{2,1,0:T(8,128)(2,1)} %bitcast.54), custom_call_target="tpu_custom_call" | custom-call | tf_op jit(solution)/shard_map/mask/pallas_call | solution.py:41
  2.4 1.3 %collective-permute-start.5 = (bf16[11,128,128]{2,1,0:T(8,128)(2,1)}, bf16[11,128,128]{2,1,0:T(8,128)(2,1)S(1)}, u32[]{:S(2)}, u32[]{:S(2)}) collective-permute-start(bf16[11,128,128]{2,1,0:T(8,128)(2,1)} %mask.1.refs_0_.own), channel_id=1, source_target_pairs={{2,0},{1,3},{6,4},{5,7},{10,8},{9,11},{14,12},{13,15},{18,16},{17,... | collective-permute-start | bytes 1081352 | tf_op jit(solution)/shard_map/ppermute | solution.py:290
  3.7 5.1 %collective-permute-start.4 = (bf16[11,128,128]{2,1,0:T(8,128)(2,1)}, bf16[11,128,128]{2,1,0:T(8,128)(2,1)S(1)}, u32[]{:S(2)}, u32[]{:S(2)}) collective-permute-start(bf16[11,128,128]{2,1,0:T(8,128)(2,1)} %mask.1.refs_0_.own), channel_id=1, source_target_pairs={{1,0},{2,1},{3,2},{0,3},{5,4},{6,5},{7,6},{4,7},{9,8},{10,9},{11,1... | collective-permute-start | bytes 1081352 | tf_op jit(solution)/shard_map/ppermute | solution.py:290
  8.8 2.4 %collective-permute-start.3 = (bf16[11,128,128]{2,1,0:T(8,128)(2,1)}, bf16[11,128,128]{2,1,0:T(8,128)(2,1)S(1)}, u32[]{:S(2)}, u32[]{:S(2)}) collective-permute-start(bf16[11,128,128]{2,1,0:T(8,128)(2,1)} %mask.1.refs_0_.own), channel_id=1, source_target_pairs={{0,24},{4,28},{8,16},{12,20},{16,8},{20,12},{24,0},{28,4},{1,25},{... | collective-permute-start | bytes 1081352 | tf_op jit(solution)/shard_map/ppermute | solution.py:23
  11.3 0.5 collective-permute-start.2
  11.8 0.5 collective-permute-start.1
  12.3 4.9 %collective-permute-done.5.refs_2_.refs_1_ = bf16[11,128,128]{2,1,0:T(8,128)(2,1)S(1)} collective-permute-done((bf16[11,128,128]{2,1,0:T(8,128)(2,1)}, bf16[11,128,128]{2,1,0:T(8,128)(2,1)S(1)}, u32[]{:S(2)}, u32[]{:S(2)}) %collective-permute-start.5) | collective-permute-done | bytes 360480 | tf_op jit(solution)/shard_map/ppermute | solution.py:290
  17.2 0.0 collective-permute-start
  17.2 6.8 %collective-permute-done.4.refs_1_.refs_0_ = bf16[11,128,128]{2,1,0:T(8,128)(2,1)S(1)} collective-permute-done((bf16[11,128,128]{2,1,0:T(8,128)(2,1)}, bf16[11,128,128]{2,1,0:T(8,128)(2,1)S(1)}, u32[]{:S(2)}, u32[]{:S(2)}) %collective-permute-start.4) | collective-permute-done | bytes 360480 | tf_op jit(solution)/shard_map/ppermute | solution.py:290
  24.1 1.0 %copy-done = bf16[11,128,128]{2,1,0:T(8,128)(2,1)S(1)} copy-done((bf16[11,128,128]{2,1,0:T(8,128)(2,1)S(1)}, bf16[11,128,128]{2,1,0:T(8,128)(2,1)}, u32[]{:S(2)}) %copy-start) | copy-done | bytes 360472
  25.1 0.3 turn.1.refs_3_.turned
  25.4 0.0 copy-start.2
  25.4 0.0 copy-start.3
  25.4 2.1 %collective-permute-done.2.refs_1_ = bf16[11,128,128]{2,1,0:T(8,128)(2,1)S(1)} collective-permute-done((bf16[11,128,128]{2,1,0:T(8,128)(2,1)}, bf16[11,128,128]{2,1,0:T(8,128)(2,1)S(1)}, u32[]{:S(2)}, u32[]{:S(2)}) %collective-permute-start.2) | collective-permute-done | bytes 360480 | tf_op jit(solution)/shard_map/ppermute | solution.py:23
  27.5 0.1 collective-permute-done.1.refs_0_
  27.6 0.1 stack.21.near
  27.7 0.0 copy-start.1
  27.7 0.1 collective-permute-start.6
  27.8 0.4 top.1
  28.2 1.0 %partial.1 = (f32[4,11,128,128]{3,2,1,0:T(8,128)S(1)}, bf16[4,11,128,128]{3,2,1,0:T(8,128)(2,1)S(1)}) custom-call(bf16[1024,256]{1,0:T(8,128)(2,1)S(1)} %get-tuple-element.42.top, bf16[11,128,128]{2,1,0:T(8,128)(2,1)S(1)} %collective-permute-done.4.refs_1_.refs_0_, bf16[11,128,128]{2,1,0:T(8,128)(2,1)S(1)} %collective-permute-done.5.refs_2_.refs_1_), custom_call_target="tpu_custom_call" | custom-call | tf_op jit(solution)/shard_map/partial/pallas_call | solution.py:41
  29.2 0.5 collective-permute-start.8
  29.7 0.8 %first.1.start = f32[6,384,256]{2,1,0:T(8,128)S(1)} custom-call(bf16[2,384,512]{2,1,0:T(8,128)(2,1)S(1)} %get-tuple-element.38.top, bf16[11,128,128]{2,1,0:T(8,128)(2,1)S(1)} %copy-done.1, bf16[3,11,128,128]{3,2,1,0:T(8,128)(2,1)S(1)} %stack.21.near), custom_call_target="tpu_custom_call" | custom-call | tf_op jit(solution)/shard_map/first/pallas_call | solution.py:41
  30.5 2.5 %second.1 = (f32[11,128,128]{2,1,0:T(8,128)S(1)}, bf16[11,128,128]{2,1,0:T(8,128)(2,1)S(1)}, bf16[11,128,128]{2,1,0:T(8,128)(2,1)S(1)}, f32[4,240,128]{2,1,0:T(8,128)S(1)}, f32[4,240,128]{2,1,0:T(8,128)S(1)}) custom-call(s32[8]{0:T(128)S(1)} %copy-done.6, bf16[2,384,512]{2,1,0:T(8,128)(2,1)S(1)} %get-tuple-element.38.top, ...), custom_call_target="tpu_custom_call" | custom-call | tf_op jit(solution)/shard_map/second/pallas_call | solution.py:41
  33.1 0.2 collective-permute-start.7
  33.3 4.3 %collective-permute-start.17 = (bf16[11,128,128]{2,1,0:T(8,128)(2,1)S(1)}, bf16[11,128,128]{2,1,0:T(8,128)(2,1)S(1)}, u32[]{:S(2)}, u32[]{:S(2)}) collective-permute-start(bf16[11,128,128]{2,1,0:T(8,128)(2,1)S(1)} %get-tuple-element.49), channel_id=1, source_target_pairs={{0,2},{3,1},{4,6},{7,5},{8,10},{11,9},{12,14},{15,13},{16,18},{19,... | collective-permute-start | bytes 1081352 | tf_op jit(solution)/shard_map/ppermute | solution.py:294
  37.5 0.0 collective-permute-done.8
  37.6 0.1 fusion.8
  37.7 1.6 %collective-permute-start.9 = (bf16[240,128]{1,0:T(8,128)(2,1)S(1)}, bf16[240,128]{1,0:T(8,128)(2,1)S(1)}, u32[]{:S(2)}, u32[]{:S(2)}) collective-permute-start(bf16[240,128]{1,0:T(8,128)(2,1)S(1)} %get-tuple-element.78), channel_id=1, source_target_pairs={{0,8},{4,12},{8,0},{12,4},{16,24},{20,28},{24,16},{28,20},{1,9},{5... | collective-permute-start | bytes 184328 | tf_op jit(solution)/shard_map/ppermute | solution.py:23
  39.3 1.4 %collective-permute-start.11 = (bf16[240,128]{1,0:T(8,128)(2,1)S(1)}, bf16[240,128]{1,0:T(8,128)(2,1)S(1)}, u32[]{:S(2)}, u32[]{:S(2)}) collective-permute-start(bf16[240,128]{1,0:T(8,128)(2,1)S(1)} %get-tuple-element.79), channel_id=1, source_target_pairs={{0,24},{4,28},{8,16},{12,20},{16,8},{20,12},{24,0},{28,4},{1,25},{... | collective-permute-start | bytes 184328 | tf_op jit(solution)/shard_map/ppermute | solution.py:23
  40.6 0.6 collective-permute-start.10
  41.2 0.5 convert_add_fusion
  41.7 0.4 collective-permute-done.9
  42.1 0.1 slice.95
  42.2 0.1 slice.55
  42.3 1.7 %collective-permute-start.16 = (bf16[2,6,128,128]{3,2,1,0:T(8,128)(2,1)S(1)}, bf16[2,6,128,128]{3,2,1,0:T(8,128)(2,1)S(1)}, u32[]{:S(2)}, u32[]{:S(2)}) collective-permute-start(bf16[2,6,128,128]{3,2,1,0:T(8,128)(2,1)S(1)} %slice.95), channel_id=1, source_target_pairs={{0,16},{4,20},{8,24},{12,28},{16,0},{20,4},{24,8},{28,12},{1,17},{... | collective-permute-start | bytes 1179656 | tf_op jit(solution)/shard_map/ppermute | solution.py:23
  44.0 0.1 fusion.1
  44.0 1.0 %collective-permute-start.15 = (bf16[2,5,128,128]{3,2,1,0:T(8,128)(2,1)S(1)}, bf16[2,5,128,128]{3,2,1,0:T(8,128)(2,1)S(1)}, u32[]{:S(2)}, u32[]{:S(2)}) collective-permute-start(bf16[2,5,128,128]{3,2,1,0:T(8,128)(2,1)S(1)} %fusion.1), channel_id=1, source_target_pairs={{0,8},{4,12},{8,0},{12,4},{16,24},{20,28},{24,16},{28,20},{1,9},{5... | collective-permute-start | bytes 983048 | tf_op jit(solution)/shard_map/ppermute | solution.py:23
  45.0 0.8 %collective-permute-done.10 = bf16[240,128]{1,0:T(8,128)(2,1)S(1)} collective-permute-done((bf16[240,128]{1,0:T(8,128)(2,1)S(1)}, bf16[240,128]{1,0:T(8,128)(2,1)S(1)}, u32[]{:S(2)}, u32[]{:S(2)}) %collective-permute-start.10) | collective-permute-done | bytes 61472 | tf_op jit(solution)/shard_map/ppermute | solution.py:23
  45.8 0.1 collective-permute-start.14
  45.9 1.8 %collective-permute-start.13 = (bf16[240,128]{1,0:T(8,128)(2,1)S(1)}, bf16[240,128]{1,0:T(8,128)(2,1)S(1)}, u32[]{:S(2)}, u32[]{:S(2)}) collective-permute-start(bf16[240,128]{1,0:T(8,128)(2,1)S(1)} %fusion.7.refs_0_), channel_id=1, source_target_pairs={{0,2},{1,3},{2,0},{3,1},{4,6},{5,7},{6,4},{7,5},{8,10},{9,11},{10,... | collective-permute-start | bytes 184328 | tf_op jit(solution)/shard_map/ppermute | solution.py:28
  47.7 2.0 %collective-permute-start.12 = (bf16[240,128]{1,0:T(8,128)(2,1)S(1)}, bf16[240,128]{1,0:T(8,128)(2,1)S(1)}, u32[]{:S(2)}, u32[]{:S(2)}) collective-permute-start(bf16[240,128]{1,0:T(8,128)(2,1)S(1)} %fusion.7.refs_0_), channel_id=1, source_target_pairs={{0,3},{1,0},{2,1},{3,2},{4,7},{5,4},{6,5},{7,6},{8,11},{9,8},{10,9... | collective-permute-start | bytes 184328 | tf_op jit(solution)/shard_map/ppermute | solution.py:28
  49.7 2.5 %collective-permute-done.14.refs_3_ = bf16[240,128]{1,0:T(8,128)(2,1)S(1)} collective-permute-done((bf16[240,128]{1,0:T(8,128)(2,1)S(1)}, bf16[240,128]{1,0:T(8,128)(2,1)S(1)}, u32[]{:S(2)}, u32[]{:S(2)}) %collective-permute-start.14) | collective-permute-done | bytes 61472 | tf_op jit(solution)/shard_map/ppermute | solution.py:28
  52.2 1.0 %collective-permute-done.13.refs_2_ = bf16[240,128]{1,0:T(8,128)(2,1)S(1)} collective-permute-done((bf16[240,128]{1,0:T(8,128)(2,1)S(1)}, bf16[240,128]{1,0:T(8,128)(2,1)S(1)}, u32[]{:S(2)}, u32[]{:S(2)}) %collective-permute-start.13) | collective-permute-done | bytes 61472 | tf_op jit(solution)/shard_map/ppermute | solution.py:28
  53.1 0.6 collective-permute-done.16
  53.7 0.1 convert_add_fusion.1
  53.8 0.1 fusion
  53.8 0.1 line.1
  53.9 0.0 copy-start.4
  53.9 0.0 copy-start.5
  54.0 1.6 %collective-permute-start.22 = (bf16[240,128]{1,0:T(8,128)(2,1)S(1)}, bf16[240,128]{1,0:T(8,128)(2,1)S(1)}, u32[]{:S(2)}, u32[]{:S(2)}) collective-permute-start(bf16[240,128]{1,0:T(8,128)(2,1)S(1)} %line.1), channel_id=1, source_target_pairs={{0,24},{4,28},{8,16},{12,20},{16,8},{20,12},{24,0},{28,4},{1,25},{... | collective-permute-start | bytes 184328 | tf_op jit(solution)/shard_map/ppermute | solution.py:23
  55.5 0.7 collective-permute-start.21
  56.2 1.3 %collective-permute-start.20 = (bf16[240,128]{1,0:T(8,128)(2,1)S(1)}, bf16[240,128]{1,0:T(8,128)(2,1)S(1)}, u32[]{:S(2)}, u32[]{:S(2)}) collective-permute-start(bf16[240,128]{1,0:T(8,128)(2,1)S(1)} %line.1), channel_id=1, source_target_pairs={{0,8},{4,12},{8,0},{12,4},{16,24},{20,28},{24,16},{28,20},{1,9},{5... | collective-permute-start | bytes 184328 | tf_op jit(solution)/shard_map/ppermute | solution.py:23
  57.5 0.8 %collective-permute-start.18 = (bf16[5,128,128]{2,1,0:T(8,128)(2,1)S(1)}, bf16[5,128,128]{2,1,0:T(8,128)(2,1)S(1)}, u32[]{:S(2)}, u32[]{:S(2)}) collective-permute-start(bf16[5,128,128]{2,1,0:T(8,128)(2,1)S(1)} %fusion.3), channel_id=1, source_target_pairs={{0,16},{4,20},{8,24},{12,28},{16,0},{20,4},{24,8},{28,12},{1,17},{... | collective-permute-start | bytes 491528 | tf_op jit(solution)/shard_map/ppermute | solution.py:23
  58.3 1.4 %collective-permute-start.19 = (bf16[6,128,128]{2,1,0:T(8,128)(2,1)S(1)}, bf16[6,128,128]{2,1,0:T(8,128)(2,1)S(1)}, u32[]{:S(2)}, u32[]{:S(2)}) collective-permute-start(bf16[6,128,128]{2,1,0:T(8,128)(2,1)S(1)} %fusion.2), channel_id=1, source_target_pairs={{0,8},{4,12},{8,0},{12,4},{16,24},{20,28},{24,16},{28,20},{1,9},{5... | collective-permute-start | bytes 589832 | tf_op jit(solution)/shard_map/ppermute | solution.py:23
  59.8 1.0 %collective-permute-start.24 = (bf16[11,128,128]{2,1,0:T(8,128)(2,1)S(1)}, bf16[11,128,128]{2,1,0:T(8,128)(2,1)S(1)}, u32[]{:S(2)}, u32[]{:S(2)}) collective-permute-start(bf16[11,128,128]{2,1,0:T(8,128)(2,1)S(1)} %get-tuple-element.63), channel_id=1, source_target_pairs={{0,1},{1,2},{2,3},{3,0},{4,5},{5,6},{6,7},{7,4},{8,9},{9,10},{10,1... | collective-permute-start | bytes 1081352 | tf_op jit(solution)/shard_map/ppermute | solution.py:294
  60.8 0.3 collective-permute-done.20
  61.1 0.1 collective-permute-start.23
  61.2 2.2 %collective-permute-done.18 = bf16[5,128,128]{2,1,0:T(8,128)(2,1)S(1)} collective-permute-done((bf16[5,128,128]{2,1,0:T(8,128)(2,1)S(1)}, bf16[5,128,128]{2,1,0:T(8,128)(2,1)S(1)}, u32[]{:S(2)}, u32[]{:S(2)}) %collective-permute-start.18) | collective-permute-done | bytes 163872 | tf_op jit(solution)/shard_map/ppermute | solution.py:23
  63.4 0.0 copy-start.7
  63.4 0.0 copy-start.8
  63.5 0.6 collective-permute-done.19
  64.1 2.1 %blocks.1 = (f32[3,128,128]{2,1,0:T(8,128)}, f32[8,128,128]{2,1,0:T(8,128)}, f32[8,128,128]{2,1,0:T(8,128)}) custom-call(s32[8]{0:T(128)S(1)} %copy-done.6, bf16[4,240,128]{2,1,0:T(8,128)(2,1)S(1)} %pad_maximum_fusion.near, bf16[4,240,128]{2,1,0:T(8,128)(2,1)S(1)} %collective-permute-done.23.far, f32[3,128,128]{2,1,0:T(8,128)S(1)} %copy-done.5, ...), custom_call_target="tpu_custom_call" | custom-call | tf_op jit(solution)/shard_map/blocks/pallas_call | solution.py:41
  66.3 3.3 %collective-permute-done.24.refs_1_ = bf16[11,128,128]{2,1,0:T(8,128)(2,1)S(1)} collective-permute-done((bf16[11,128,128]{2,1,0:T(8,128)(2,1)S(1)}, bf16[11,128,128]{2,1,0:T(8,128)(2,1)S(1)}, u32[]{:S(2)}, u32[]{:S(2)}) %collective-permute-start.24) | collective-permute-done | bytes 360480 | tf_op jit(solution)/shard_map/ppermute | solution.py:294
  69.6 1.5 %columns.1 = (bf16[3,128,128]{2,1,0:T(8,128)(2,1)}, bf16[8,128,128]{2,1,0:T(8,128)(2,1)}) custom-call(s32[8]{0:T(128)S(1)} %copy-done.6, s32[3]{0:T(128)S(1)} %bitcast.49, s32[8]{0:T(128)S(1)} %bitcast.51, bf16[8,128,128]{2,1,0:T(8,128)(2,1)S(1)} %copy-done.2, f32[11,128,128]{2,1,0:T(8,128)S(1)} %get-tuple-element.39.own, ...), custom_call_target="tpu_custom_call" | custom-call | tf_op jit(solution)/shard_map/columns/pallas_call | solution.py:41
  (28 shorter events, 0.3 us)
Async XLA Ops:
  2.4 14.8 %collective-permute-start.5 = (bf16[11,128,128]{2,1,0:T(8,128)(2,1)}, bf16[11,128,128]{2,1,0:T(8,128)(2,1)S(1)}, u32[]{:S(2)}, u32[]{:S(2)}) collective-permute-start(bf16[11,128,128]{2,1,0:T(8,128)(2,1)} %mask.1.refs_0_.own), channel_id=1, source_target_pairs={{2,0},{1,3},{6,4},{5,7},{10,8},{9,11},{14,12},{13,15},{18,16},{17,... | collective-permute-start | bytes 1081352 | tf_op jit(solution)/shard_map/ppermute | solution.py:290
  3.7 20.4 %collective-permute-start.4 = (bf16[11,128,128]{2,1,0:T(8,128)(2,1)}, bf16[11,128,128]{2,1,0:T(8,128)(2,1)S(1)}, u32[]{:S(2)}, u32[]{:S(2)}) collective-permute-start(bf16[11,128,128]{2,1,0:T(8,128)(2,1)} %mask.1.refs_0_.own), channel_id=1, source_target_pairs={{1,0},{2,1},{3,2},{0,3},{5,4},{6,5},{7,6},{4,7},{9,8},{10,9},{11,1... | collective-permute-start | bytes 1081352 | tf_op jit(solution)/shard_map/ppermute | solution.py:290
  8.8 16.6 %collective-permute-start.3 = (bf16[11,128,128]{2,1,0:T(8,128)(2,1)}, bf16[11,128,128]{2,1,0:T(8,128)(2,1)S(1)}, u32[]{:S(2)}, u32[]{:S(2)}) collective-permute-start(bf16[11,128,128]{2,1,0:T(8,128)(2,1)} %mask.1.refs_0_.own), channel_id=1, source_target_pairs={{0,24},{4,28},{8,16},{12,20},{16,8},{20,12},{24,0},{28,4},{1,25},{... | collective-permute-start | bytes 1081352 | tf_op jit(solution)/shard_map/ppermute | solution.py:23
  11.3 16.3 %collective-permute-start.2 = (bf16[11,128,128]{2,1,0:T(8,128)(2,1)}, bf16[11,128,128]{2,1,0:T(8,128)(2,1)S(1)}, u32[]{:S(2)}, u32[]{:S(2)}) collective-permute-start(bf16[11,128,128]{2,1,0:T(8,128)(2,1)} %mask.1.refs_0_.own), channel_id=1, source_target_pairs={{0,16},{4,20},{8,24},{12,28},{16,0},{20,4},{24,8},{28,12},{1,17},{... | collective-permute-start | bytes 1081352 | tf_op jit(solution)/shard_map/ppermute | solution.py:23
  11.8 15.9 %collective-permute-start.1 = (bf16[11,128,128]{2,1,0:T(8,128)(2,1)}, bf16[11,128,128]{2,1,0:T(8,128)(2,1)S(1)}, u32[]{:S(2)}, u32[]{:S(2)}) collective-permute-start(bf16[11,128,128]{2,1,0:T(8,128)(2,1)} %mask.1.refs_0_.own), channel_id=1, source_target_pairs={{0,8},{4,12},{8,0},{12,4},{16,24},{20,28},{24,16},{28,20},{1,9},{5... | collective-permute-start | bytes 1081352 | tf_op jit(solution)/shard_map/ppermute | solution.py:23
  17.2 10.4 %collective-permute-start = (bf16[11,128,128]{2,1,0:T(8,128)(2,1)}, bf16[11,128,128]{2,1,0:T(8,128)(2,1)S(1)}, u32[]{:S(2)}, u32[]{:S(2)}) collective-permute-start(bf16[11,128,128]{2,1,0:T(8,128)(2,1)} %mask.1.refs_0_.own), channel_id=1, source_target_pairs={{0,4},{4,0},{8,12},{12,8},{16,20},{20,16},{24,28},{28,24},{1,5},{5... | collective-permute-start | bytes 1081352 | tf_op jit(solution)/shard_map/ppermute | solution.py:23
  24.1 1.0 %copy-start = (bf16[11,128,128]{2,1,0:T(8,128)(2,1)S(1)}, bf16[11,128,128]{2,1,0:T(8,128)(2,1)}, u32[]{:S(2)}) copy-start(bf16[11,128,128]{2,1,0:T(8,128)(2,1)} %mask.1.refs_0_.own) | copy-start | bytes 1081348
  25.4 2.4 %copy-start.2 = (bf16[8,128,128]{2,1,0:T(8,128)(2,1)S(1)}, bf16[8,128,128]{2,1,0:T(8,128)(2,1)}, u32[]{:S(2)}) copy-start(bf16[8,128,128]{2,1,0:T(8,128)(2,1)} %panel.5) | copy-start | bytes 786436
  25.4 2.4 %copy-start.3 = (bf16[1,4,8,1,128,128]{5,4,3,2,1,0:T(8,128)(2,1)S(1)}, bf16[1,4,8,1,128,128]{5,4,3,2,1,0:T(8,128)(2,1)}, u32[]{:S(2)}) copy-start(bf16[1,4,8,1,128,128]{5,4,3,2,1,0:T(8,128)(2,1)} %param.9) | copy-start | bytes 3145732
  27.7 2.0 %copy-start.1 = (bf16[11,128,128]{2,1,0:T(8,128)(2,1)S(1)}, bf16[11,128,128]{2,1,0:T(8,128)(2,1)}, u32[]{:S(2)}) copy-start(bf16[11,128,128]{2,1,0:T(8,128)(2,1)} %mask.1.refs_0_.own) | copy-start | bytes 1081348
  27.7 2.8 %collective-permute-start.6 = (bf16[3,11,128,128]{3,2,1,0:T(8,128)(2,1)S(1)}, bf16[3,11,128,128]{3,2,1,0:T(8,128)(2,1)S(1)}, u32[]{:S(2)}, u32[]{:S(2)}) collective-permute-start(bf16[3,11,128,128]{3,2,1,0:T(8,128)(2,1)S(1)} %stack.21.near), channel_id=1, source_target_pairs={{0,4},{4,0},{8,12},{12,8},{16,20},{20,16},{24,28},{28,24},{1,5},{5... | collective-permute-start | bytes 3244040 | tf_op jit(solution)/shard_map/ppermute | solution.py:23
  29.2 8.4 %collective-permute-start.8 = (bf16[4,11,128,128]{3,2,1,0:T(8,128)(2,1)S(1)}, bf16[4,11,128,128]{3,2,1,0:T(8,128)(2,1)S(1)}, u32[]{:S(2)}, u32[]{:S(2)}) collective-permute-start(bf16[4,11,128,128]{3,2,1,0:T(8,128)(2,1)S(1)} %get-tuple-element.43), channel_id=1, source_target_pairs={{0,4},{4,0},{8,12},{12,8},{16,20},{20,16},{24,28},{28,24},{1,5},{5... | collective-permute-start | bytes 4325384 | tf_op jit(solution)/shard_map/ppermute | solution.py:23
  29.7 0.8 %copy-start.6 = (s32[8]{0:T(128)S(1)}, s32[8]{0:T(128)}, u32[]{:S(2)}) copy-start(s32[8]{0:T(128)} %parents.5) | copy-start | bytes 100
  33.1 4.5 %collective-permute-start.7 = (f32[4,240,128]{2,1,0:T(8,128)S(1)}, f32[4,240,128]{2,1,0:T(8,128)S(1)}, u32[]{:S(2)}, u32[]{:S(2)}) collective-permute-start(f32[4,240,128]{2,1,0:T(8,128)S(1)} %get-tuple-element.41), channel_id=1, source_target_pairs={{0,4},{4,0},{8,12},{12,8},{16,20},{20,16},{24,28},{28,24},{1,5},{5... | collective-permute-start | bytes 1474568 | tf_op jit(solution)/shard_map/ppermute | solution.py:23
  33.3 14.5 %collective-permute-start.17 = (bf16[11,128,128]{2,1,0:T(8,128)(2,1)S(1)}, bf16[11,128,128]{2,1,0:T(8,128)(2,1)S(1)}, u32[]{:S(2)}, u32[]{:S(2)}) collective-permute-start(bf16[11,128,128]{2,1,0:T(8,128)(2,1)S(1)} %get-tuple-element.49), channel_id=1, source_target_pairs={{0,2},{3,1},{4,6},{7,5},{8,10},{11,9},{12,14},{15,13},{16,18},{19,... | collective-permute-start | bytes 1081352 | tf_op jit(solution)/shard_map/ppermute | solution.py:294
  37.7 4.5 %collective-permute-start.9 = (bf16[240,128]{1,0:T(8,128)(2,1)S(1)}, bf16[240,128]{1,0:T(8,128)(2,1)S(1)}, u32[]{:S(2)}, u32[]{:S(2)}) collective-permute-start(bf16[240,128]{1,0:T(8,128)(2,1)S(1)} %get-tuple-element.78), channel_id=1, source_target_pairs={{0,8},{4,12},{8,0},{12,4},{16,24},{20,28},{24,16},{28,20},{1,9},{5... | collective-permute-start | bytes 184328 | tf_op jit(solution)/shard_map/ppermute | solution.py:23
  39.3 5.8 %collective-permute-start.11 = (bf16[240,128]{1,0:T(8,128)(2,1)S(1)}, bf16[240,128]{1,0:T(8,128)(2,1)S(1)}, u32[]{:S(2)}, u32[]{:S(2)}) collective-permute-start(bf16[240,128]{1,0:T(8,128)(2,1)S(1)} %get-tuple-element.79), channel_id=1, source_target_pairs={{0,24},{4,28},{8,16},{12,20},{16,8},{20,12},{24,0},{28,4},{1,25},{... | collective-permute-start | bytes 184328 | tf_op jit(solution)/shard_map/ppermute | solution.py:23
  40.6 5.2 %collective-permute-start.10 = (bf16[240,128]{1,0:T(8,128)(2,1)S(1)}, bf16[240,128]{1,0:T(8,128)(2,1)S(1)}, u32[]{:S(2)}, u32[]{:S(2)}) collective-permute-start(bf16[240,128]{1,0:T(8,128)(2,1)S(1)} %get-tuple-element.80), channel_id=1, source_target_pairs={{0,16},{4,20},{8,24},{12,28},{16,0},{20,4},{24,8},{28,12},{1,17},{... | collective-permute-start | bytes 184328 | tf_op jit(solution)/shard_map/ppermute | solution.py:23
  42.3 11.4 %collective-permute-start.16 = (bf16[2,6,128,128]{3,2,1,0:T(8,128)(2,1)S(1)}, bf16[2,6,128,128]{3,2,1,0:T(8,128)(2,1)S(1)}, u32[]{:S(2)}, u32[]{:S(2)}) collective-permute-start(bf16[2,6,128,128]{3,2,1,0:T(8,128)(2,1)S(1)} %slice.95), channel_id=1, source_target_pairs={{0,16},{4,20},{8,24},{12,28},{16,0},{20,4},{24,8},{28,12},{1,17},{... | collective-permute-start | bytes 1179656 | tf_op jit(solution)/shard_map/ppermute | solution.py:23
  44.0 9.1 %collective-permute-start.15 = (bf16[2,5,128,128]{3,2,1,0:T(8,128)(2,1)S(1)}, bf16[2,5,128,128]{3,2,1,0:T(8,128)(2,1)S(1)}, u32[]{:S(2)}, u32[]{:S(2)}) collective-permute-start(bf16[2,5,128,128]{3,2,1,0:T(8,128)(2,1)S(1)} %fusion.1), channel_id=1, source_target_pairs={{0,8},{4,12},{8,0},{12,4},{16,24},{20,28},{24,16},{28,20},{1,9},{5... | collective-permute-start | bytes 983048 | tf_op jit(solution)/shard_map/ppermute | solution.py:23
  45.8 6.3 %collective-permute-start.14 = (bf16[240,128]{1,0:T(8,128)(2,1)S(1)}, bf16[240,128]{1,0:T(8,128)(2,1)S(1)}, u32[]{:S(2)}, u32[]{:S(2)}) collective-permute-start(bf16[240,128]{1,0:T(8,128)(2,1)S(1)} %fusion.7.refs_0_), channel_id=1, source_target_pairs={{0,1},{1,2},{2,3},{3,0},{4,5},{5,6},{6,7},{7,4},{8,9},{9,10},{10,1... | collective-permute-start | bytes 184328 | tf_op jit(solution)/shard_map/ppermute | solution.py:28
  45.9 7.2 %collective-permute-start.13 = (bf16[240,128]{1,0:T(8,128)(2,1)S(1)}, bf16[240,128]{1,0:T(8,128)(2,1)S(1)}, u32[]{:S(2)}, u32[]{:S(2)}) collective-permute-start(bf16[240,128]{1,0:T(8,128)(2,1)S(1)} %fusion.7.refs_0_), channel_id=1, source_target_pairs={{0,2},{1,3},{2,0},{3,1},{4,6},{5,7},{6,4},{7,5},{8,10},{9,11},{10,... | collective-permute-start | bytes 184328 | tf_op jit(solution)/shard_map/ppermute | solution.py:28
  47.7 5.4 %collective-permute-start.12 = (bf16[240,128]{1,0:T(8,128)(2,1)S(1)}, bf16[240,128]{1,0:T(8,128)(2,1)S(1)}, u32[]{:S(2)}, u32[]{:S(2)}) collective-permute-start(bf16[240,128]{1,0:T(8,128)(2,1)S(1)} %fusion.7.refs_0_), channel_id=1, source_target_pairs={{0,3},{1,0},{2,1},{3,2},{4,7},{5,4},{6,5},{7,6},{8,11},{9,8},{10,9... | collective-permute-start | bytes 184328 | tf_op jit(solution)/shard_map/ppermute | solution.py:28
  53.9 10.2 %copy-start.4 = (f32[8,128,128]{2,1,0:T(8,128)S(1)}, f32[8,128,128]{2,1,0:T(8,128)}, u32[]{:S(2)}) copy-start(f32[8,128,128]{2,1,0:T(8,128)} %lower_diagonal.1) | copy-start | bytes 1572868
  53.9 10.2 %copy-start.5 = (f32[3,128,128]{2,1,0:T(8,128)S(1)}, f32[3,128,128]{2,1,0:T(8,128)}, u32[]{:S(2)}) copy-start(f32[3,128,128]{2,1,0:T(8,128)} %upper_diagonal.1) | copy-start | bytes 589828
  54.0 5.8 %collective-permute-start.22 = (bf16[240,128]{1,0:T(8,128)(2,1)S(1)}, bf16[240,128]{1,0:T(8,128)(2,1)S(1)}, u32[]{:S(2)}, u32[]{:S(2)}) collective-permute-start(bf16[240,128]{1,0:T(8,128)(2,1)S(1)} %line.1), channel_id=1, source_target_pairs={{0,24},{4,28},{8,16},{12,20},{16,8},{20,12},{24,0},{28,4},{1,25},{... | collective-permute-start | bytes 184328 | tf_op jit(solution)/shard_map/ppermute | solution.py:23
  55.5 5.3 %collective-permute-start.21 = (bf16[240,128]{1,0:T(8,128)(2,1)S(1)}, bf16[240,128]{1,0:T(8,128)(2,1)S(1)}, u32[]{:S(2)}, u32[]{:S(2)}) collective-permute-start(bf16[240,128]{1,0:T(8,128)(2,1)S(1)} %line.1), channel_id=1, source_target_pairs={{0,16},{4,20},{8,24},{12,28},{16,0},{20,4},{24,8},{28,12},{1,17},{... | collective-permute-start | bytes 184328 | tf_op jit(solution)/shard_map/ppermute | solution.py:23
  56.2 4.9 %collective-permute-start.20 = (bf16[240,128]{1,0:T(8,128)(2,1)S(1)}, bf16[240,128]{1,0:T(8,128)(2,1)S(1)}, u32[]{:S(2)}, u32[]{:S(2)}) collective-permute-start(bf16[240,128]{1,0:T(8,128)(2,1)S(1)} %line.1), channel_id=1, source_target_pairs={{0,8},{4,12},{8,0},{12,4},{16,24},{20,28},{24,16},{28,20},{1,9},{5... | collective-permute-start | bytes 184328 | tf_op jit(solution)/shard_map/ppermute | solution.py:23
  57.5 5.9 %collective-permute-start.18 = (bf16[5,128,128]{2,1,0:T(8,128)(2,1)S(1)}, bf16[5,128,128]{2,1,0:T(8,128)(2,1)S(1)}, u32[]{:S(2)}, u32[]{:S(2)}) collective-permute-start(bf16[5,128,128]{2,1,0:T(8,128)(2,1)S(1)} %fusion.3), channel_id=1, source_target_pairs={{0,16},{4,20},{8,24},{12,28},{16,0},{20,4},{24,8},{28,12},{1,17},{... | collective-permute-start | bytes 491528 | tf_op jit(solution)/shard_map/ppermute | solution.py:23
  58.3 5.7 %collective-permute-start.19 = (bf16[6,128,128]{2,1,0:T(8,128)(2,1)S(1)}, bf16[6,128,128]{2,1,0:T(8,128)(2,1)S(1)}, u32[]{:S(2)}, u32[]{:S(2)}) collective-permute-start(bf16[6,128,128]{2,1,0:T(8,128)(2,1)S(1)} %fusion.2), channel_id=1, source_target_pairs={{0,8},{4,12},{8,0},{12,4},{16,24},{20,28},{24,16},{28,20},{1,9},{5... | collective-permute-start | bytes 589832 | tf_op jit(solution)/shard_map/ppermute | solution.py:23
  59.8 9.8 %collective-permute-start.24 = (bf16[11,128,128]{2,1,0:T(8,128)(2,1)S(1)}, bf16[11,128,128]{2,1,0:T(8,128)(2,1)S(1)}, u32[]{:S(2)}, u32[]{:S(2)}) collective-permute-start(bf16[11,128,128]{2,1,0:T(8,128)(2,1)S(1)} %get-tuple-element.63), channel_id=1, source_target_pairs={{0,1},{1,2},{2,3},{3,0},{4,5},{5,6},{6,7},{7,4},{8,9},{9,10},{10,1... | collective-permute-start | bytes 1081352 | tf_op jit(solution)/shard_map/ppermute | solution.py:294
  61.1 3.0 %collective-permute-start.23 = (bf16[4,240,128]{2,1,0:T(8,128)(2,1)S(1)}, bf16[4,240,128]{2,1,0:T(8,128)(2,1)S(1)}, u32[]{:S(2)}, u32[]{:S(2)}) collective-permute-start(bf16[4,240,128]{2,1,0:T(8,128)(2,1)S(1)} %pad_maximum_fusion.near), channel_id=1, source_target_pairs={{0,4},{4,0},{8,12},{12,8},{16,20},{20,16},{24,28},{28,24},{1,5},{5... | collective-permute-start | bytes 737288 | tf_op jit(solution)/shard_map/ppermute | solution.py:23
  63.4 6.2 %copy-start.7 = (s32[3,1,1]{0,2,1:T(1,128)S(1)}, s32[3,1,1]{0,2,1:T(1,128)}, u32[]{:S(2)}) copy-start(s32[3,1,1]{0,2,1:T(1,128)} %param.11) | copy-start | bytes 40
  63.4 6.2 %copy-start.8 = (s32[8,1,1]{0,2,1:T(1,128)S(1)}, s32[8,1,1]{0,2,1:T(1,128)}, u32[]{:S(2)}) copy-start(s32[8,1,1]{0,2,1:T(1,128)} %param.14) | copy-start | bytes 100

commit v7 on v5

--- a/solution.py
+++ b/solution.py
@@ -51,7 +51,7 @@
 
 
 def stack_kernel(*refs):
-    for i, piece in enumerate(refs[:-3]):
+    for i, piece in enumerate(refs[:-4]):
         refs[-1][i] = piece[...]
 
 
@@ -354,15 +354,6 @@
         (masked, *pieces),
         [shape_of((total, block, (reach + 1) * block), bf16)],
     )
-    far_own = flip(masked, "row", 1)
-    (near,) = call(
-        stack_kernel,
-        "stack",
-        (),
-        (*gather_near(masked, "row")[1:], turned, far_own),
-        [shape_of((half - 1, total, block, block), bf16)],
-    )
-    far = flip(near, "row", 1)
     top, top_turned, panel_turned = call(
         top_kernel,
         "top",
@@ -374,6 +365,15 @@
             shape_of(parent_panel.shape, bf16),
         ],
     )
+    far_own = flip(masked, "row", 1)
+    (near,) = call(
+        stack_kernel,
+        "stack",
+        (),
+        (*gather_near(masked, "row")[1:], turned, far_own, top_turned),
+        [shape_of((half - 1, total, block, block), bf16)],
+    )
+    far = flip(near, "row", 1)
     keep, away = call(
         partial_kernel,
         "partial",

time: 68.9 us -> 70.1 us (1.017); the launches traced: 68.7 us -> 68.8 us
  waiting for transfers between devices: 21.6 us -> 20.1 us
  local copies, waits for them, and re-layouts: 1.32 us -> 2.5 us
    ppermute x2, waiting for transfers between devices: 11.8 us -> 9.24 us  [gather_pair(): lax.ppermute(value, axis, [(b, c) for c, b in pairs(lax.axis_size(axis),...]
    ppermute x18, waiting for transfers between devices: 4.87 us -> 6.09 us  [flip(): return lax.ppermute(value, axis, [(i, i ^ mask) for i in range(size)])]
    unnamed x18, local copies, waits for them, and re-layouts: 1.03 us -> 2.21 us
  transfers between devices with their start and end apart: 25 -> 25, of which waited for: 13 -> 15; matrix products, arithmetic and copies ran while one was open for 1% -> 1% of each run, Pallas kernels for 10% -> 10%
where the time goes in v7:
time: 70.1 us; the launch traced here: 68.8 us
  starting transfers between devices  33.8 us (48%)
  waiting for transfers between devices  20.1 us (29%)
  Pallas kernels  10.6 us (15%)
  local copies, waits for them, and re-layouts  2.5 us (4%)
  between operations  0.89 us (1%)
  other arithmetic  0.85 us (1%)
    ppermute x18, starting transfers between devices, flip(): return lax.ppermute(value, axis, [(i, i ^ mask) for i in range(size)])  16.8 us
    pallas_call x10, Pallas kernels, call(): pl.pallas_call(kernel, out_shape=outs, in_specs=[SMEM] * len(scalars) + [...  10.6 us
    ppermute x2, waiting for transfers between devices, gather_pair(): lax.ppermute(value, axis, [(b, c) for c, b in pairs(lax.axis_size(axis),...  9.24 us
    ppermute x2, starting transfers between devices, gather_pair(): lax.ppermute(value, axis, [(b, c) for c, b in pairs(lax.axis_size(axis),...  6.51 us
    ppermute x18, waiting for transfers between devices, flip(): return lax.ppermute(value, axis, [(i, i ^ mask) for i in range(size)])  6.09 us
    ppermute x3, starting transfers between devices, shift(): lax.ppermute(value, axis, [(i, (i + step) % size) for i in range(size)])  5.85 us
    ppermute x2, starting transfers between devices, return_pair(): return lax.ppermute(value, axis, pairs(lax.axis_size(axis), offset))  4.71 us
    ppermute x3, waiting for transfers between devices, shift(): lax.ppermute(value, axis, [(i, (i + step) % size) for i in range(size)])  3.2 us
  transfers between devices with their start and end apart: 25, of which 15 were waited for; matrix products, arithmetic and copies ran while one was open for 1% of the time, Pallas kernels for 10%

profile of v7, /device:TPU:0, one launch (start us, length us, event | category | flops | bytes accessed | tf_op | source)
XLA Modules:
  0.0 68.8 jit_solution(7522466687243702524)
XLA Ops:
  0.6 1.8 %mask.1.refs_0_.own = bf16[11,128,128]{2,1,0:T(8,128)(2,1)} custom-call(s32[3]{0:T(128)} %bitcast.48, s32[8]{0:T(128)} %bitcast.50, bf16[3,128,128]{2,1,0:T(8,128)(2,1)} %bitcast.55, bf16[8,128,128]{2,1,0:T(8,128)(2,1)} %bitcast.54), custom_call_target="tpu_custom_call" | custom-call | tf_op jit(solution)/shard_map/mask/pallas_call | solution.py:41
  2.4 1.4 %collective-permute-start.5 = (bf16[11,128,128]{2,1,0:T(8,128)(2,1)}, bf16[11,128,128]{2,1,0:T(8,128)(2,1)S(1)}, u32[]{:S(2)}, u32[]{:S(2)}) collective-permute-start(bf16[11,128,128]{2,1,0:T(8,128)(2,1)} %mask.1.refs_0_.own), channel_id=1, source_target_pairs={{2,0},{1,3},{6,4},{5,7},{10,8},{9,11},{14,12},{13,15},{18,16},{17,... | collective-permute-start | bytes 1081352 | tf_op jit(solution)/shard_map/ppermute | solution.py:290
  3.9 5.1 %collective-permute-start.4 = (bf16[11,128,128]{2,1,0:T(8,128)(2,1)}, bf16[11,128,128]{2,1,0:T(8,128)(2,1)S(1)}, u32[]{:S(2)}, u32[]{:S(2)}) collective-permute-start(bf16[11,128,128]{2,1,0:T(8,128)(2,1)} %mask.1.refs_0_.own), channel_id=1, source_target_pairs={{1,0},{2,1},{3,2},{0,3},{5,4},{6,5},{7,6},{4,7},{9,8},{10,9},{11,1... | collective-permute-start | bytes 1081352 | tf_op jit(solution)/shard_map/ppermute | solution.py:290
  9.0 2.4 %collective-permute-start.3 = (bf16[11,128,128]{2,1,0:T(8,128)(2,1)}, bf16[11,128,128]{2,1,0:T(8,128)(2,1)S(1)}, u32[]{:S(2)}, u32[]{:S(2)}) collective-permute-start(bf16[11,128,128]{2,1,0:T(8,128)(2,1)} %mask.1.refs_0_.own), channel_id=1, source_target_pairs={{0,24},{4,28},{8,16},{12,20},{16,8},{20,12},{24,0},{28,4},{1,25},{... | collective-permute-start | bytes 1081352 | tf_op jit(solution)/shard_map/ppermute | solution.py:23
  11.4 0.5 collective-permute-start.2
  11.9 0.5 collective-permute-start.1
  12.5 4.9 %collective-permute-done.5.refs_2_.refs_1_ = bf16[11,128,128]{2,1,0:T(8,128)(2,1)S(1)} collective-permute-done((bf16[11,128,128]{2,1,0:T(8,128)(2,1)}, bf16[11,128,128]{2,1,0:T(8,128)(2,1)S(1)}, u32[]{:S(2)}, u32[]{:S(2)}) %collective-permute-start.5) | collective-permute-done | bytes 360480 | tf_op jit(solution)/shard_map/ppermute | solution.py:290
  17.4 0.9 %copy-done.1 = bf16[8,128,128]{2,1,0:T(8,128)(2,1)S(1)} copy-done((bf16[8,128,128]{2,1,0:T(8,128)(2,1)S(1)}, bf16[8,128,128]{2,1,0:T(8,128)(2,1)}, u32[]{:S(2)}) %copy-start.1) | copy-done | bytes 262168
  18.3 1.2 %copy-done.3 = bf16[1,4,8,1,128,128]{5,4,3,2,1,0:T(8,128)(2,1)S(1)} copy-done((bf16[1,4,8,1,128,128]{5,4,3,2,1,0:T(8,128)(2,1)S(1)}, bf16[1,4,8,1,128,128]{5,4,3,2,1,0:T(8,128)(2,1)}, u32[]{:S(2)}) %copy-start.3) | copy-done | bytes 1048600
  19.5 0.3 top.1
  19.9 4.3 %collective-permute-done.4.refs_1_.refs_0_ = bf16[11,128,128]{2,1,0:T(8,128)(2,1)S(1)} collective-permute-done((bf16[11,128,128]{2,1,0:T(8,128)(2,1)}, bf16[11,128,128]{2,1,0:T(8,128)(2,1)S(1)}, u32[]{:S(2)}, u32[]{:S(2)}) %collective-permute-start.4) | collective-permute-done | bytes 360480 | tf_op jit(solution)/shard_map/ppermute | solution.py:290
  24.2 0.3 turn.1.refs_3_.turned
  24.6 3.1 %collective-permute-done.2.refs_1_ = bf16[11,128,128]{2,1,0:T(8,128)(2,1)S(1)} collective-permute-done((bf16[11,128,128]{2,1,0:T(8,128)(2,1)}, bf16[11,128,128]{2,1,0:T(8,128)(2,1)S(1)}, u32[]{:S(2)}, u32[]{:S(2)}) %collective-permute-start.2) | collective-permute-done | bytes 360480 | tf_op jit(solution)/shard_map/ppermute | solution.py:23
  27.7 0.1 collective-permute-done.1.refs_0_
  27.8 0.1 stack.21.near
  27.8 0.1 collective-permute-start.6
  27.9 1.0 %partial.1 = (f32[4,11,128,128]{3,2,1,0:T(8,128)S(1)}, bf16[4,11,128,128]{3,2,1,0:T(8,128)(2,1)S(1)}) custom-call(bf16[1024,256]{1,0:T(8,128)(2,1)S(1)} %get-tuple-element.39.refs_5_.top, bf16[11,128,128]{2,1,0:T(8,128)(2,1)S(1)} %collective-permute-done.4.refs_1_.refs_0_, bf16[11,128,128]{2,1,0:T(8,128)(2,1)S(1)} %collective-permute-done.5.refs_2_.refs_1_), custom_call_target="tpu_custom_call" | custom-call | tf_op jit(solution)/shard_map/partial/pallas_call | solution.py:41
  28.9 0.6 collective-permute-start.8
  29.5 0.8 %first.1.start = f32[6,384,256]{2,1,0:T(8,128)S(1)} custom-call(bf16[2,384,512]{2,1,0:T(8,128)(2,1)S(1)} %get-tuple-element.38.top, bf16[11,128,128]{2,1,0:T(8,128)(2,1)S(1)} %copy-done, bf16[3,11,128,128]{3,2,1,0:T(8,128)(2,1)S(1)} %stack.21.near), custom_call_target="tpu_custom_call" | custom-call | tf_op jit(solution)/shard_map/first/pallas_call | solution.py:41
  30.3 0.4 collective-permute-done.6.far
  30.6 2.5 %second.1 = (f32[11,128,128]{2,1,0:T(8,128)S(1)}, bf16[11,128,128]{2,1,0:T(8,128)(2,1)S(1)}, bf16[11,128,128]{2,1,0:T(8,128)(2,1)S(1)}, f32[4,240,128]{2,1,0:T(8,128)S(1)}, f32[4,240,128]{2,1,0:T(8,128)S(1)}) custom-call(s32[8]{0:T(128)S(1)} %copy-done.6, bf16[2,384,512]{2,1,0:T(8,128)(2,1)S(1)} %get-tuple-element.38.top, ...), custom_call_target="tpu_custom_call" | custom-call | tf_op jit(solution)/shard_map/second/pallas_call | solution.py:41
  33.2 0.2 collective-permute-start.7
  33.4 1.3 %collective-permute-start.17 = (bf16[11,128,128]{2,1,0:T(8,128)(2,1)S(1)}, bf16[11,128,128]{2,1,0:T(8,128)(2,1)S(1)}, u32[]{:S(2)}, u32[]{:S(2)}) collective-permute-start(bf16[11,128,128]{2,1,0:T(8,128)(2,1)S(1)} %get-tuple-element.49), channel_id=1, source_target_pairs={{0,1},{1,2},{2,3},{3,0},{4,5},{5,6},{6,7},{7,4},{8,9},{9,10},{10,1... | collective-permute-start | bytes 1081352 | tf_op jit(solution)/shard_map/ppermute | solution.py:294
  34.7 0.4 collective-permute-done.7
  35.1 0.1 fusion.8
  35.2 1.6 %collective-permute-start.9 = (bf16[240,128]{1,0:T(8,128)(2,1)S(1)}, bf16[240,128]{1,0:T(8,128)(2,1)S(1)}, u32[]{:S(2)}, u32[]{:S(2)}) collective-permute-start(bf16[240,128]{1,0:T(8,128)(2,1)S(1)} %get-tuple-element.78), channel_id=1, source_target_pairs={{0,8},{4,12},{8,0},{12,4},{16,24},{20,28},{24,16},{28,20},{1,9},{5... | collective-permute-start | bytes 184328 | tf_op jit(solution)/shard_map/ppermute | solution.py:23
  36.8 1.4 %collective-permute-start.11 = (bf16[240,128]{1,0:T(8,128)(2,1)S(1)}, bf16[240,128]{1,0:T(8,128)(2,1)S(1)}, u32[]{:S(2)}, u32[]{:S(2)}) collective-permute-start(bf16[240,128]{1,0:T(8,128)(2,1)S(1)} %get-tuple-element.79), channel_id=1, source_target_pairs={{0,24},{4,28},{8,16},{12,20},{16,8},{20,12},{24,0},{28,4},{1,25},{... | collective-permute-start | bytes 184328 | tf_op jit(solution)/shard_map/ppermute | solution.py:23
  38.1 0.6 collective-permute-start.10
  38.7 0.5 convert_add_fusion
  39.3 0.3 collective-permute-done.9
  39.5 0.1 slice.95
  39.6 0.1 slice.55
  39.7 1.7 %collective-permute-start.16 = (bf16[2,6,128,128]{3,2,1,0:T(8,128)(2,1)S(1)}, bf16[2,6,128,128]{3,2,1,0:T(8,128)(2,1)S(1)}, u32[]{:S(2)}, u32[]{:S(2)}) collective-permute-start(bf16[2,6,128,128]{3,2,1,0:T(8,128)(2,1)S(1)} %slice.95), channel_id=1, source_target_pairs={{0,16},{4,20},{8,24},{12,28},{16,0},{20,4},{24,8},{28,12},{1,17},{... | collective-permute-start | bytes 1179656 | tf_op jit(solution)/shard_map/ppermute | solution.py:23
  41.5 0.1 fusion.1
  41.5 1.4 %collective-permute-start.15 = (bf16[2,5,128,128]{3,2,1,0:T(8,128)(2,1)S(1)}, bf16[2,5,128,128]{3,2,1,0:T(8,128)(2,1)S(1)}, u32[]{:S(2)}, u32[]{:S(2)}) collective-permute-start(bf16[2,5,128,128]{3,2,1,0:T(8,128)(2,1)S(1)} %fusion.1), channel_id=1, source_target_pairs={{0,8},{4,12},{8,0},{12,4},{16,24},{20,28},{24,16},{28,20},{1,9},{5... | collective-permute-start | bytes 983048 | tf_op jit(solution)/shard_map/ppermute | solution.py:23
  42.9 0.4 collective-permute-done.10
  43.3 1.3 %collective-permute-start.14 = (bf16[240,128]{1,0:T(8,128)(2,1)S(1)}, bf16[240,128]{1,0:T(8,128)(2,1)S(1)}, u32[]{:S(2)}, u32[]{:S(2)}) collective-permute-start(bf16[240,128]{1,0:T(8,128)(2,1)S(1)} %fusion.7.refs_0_), channel_id=1, source_target_pairs={{0,1},{1,2},{2,3},{3,0},{4,5},{5,6},{6,7},{7,4},{8,9},{9,10},{10,1... | collective-permute-start | bytes 184328 | tf_op jit(solution)/shard_map/ppermute | solution.py:28
  44.7 3.3 %collective-permute-start.13 = (bf16[240,128]{1,0:T(8,128)(2,1)S(1)}, bf16[240,128]{1,0:T(8,128)(2,1)S(1)}, u32[]{:S(2)}, u32[]{:S(2)}) collective-permute-start(bf16[240,128]{1,0:T(8,128)(2,1)S(1)} %fusion.7.refs_0_), channel_id=1, source_target_pairs={{0,2},{1,3},{2,0},{3,1},{4,6},{5,7},{6,4},{7,5},{8,10},{9,11},{10,... | collective-permute-start | bytes 184328 | tf_op jit(solution)/shard_map/ppermute | solution.py:28
  47.9 1.2 %collective-permute-start.12 = (bf16[240,128]{1,0:T(8,128)(2,1)S(1)}, bf16[240,128]{1,0:T(8,128)(2,1)S(1)}, u32[]{:S(2)}, u32[]{:S(2)}) collective-permute-start(bf16[240,128]{1,0:T(8,128)(2,1)S(1)} %fusion.7.refs_0_), channel_id=1, source_target_pairs={{0,3},{1,0},{2,1},{3,2},{4,7},{5,4},{6,5},{7,6},{8,11},{9,8},{10,9... | collective-permute-start | bytes 184328 | tf_op jit(solution)/shard_map/ppermute | solution.py:28
  49.2 1.1 %collective-permute-done.14.refs_3_ = bf16[240,128]{1,0:T(8,128)(2,1)S(1)} collective-permute-done((bf16[240,128]{1,0:T(8,128)(2,1)S(1)}, bf16[240,128]{1,0:T(8,128)(2,1)S(1)}, u32[]{:S(2)}, u32[]{:S(2)}) %collective-permute-start.14) | collective-permute-done | bytes 61472 | tf_op jit(solution)/shard_map/ppermute | solution.py:28
  50.3 1.5 %collective-permute-done.13.refs_2_ = bf16[240,128]{1,0:T(8,128)(2,1)S(1)} collective-permute-done((bf16[240,128]{1,0:T(8,128)(2,1)S(1)}, bf16[240,128]{1,0:T(8,128)(2,1)S(1)}, u32[]{:S(2)}, u32[]{:S(2)}) %collective-permute-start.13) | collective-permute-done | bytes 61472 | tf_op jit(solution)/shard_map/ppermute | solution.py:28
  51.8 0.6 collective-permute-done.12.refs_1_
  52.4 0.1 convert_add_fusion.1
  52.5 0.1 fusion
  52.5 0.1 line.1
  52.6 0.0 copy-start.2
  52.6 0.0 copy-start.4
  52.6 0.0 copy-start.5
  52.7 1.5 %collective-permute-start.22 = (bf16[240,128]{1,0:T(8,128)(2,1)S(1)}, bf16[240,128]{1,0:T(8,128)(2,1)S(1)}, u32[]{:S(2)}, u32[]{:S(2)}) collective-permute-start(bf16[240,128]{1,0:T(8,128)(2,1)S(1)} %line.1), channel_id=1, source_target_pairs={{0,24},{4,28},{8,16},{12,20},{16,8},{20,12},{24,0},{28,4},{1,25},{... | collective-permute-start | bytes 184328 | tf_op jit(solution)/shard_map/ppermute | solution.py:23
  54.2 1.2 %collective-permute-start.21 = (bf16[240,128]{1,0:T(8,128)(2,1)S(1)}, bf16[240,128]{1,0:T(8,128)(2,1)S(1)}, u32[]{:S(2)}, u32[]{:S(2)}) collective-permute-start(bf16[240,128]{1,0:T(8,128)(2,1)S(1)} %line.1), channel_id=1, source_target_pairs={{0,16},{4,20},{8,24},{12,28},{16,0},{20,4},{24,8},{28,12},{1,17},{... | collective-permute-start | bytes 184328 | tf_op jit(solution)/shard_map/ppermute | solution.py:23
  55.3 0.9 %collective-permute-start.20 = (bf16[240,128]{1,0:T(8,128)(2,1)S(1)}, bf16[240,128]{1,0:T(8,128)(2,1)S(1)}, u32[]{:S(2)}, u32[]{:S(2)}) collective-permute-start(bf16[240,128]{1,0:T(8,128)(2,1)S(1)} %line.1), channel_id=1, source_target_pairs={{0,8},{4,12},{8,0},{12,4},{16,24},{20,28},{24,16},{28,20},{1,9},{5... | collective-permute-start | bytes 184328 | tf_op jit(solution)/shard_map/ppermute | solution.py:23
  56.2 0.6 collective-permute-start.18
  56.8 1.6 %collective-permute-start.19 = (bf16[6,128,128]{2,1,0:T(8,128)(2,1)S(1)}, bf16[6,128,128]{2,1,0:T(8,128)(2,1)S(1)}, u32[]{:S(2)}, u32[]{:S(2)}) collective-permute-start(bf16[6,128,128]{2,1,0:T(8,128)(2,1)S(1)} %fusion.2), channel_id=1, source_target_pairs={{0,8},{4,12},{8,0},{12,4},{16,24},{20,28},{24,16},{28,20},{1,9},{5... | collective-permute-start | bytes 589832 | tf_op jit(solution)/shard_map/ppermute | solution.py:23
  58.4 0.0 collective-permute-done.22
  58.4 3.4 %collective-permute-start.24 = (bf16[11,128,128]{2,1,0:T(8,128)(2,1)S(1)}, bf16[11,128,128]{2,1,0:T(8,128)(2,1)S(1)}, u32[]{:S(2)}, u32[]{:S(2)}) collective-permute-start(bf16[11,128,128]{2,1,0:T(8,128)(2,1)S(1)} %get-tuple-element.63), channel_id=1, source_target_pairs={{0,2},{3,1},{4,6},{7,5},{8,10},{11,9},{12,14},{15,13},{16,18},{19,... | collective-permute-start | bytes 1081352 | tf_op jit(solution)/shard_map/ppermute | solution.py:294
  61.9 0.1 collective-permute-start.23
  62.0 0.1 collective-permute-done.18
  62.2 0.0 copy-start.7
  62.2 0.0 copy-start.8
  62.2 0.4 collective-permute-done.19
  62.6 0.9 %collective-permute-done.23.far = bf16[4,240,128]{2,1,0:T(8,128)(2,1)S(1)} collective-permute-done((bf16[4,240,128]{2,1,0:T(8,128)(2,1)S(1)}, bf16[4,240,128]{2,1,0:T(8,128)(2,1)S(1)}, u32[]{:S(2)}, u32[]{:S(2)}) %collective-permute-start.23) | collective-permute-done | bytes 245792 | tf_op jit(solution)/shard_map/ppermute | solution.py:23
  63.5 2.1 %blocks.1 = (f32[3,128,128]{2,1,0:T(8,128)}, f32[8,128,128]{2,1,0:T(8,128)}, f32[8,128,128]{2,1,0:T(8,128)}) custom-call(s32[8]{0:T(128)S(1)} %copy-done.6, bf16[4,240,128]{2,1,0:T(8,128)(2,1)S(1)} %pad_maximum_fusion.near, bf16[4,240,128]{2,1,0:T(8,128)(2,1)S(1)} %collective-permute-done.23.far, f32[3,128,128]{2,1,0:T(8,128)S(1)} %copy-done.5, ...), custom_call_target="tpu_custom_call" | custom-call | tf_op jit(solution)/shard_map/blocks/pallas_call | solution.py:41
  65.6 1.6 %collective-permute-done.24.refs_1_ = bf16[11,128,128]{2,1,0:T(8,128)(2,1)S(1)} collective-permute-done((bf16[11,128,128]{2,1,0:T(8,128)(2,1)S(1)}, bf16[11,128,128]{2,1,0:T(8,128)(2,1)S(1)}, u32[]{:S(2)}, u32[]{:S(2)}) %collective-permute-start.24) | collective-permute-done | bytes 360480 | tf_op jit(solution)/shard_map/ppermute | solution.py:294
  67.3 1.5 %columns.1 = (bf16[3,128,128]{2,1,0:T(8,128)(2,1)}, bf16[8,128,128]{2,1,0:T(8,128)(2,1)}) custom-call(s32[8]{0:T(128)S(1)} %copy-done.6, s32[3]{0:T(128)S(1)} %bitcast.49, s32[8]{0:T(128)S(1)} %bitcast.51, bf16[8,128,128]{2,1,0:T(8,128)(2,1)S(1)} %copy-done.2, f32[11,128,128]{2,1,0:T(8,128)S(1)} %get-tuple-element.40.own, ...), custom_call_target="tpu_custom_call" | custom-call | tf_op jit(solution)/shard_map/columns/pallas_call | solution.py:41
  (28 shorter events, 0.2 us)
Async XLA Ops:
  2.4 21.8 %copy-start = (bf16[11,128,128]{2,1,0:T(8,128)(2,1)S(1)}, bf16[11,128,128]{2,1,0:T(8,128)(2,1)}, u32[]{:S(2)}) copy-start(bf16[11,128,128]{2,1,0:T(8,128)(2,1)} %mask.1.refs_0_.own) | copy-start | bytes 1081348
  2.4 14.9 %collective-permute-start.5 = (bf16[11,128,128]{2,1,0:T(8,128)(2,1)}, bf16[11,128,128]{2,1,0:T(8,128)(2,1)S(1)}, u32[]{:S(2)}, u32[]{:S(2)}) collective-permute-start(bf16[11,128,128]{2,1,0:T(8,128)(2,1)} %mask.1.refs_0_.own), channel_id=1, source_target_pairs={{2,0},{1,3},{6,4},{5,7},{10,8},{9,11},{14,12},{13,15},{18,16},{17,... | collective-permute-start | bytes 1081352 | tf_op jit(solution)/shard_map/ppermute | solution.py:290
  3.9 20.4 %collective-permute-start.4 = (bf16[11,128,128]{2,1,0:T(8,128)(2,1)}, bf16[11,128,128]{2,1,0:T(8,128)(2,1)S(1)}, u32[]{:S(2)}, u32[]{:S(2)}) collective-permute-start(bf16[11,128,128]{2,1,0:T(8,128)(2,1)} %mask.1.refs_0_.own), channel_id=1, source_target_pairs={{1,0},{2,1},{3,2},{0,3},{5,4},{6,5},{7,6},{4,7},{9,8},{10,9},{11,1... | collective-permute-start | bytes 1081352 | tf_op jit(solution)/shard_map/ppermute | solution.py:290
  9.0 15.6 %collective-permute-start.3 = (bf16[11,128,128]{2,1,0:T(8,128)(2,1)}, bf16[11,128,128]{2,1,0:T(8,128)(2,1)S(1)}, u32[]{:S(2)}, u32[]{:S(2)}) collective-permute-start(bf16[11,128,128]{2,1,0:T(8,128)(2,1)} %mask.1.refs_0_.own), channel_id=1, source_target_pairs={{0,24},{4,28},{8,16},{12,20},{16,8},{20,12},{24,0},{28,4},{1,25},{... | collective-permute-start | bytes 1081352 | tf_op jit(solution)/shard_map/ppermute | solution.py:23
  11.4 16.3 %collective-permute-start.2 = (bf16[11,128,128]{2,1,0:T(8,128)(2,1)}, bf16[11,128,128]{2,1,0:T(8,128)(2,1)S(1)}, u32[]{:S(2)}, u32[]{:S(2)}) collective-permute-start(bf16[11,128,128]{2,1,0:T(8,128)(2,1)} %mask.1.refs_0_.own), channel_id=1, source_target_pairs={{0,16},{4,20},{8,24},{12,28},{16,0},{20,4},{24,8},{28,12},{1,17},{... | collective-permute-start | bytes 1081352 | tf_op jit(solution)/shard_map/ppermute | solution.py:23
  11.9 15.9 %collective-permute-start.1 = (bf16[11,128,128]{2,1,0:T(8,128)(2,1)}, bf16[11,128,128]{2,1,0:T(8,128)(2,1)S(1)}, u32[]{:S(2)}, u32[]{:S(2)}) collective-permute-start(bf16[11,128,128]{2,1,0:T(8,128)(2,1)} %mask.1.refs_0_.own), channel_id=1, source_target_pairs={{0,8},{4,12},{8,0},{12,4},{16,24},{20,28},{24,16},{28,20},{1,9},{5... | collective-permute-start | bytes 1081352 | tf_op jit(solution)/shard_map/ppermute | solution.py:23
  17.4 10.4 %collective-permute-start = (bf16[11,128,128]{2,1,0:T(8,128)(2,1)}, bf16[11,128,128]{2,1,0:T(8,128)(2,1)S(1)}, u32[]{:S(2)}, u32[]{:S(2)}) collective-permute-start(bf16[11,128,128]{2,1,0:T(8,128)(2,1)} %mask.1.refs_0_.own), channel_id=1, source_target_pairs={{0,4},{4,0},{8,12},{12,8},{16,20},{20,16},{24,28},{28,24},{1,5},{5... | collective-permute-start | bytes 1081352 | tf_op jit(solution)/shard_map/ppermute | solution.py:23
  17.4 1.0 %copy-start.1 = (bf16[8,128,128]{2,1,0:T(8,128)(2,1)S(1)}, bf16[8,128,128]{2,1,0:T(8,128)(2,1)}, u32[]{:S(2)}) copy-start(bf16[8,128,128]{2,1,0:T(8,128)(2,1)} %panel.5) | copy-start | bytes 786436
  18.3 1.2 %copy-start.3 = (bf16[1,4,8,1,128,128]{5,4,3,2,1,0:T(8,128)(2,1)S(1)}, bf16[1,4,8,1,128,128]{5,4,3,2,1,0:T(8,128)(2,1)}, u32[]{:S(2)}) copy-start(bf16[1,4,8,1,128,128]{5,4,3,2,1,0:T(8,128)(2,1)} %param.9) | copy-start | bytes 3145732
  27.8 2.8 %collective-permute-start.6 = (bf16[3,11,128,128]{3,2,1,0:T(8,128)(2,1)S(1)}, bf16[3,11,128,128]{3,2,1,0:T(8,128)(2,1)S(1)}, u32[]{:S(2)}, u32[]{:S(2)}) collective-permute-start(bf16[3,11,128,128]{3,2,1,0:T(8,128)(2,1)S(1)} %stack.21.near), channel_id=1, source_target_pairs={{0,4},{4,0},{8,12},{12,8},{16,20},{20,16},{24,28},{28,24},{1,5},{5... | collective-permute-start | bytes 3244040 | tf_op jit(solution)/shard_map/ppermute | solution.py:23
  28.9 5.8 %collective-permute-start.8 = (bf16[4,11,128,128]{3,2,1,0:T(8,128)(2,1)S(1)}, bf16[4,11,128,128]{3,2,1,0:T(8,128)(2,1)S(1)}, u32[]{:S(2)}, u32[]{:S(2)}) collective-permute-start(bf16[4,11,128,128]{3,2,1,0:T(8,128)(2,1)S(1)} %get-tuple-element.43), channel_id=1, source_target_pairs={{0,4},{4,0},{8,12},{12,8},{16,20},{20,16},{24,28},{28,24},{1,5},{5... | collective-permute-start | bytes 4325384 | tf_op jit(solution)/shard_map/ppermute | solution.py:23
  29.5 1.1 %copy-start.6 = (s32[8]{0:T(128)S(1)}, s32[8]{0:T(128)}, u32[]{:S(2)}) copy-start(s32[8]{0:T(128)} %parents.5) | copy-start | bytes 100
  33.2 1.9 %collective-permute-start.7 = (f32[4,240,128]{2,1,0:T(8,128)S(1)}, f32[4,240,128]{2,1,0:T(8,128)S(1)}, u32[]{:S(2)}, u32[]{:S(2)}) collective-permute-start(f32[4,240,128]{2,1,0:T(8,128)S(1)} %get-tuple-element.42), channel_id=1, source_target_pairs={{0,4},{4,0},{8,12},{12,8},{16,20},{20,16},{24,28},{28,24},{1,5},{5... | collective-permute-start | bytes 1474568 | tf_op jit(solution)/shard_map/ppermute | solution.py:23
  33.4 14.6 %collective-permute-start.17 = (bf16[11,128,128]{2,1,0:T(8,128)(2,1)S(1)}, bf16[11,128,128]{2,1,0:T(8,128)(2,1)S(1)}, u32[]{:S(2)}, u32[]{:S(2)}) collective-permute-start(bf16[11,128,128]{2,1,0:T(8,128)(2,1)S(1)} %get-tuple-element.49), channel_id=1, source_target_pairs={{0,1},{1,2},{2,3},{3,0},{4,5},{5,6},{6,7},{7,4},{8,9},{9,10},{10,1... | collective-permute-start | bytes 1081352 | tf_op jit(solution)/shard_map/ppermute | solution.py:294
  35.2 4.4 %collective-permute-start.9 = (bf16[240,128]{1,0:T(8,128)(2,1)S(1)}, bf16[240,128]{1,0:T(8,128)(2,1)S(1)}, u32[]{:S(2)}, u32[]{:S(2)}) collective-permute-start(bf16[240,128]{1,0:T(8,128)(2,1)S(1)} %get-tuple-element.78), channel_id=1, source_target_pairs={{0,8},{4,12},{8,0},{12,4},{16,24},{20,28},{24,16},{28,20},{1,9},{5... | collective-permute-start | bytes 184328 | tf_op jit(solution)/shard_map/ppermute | solution.py:23
  36.8 6.1 %collective-permute-start.11 = (bf16[240,128]{1,0:T(8,128)(2,1)S(1)}, bf16[240,128]{1,0:T(8,128)(2,1)S(1)}, u32[]{:S(2)}, u32[]{:S(2)}) collective-permute-start(bf16[240,128]{1,0:T(8,128)(2,1)S(1)} %get-tuple-element.79), channel_id=1, source_target_pairs={{0,24},{4,28},{8,16},{12,20},{16,8},{20,12},{24,0},{28,4},{1,25},{... | collective-permute-start | bytes 184328 | tf_op jit(solution)/shard_map/ppermute | solution.py:23
  38.1 5.1 %collective-permute-start.10 = (bf16[240,128]{1,0:T(8,128)(2,1)S(1)}, bf16[240,128]{1,0:T(8,128)(2,1)S(1)}, u32[]{:S(2)}, u32[]{:S(2)}) collective-permute-start(bf16[240,128]{1,0:T(8,128)(2,1)S(1)} %get-tuple-element.80), channel_id=1, source_target_pairs={{0,16},{4,20},{8,24},{12,28},{16,0},{20,4},{24,8},{28,12},{1,17},{... | collective-permute-start | bytes 184328 | tf_op jit(solution)/shard_map/ppermute | solution.py:23
  39.7 12.7 %collective-permute-start.16 = (bf16[2,6,128,128]{3,2,1,0:T(8,128)(2,1)S(1)}, bf16[2,6,128,128]{3,2,1,0:T(8,128)(2,1)S(1)}, u32[]{:S(2)}, u32[]{:S(2)}) collective-permute-start(bf16[2,6,128,128]{3,2,1,0:T(8,128)(2,1)S(1)} %slice.95), channel_id=1, source_target_pairs={{0,16},{4,20},{8,24},{12,28},{16,0},{20,4},{24,8},{28,12},{1,17},{... | collective-permute-start | bytes 1179656 | tf_op jit(solution)/shard_map/ppermute | solution.py:23
  41.5 10.9 %collective-permute-start.15 = (bf16[2,5,128,128]{3,2,1,0:T(8,128)(2,1)S(1)}, bf16[2,5,128,128]{3,2,1,0:T(8,128)(2,1)S(1)}, u32[]{:S(2)}, u32[]{:S(2)}) collective-permute-start(bf16[2,5,128,128]{3,2,1,0:T(8,128)(2,1)S(1)} %fusion.1), channel_id=1, source_target_pairs={{0,8},{4,12},{8,0},{12,4},{16,24},{20,28},{24,16},{28,20},{1,9},{5... | collective-permute-start | bytes 983048 | tf_op jit(solution)/shard_map/ppermute | solution.py:23
  43.3 7.0 %collective-permute-start.14 = (bf16[240,128]{1,0:T(8,128)(2,1)S(1)}, bf16[240,128]{1,0:T(8,128)(2,1)S(1)}, u32[]{:S(2)}, u32[]{:S(2)}) collective-permute-start(bf16[240,128]{1,0:T(8,128)(2,1)S(1)} %fusion.7.refs_0_), channel_id=1, source_target_pairs={{0,1},{1,2},{2,3},{3,0},{4,5},{5,6},{6,7},{7,4},{8,9},{9,10},{10,1... | collective-permute-start | bytes 184328 | tf_op jit(solution)/shard_map/ppermute | solution.py:28
  44.7 7.2 %collective-permute-start.13 = (bf16[240,128]{1,0:T(8,128)(2,1)S(1)}, bf16[240,128]{1,0:T(8,128)(2,1)S(1)}, u32[]{:S(2)}, u32[]{:S(2)}) collective-permute-start(bf16[240,128]{1,0:T(8,128)(2,1)S(1)} %fusion.7.refs_0_), channel_id=1, source_target_pairs={{0,2},{1,3},{2,0},{3,1},{4,6},{5,7},{6,4},{7,5},{8,10},{9,11},{10,... | collective-permute-start | bytes 184328 | tf_op jit(solution)/shard_map/ppermute | solution.py:28
  47.9 4.4 %collective-permute-start.12 = (bf16[240,128]{1,0:T(8,128)(2,1)S(1)}, bf16[240,128]{1,0:T(8,128)(2,1)S(1)}, u32[]{:S(2)}, u32[]{:S(2)}) collective-permute-start(bf16[240,128]{1,0:T(8,128)(2,1)S(1)} %fusion.7.refs_0_), channel_id=1, source_target_pairs={{0,3},{1,0},{2,1},{3,2},{4,7},{5,4},{6,5},{7,6},{8,11},{9,8},{10,9... | collective-permute-start | bytes 184328 | tf_op jit(solution)/shard_map/ppermute | solution.py:28
  52.6 10.9 %copy-start.2 = (bf16[8,128,128]{2,1,0:T(8,128)(2,1)S(1)}, bf16[8,128,128]{2,1,0:T(8,128)(2,1)}, u32[]{:S(2)}) copy-start(bf16[8,128,128]{2,1,0:T(8,128)(2,1)} %panel.5) | copy-start | bytes 786436
  52.6 10.9 %copy-start.4 = (f32[8,128,128]{2,1,0:T(8,128)S(1)}, f32[8,128,128]{2,1,0:T(8,128)}, u32[]{:S(2)}) copy-start(f32[8,128,128]{2,1,0:T(8,128)} %lower_diagonal.1) | copy-start | bytes 1572868
  52.6 10.9 %copy-start.5 = (f32[3,128,128]{2,1,0:T(8,128)S(1)}, f32[3,128,128]{2,1,0:T(8,128)}, u32[]{:S(2)}) copy-start(f32[3,128,128]{2,1,0:T(8,128)} %upper_diagonal.1) | copy-start | bytes 589828
  52.7 5.8 %collective-permute-start.22 = (bf16[240,128]{1,0:T(8,128)(2,1)S(1)}, bf16[240,128]{1,0:T(8,128)(2,1)S(1)}, u32[]{:S(2)}, u32[]{:S(2)}) collective-permute-start(bf16[240,128]{1,0:T(8,128)(2,1)S(1)} %line.1), channel_id=1, source_target_pairs={{0,24},{4,28},{8,16},{12,20},{16,8},{20,12},{24,0},{28,4},{1,25},{... | collective-permute-start | bytes 184328 | tf_op jit(solution)/shard_map/ppermute | solution.py:23
  54.2 7.7 %collective-permute-start.21 = (bf16[240,128]{1,0:T(8,128)(2,1)S(1)}, bf16[240,128]{1,0:T(8,128)(2,1)S(1)}, u32[]{:S(2)}, u32[]{:S(2)}) collective-permute-start(bf16[240,128]{1,0:T(8,128)(2,1)S(1)} %line.1), channel_id=1, source_target_pairs={{0,16},{4,20},{8,24},{12,28},{16,0},{20,4},{24,8},{28,12},{1,17},{... | collective-permute-start | bytes 184328 | tf_op jit(solution)/shard_map/ppermute | solution.py:23
  55.3 6.5 %collective-permute-start.20 = (bf16[240,128]{1,0:T(8,128)(2,1)S(1)}, bf16[240,128]{1,0:T(8,128)(2,1)S(1)}, u32[]{:S(2)}, u32[]{:S(2)}) collective-permute-start(bf16[240,128]{1,0:T(8,128)(2,1)S(1)} %line.1), channel_id=1, source_target_pairs={{0,8},{4,12},{8,0},{12,4},{16,24},{20,28},{24,16},{28,20},{1,9},{5... | collective-permute-start | bytes 184328 | tf_op jit(solution)/shard_map/ppermute | solution.py:23
  56.2 5.9 %collective-permute-start.18 = (bf16[5,128,128]{2,1,0:T(8,128)(2,1)S(1)}, bf16[5,128,128]{2,1,0:T(8,128)(2,1)S(1)}, u32[]{:S(2)}, u32[]{:S(2)}) collective-permute-start(bf16[5,128,128]{2,1,0:T(8,128)(2,1)S(1)} %fusion.3), channel_id=1, source_target_pairs={{0,16},{4,20},{8,24},{12,28},{16,0},{20,4},{24,8},{28,12},{1,17},{... | collective-permute-start | bytes 491528 | tf_op jit(solution)/shard_map/ppermute | solution.py:23
  56.8 5.7 %collective-permute-start.19 = (bf16[6,128,128]{2,1,0:T(8,128)(2,1)S(1)}, bf16[6,128,128]{2,1,0:T(8,128)(2,1)S(1)}, u32[]{:S(2)}, u32[]{:S(2)}) collective-permute-start(bf16[6,128,128]{2,1,0:T(8,128)(2,1)S(1)} %fusion.2), channel_id=1, source_target_pairs={{0,8},{4,12},{8,0},{12,4},{16,24},{20,28},{24,16},{28,20},{1,9},{5... | collective-permute-start | bytes 589832 | tf_op jit(solution)/shard_map/ppermute | solution.py:23
  58.4 8.8 %collective-permute-start.24 = (bf16[11,128,128]{2,1,0:T(8,128)(2,1)S(1)}, bf16[11,128,128]{2,1,0:T(8,128)(2,1)S(1)}, u32[]{:S(2)}, u32[]{:S(2)}) collective-permute-start(bf16[11,128,128]{2,1,0:T(8,128)(2,1)S(1)} %get-tuple-element.63), channel_id=1, source_target_pairs={{0,2},{3,1},{4,6},{7,5},{8,10},{11,9},{12,14},{15,13},{16,18},{19,... | collective-permute-start | bytes 1081352 | tf_op jit(solution)/shard_map/ppermute | solution.py:294
  61.9 1.6 %collective-permute-start.23 = (bf16[4,240,128]{2,1,0:T(8,128)(2,1)S(1)}, bf16[4,240,128]{2,1,0:T(8,128)(2,1)S(1)}, u32[]{:S(2)}, u32[]{:S(2)}) collective-permute-start(bf16[4,240,128]{2,1,0:T(8,128)(2,1)S(1)} %pad_maximum_fusion.near), channel_id=1, source_target_pairs={{0,4},{4,0},{8,12},{12,8},{16,20},{20,16},{24,28},{28,24},{1,5},{5... | collective-permute-start | bytes 737288 | tf_op jit(solution)/shard_map/ppermute | solution.py:23
  62.2 5.1 %copy-start.7 = (s32[3,1,1]{0,2,1:T(1,128)S(1)}, s32[3,1,1]{0,2,1:T(1,128)}, u32[]{:S(2)}) copy-start(s32[3,1,1]{0,2,1:T(1,128)} %param.11) | copy-start | bytes 40
  62.2 5.1 %copy-start.8 = (s32[8,1,1]{0,2,1:T(1,128)S(1)}, s32[8,1,1]{0,2,1:T(1,128)}, u32[]{:S(2)}) copy-start(s32[8,1,1]{0,2,1:T(1,128)} %param.14) | copy-start | bytes 100
